TPU v7x, 32 devices: a whole 2x2x4 slice. The times are simulated.
32 devices in a mesh: rep: 2 (over x), node: 8 (over z, y), local: 2 (over core).
Axes of the slice: x: 2, y: 2, z: 4, core: 2. Of those that a mesh axis runs over, the one named last changes fastest.
Arguments:
- tokens: bfloat16 [2048, 7168], P(('rep', 'node', 'local')), parts along dimension 0, may hold values from -6 to 6
- gate_ids: int32 [2048, 4], P(('rep', 'node', 'local')), parts along dimension 0, may hold values from 0 to 7, all different within a row; in each aligned block of 64 rows (0 to 63, 64 to 127, ...) at most 64 rows name the same one
- gate_values: bfloat16 [2048, 4], P(('rep', 'node', 'local')), parts along dimension 0, may hold values from 0.049804688 to 1
- w_gate: bfloat16 [8, 7168, 1024], P('node', None, 'local'), may hold values from -0.0625 to 0.0625
- w_up: bfloat16 [8, 7168, 1024], P('node', None, 'local'), may hold values from -0.0625 to 0.0625
- w_down: bfloat16 [8, 1024, 7168], P('node', 'local'), may hold values from -0.1875 to 0.1875
Outputs:
- mixed: bfloat16 [2048, 7168], P(('rep', 'node', 'local')), parts along dimension 0
There are 2 independent parts, one for each index of `rep`. A program takes and returns all parts, laid end to end along the dimension named above; an argument that names none is the same for every part. Nothing has to cross between parts.
Inputs may be any that keep to these rules, and one draw needn't show every extreme that they name: `gate_ids`: each row names 4 different experts. Within the rows of one device, no expert is named by more than 64 rows, and in every draw some expert is named by exactly 64 rows of some device.
All inputs are finite; a program needn't handle non-finite values.
Results may differ from a plain program's by a relative error of at most 0.0065.
Values may be sent and summed in bfloat16 or wider, within the bound.
No kernel may reach another device: no remote copies, remote signals or barrier semaphores. Data moves between devices by JAX's collectives and lax.ppermute only.
A program may use at most 128 MiB of HBM per device.

v0:
```python
import jax
import jax.numpy as jnp
from jax import lax
from jax.sharding import PartitionSpec as P


def per_device(tokens, gate_ids, gate_values, w_gate, w_up, w_down):
    node_count = lax.axis_size("node")
    token_count = tokens.shape[0]
    choose_count = gate_ids.shape[1]
    width = tokens.shape[1]
    capacity = 2 * token_count * choose_count // node_count
    flat_ids = gate_ids.reshape(-1)
    expert_row = jnp.arange(node_count, dtype=jnp.int32)
    onehot = (flat_ids[:, None] == expert_row[None, :]).astype(jnp.int32)
    earlier = jnp.cumsum(onehot, axis=0) - onehot
    within = jnp.sum(earlier * onehot, axis=1)
    slot = (flat_ids * capacity + within).reshape(token_count, choose_count)
    slot_row = jnp.arange(node_count * capacity, dtype=jnp.int32)
    matches = slot[:, :, None] == slot_row[None, None, :]
    select = jnp.any(matches, axis=1).astype(jnp.bfloat16)
    combine_table = jnp.sum(
        jnp.where(matches, gate_values.astype(jnp.float32)[:, :, None], jnp.float32(0.0)), axis=1
    ).astype(jnp.bfloat16)
    outgoing = jnp.einsum("ts,td->sd", select, tokens, preferred_element_type=jnp.float32).astype(
        jnp.bfloat16
    )
    outgoing = outgoing.reshape(node_count, capacity, width)
    gathered = lax.all_gather(
        lax.all_to_all(outgoing, "node", split_axis=0, concat_axis=0, tiled=True),
        "local",
        axis=0,
        tiled=True,
    )
    rows = gathered.reshape(-1, width)
    gate_act = jnp.dot(rows, w_gate[0], preferred_element_type=jnp.float32)
    up_act = jnp.dot(rows, w_up[0], preferred_element_type=jnp.float32)
    hidden = (jax.nn.silu(gate_act) * up_act).astype(jnp.bfloat16)
    partial_value = (
        jnp.dot(hidden, w_down[0], preferred_element_type=jnp.float32)
        .astype(jnp.bfloat16)
        .reshape(gathered.shape)
    )
    partial_value = lax.optimization_barrier(partial_value).astype(jnp.float32)
    own_rows = lax.psum_scatter(
        partial_value.astype(jnp.bfloat16), "local", scatter_dimension=0, tiled=True
    )
    expert_out = lax.all_to_all(own_rows, "node", split_axis=0, concat_axis=0, tiled=True)
    result = jnp.dot(
        combine_table,
        expert_out.reshape(node_count * capacity, width),
        preferred_element_type=jnp.float32,
    )
    return result.astype(jnp.bfloat16)


def solution(mesh):
    return jax.shard_map(
        per_device,
        mesh=mesh,
        in_specs=(
            P(("rep", "node", "local"), None),
            P(("rep", "node", "local"), None),
            P(("rep", "node", "local"), None),
            P("node", None, "local"),
            P("node", None, "local"),
            P("node", "local", None),
        ),
        out_specs=P(("rep", "node", "local"), None),
        check_vma=False,
    )
```

profile of v0, /device:TPU:0, one launch (start us, length us, event | category | flops | bytes accessed | tf_op | source)
XLA Modules:
  0.0 445.1 jit_solution(14984800012365417282)
XLA Ops:
  6.5 0.0 copy-start
  6.5 0.0 all-gather.2.cloned.1.call-start
  6.5 0.9 copy.24
  7.4 0.1 eq.42
  7.5 0.1 eq.38
  7.6 0.6 reduce-window.6
  8.2 0.2 slice_reduce_fusion
  8.5 0.1 fusion.10
  8.6 0.1 reduce_sum.21
  8.7 0.1 copy.26
  8.7 0.7 multiply_add_fusion
  9.4 0.1 fusion.7
  9.6 2.1 convolution_convert_fusion.1
  11.7 167.8 %all_to_all.10 = bf16[8,64,7168]{2,1,0:T(8,128)(2,1)} all-to-all(bf16[8,64,7168]{2,1,0:T(8,128)(2,1)S(1)} %bitcast.30), channel_id=1, replica_groups=mesh['rep'=2,'node'=8,'local'=2] {'node'}, dimensions={0} | all-to-all | bytes 14680064 | tf_op jit(solution)/shard_map/all_to_all | solution.py:30
  179.5 0.0 all-gather.2.cloned.1.call-update
  179.5 0.0 reduce-scatter.2.cloned.1.call-start
  179.6 26.1 %all-gather.2.cloned.1.call-done = bf16[16,64,7168]{2,1,0:T(8,128)(2,1)} async-done(((bf16[8,64,7168]{2,1,0:T(8,128)(2,1)}), bf16[16,64,7168]{2,1,0:T(8,128)(2,1)}) %all-gather.2.cloned.1.call-update) | async-done | bytes 14680080 | tf_op jit(solution)/shard_map/all_gather | solution.py:29
  205.7 13.4 %fusion.1 = f32[1024,512]{1,0:T(8,128)S(1)} fusion(bf16[1024,7168]{1,0:T(8,128)(2,1)} %bitcast.32, bf16[1,7168,512]{2,1,0:T(8,128)(2,1)} %param.10), kind=kOutput, calls=%fused_computation.4 | convolution fusion | flops 7516192768 | bytes 24117248 | tf_op jit(solution)/shard_map/dot_general | solution.py:37
  219.1 0.0 copy-done.3
  219.1 0.0 slice-start.1
  219.1 10.3 %multiply_convert_fusion = bf16[1024,512]{1,0:T(8,128)(2,1)S(1)} fusion(f32[1024,512]{1,0:T(8,128)S(1)} %fusion.1, bf16[1024,7168]{1,0:T(8,128)(2,1)S(1)} %bitcast.33, bf16[1,7168,512]{2,1,0:T(8,128)(2,1)} %param.9), kind=kOutput, calls=%fused_computation.8 | convolution fusion | flops 7519338496 | bytes 25165824 | tf_op jit(solution)/shard_map/dot_general | solution.py:36
  229.4 0.0 slice-done
  229.4 0.0 slice-done.1
  229.4 11.1 %convolution_convert_fusion = bf16[1024,7168]{1,0:T(8,128)(2,1)} fusion(bf16[1024,512]{1,0:T(8,128)(2,1)S(1)} %multiply_convert_fusion, bf16[1,512,7168]{2,1,0:T(8,128)(2,1)S(1)} %bitcast.35), kind=kOutput, calls=%fused_computation | convolution fusion | flops 7523532800 | bytes 23068672 | tf_op jit(solution)/shard_map/dot_general | solution.py:40
  240.5 0.0 reduce-scatter.2.cloned.1.call-update
  240.5 0.0 copy-start.2
  240.5 25.2 %reduce-scatter.2.cloned.1.call-done = bf16[8,64,7168]{2,1,0:T(8,128)(2,1)} async-done(((bf16[16,64,7168]{2,1,0:T(8,128)(2,1)}), bf16[8,64,7168]{2,1,0:T(8,128)(2,1)}) %reduce-scatter.2.cloned.1.call-update) | async-done | bytes 7340048 | tf_op jit(solution)/shard_map/reduce_scatter | solution.py:45
  265.7 5.9 %all-to-all-start.1 = ((bf16[8,64,7168]{2,1,0:T(8,128)(2,1)}), bf16[8,64,7168]{2,1,0:T(8,128)(2,1)}, u32[]{:S(2)}, u32[]{:S(2)}) async-start(bf16[8,64,7168]{2,1,0:T(8,128)(2,1)} %reduce-scatter.2.cloned.1.call-done), calls=%async_computation.2 | async-start | bytes 14680064 | tf_op jit(solution)/shard_map/all_to_all | solution.py:48
  271.6 0.0 copy-start.1
  271.6 0.1 select_reduce_fusion
  271.8 161.0 %all-to-all-done.1 = bf16[8,64,7168]{2,1,0:T(8,128)(2,1)} async-done(((bf16[8,64,7168]{2,1,0:T(8,128)(2,1)}), bf16[8,64,7168]{2,1,0:T(8,128)(2,1)}, u32[]{:S(2)}, u32[]{:S(2)}) %all-to-all-start.1) | async-done | bytes 7340064 | tf_op jit(solution)/shard_map/all_to_all | solution.py:48
  432.8 5.4 %convolution_convert_fusion.2 = bf16[64,7168]{1,0:T(8,128)(2,1)} fusion(bf16[512,7168]{1,0:T(8,128)(2,1)} %bitcast.8, bf16[64,512]{1,0:T(8,128)(2,1)S(1)} %select_reduce_fusion), kind=kOutput, calls=%fused_computation.2 | convolution fusion | flops 470220800 | bytes 8323072 | tf_op jit(solution)/shard_map/dot_general | solution.py:49
  (10 shorter events, 0.1 us)
Async XLA Ops:
  6.5 3.1 copy-start
  6.5 199.2 %all-gather.2.cloned.1.call-start = ((), (), s32[]{:S(2)}) async-start(), calls=%async_computation.3 | async-start | bytes 22020096 | tf_op jit(solution)/shard_map/all_gather | solution.py:29
  179.5 86.2 %reduce-scatter.2.cloned.1.call-start = ((), (), s32[]{:S(2)}) async-start(), calls=%async_computation.4 | async-start | bytes 22020096 | tf_op jit(solution)/shard_map/reduce_scatter | solution.py:45
  205.7 13.4 %copy-start.3 = (bf16[16,64,7168]{2,1,0:T(8,128)(2,1)S(1)}, bf16[16,64,7168]{2,1,0:T(8,128)(2,1)}, u32[]{:S(2)}) copy-start(bf16[16,64,7168]{2,1,0:T(8,128)(2,1)} %all-gather.2.cloned.1.call-done) | copy-start | bytes 44040196
  205.7 23.7 %slice-start = ((s8[7340032]{0:T(1024)(128)(4,1)}), s8[4194304]{0:T(1024)(128)(4,1)S(1)}, s32[]{:S(2)}) async-start(s8[7340032]{0:T(1024)(128)(4,1)} %bitcast.34), calls=%async_computation.5 | async-start | bytes 8388608
  219.1 10.3 %slice-start.1 = ((s8[7340032]{0:T(1024)(128)(4,1)}), s8[3145728]{0:T(1024)(128)(4,1)S(1)}, s32[]{:S(2)}) async-start(s8[7340032]{0:T(1024)(128)(4,1)} %bitcast.34), calls=%async_computation.6 | async-start | bytes 6291456
  240.5 31.1 %copy-start.2 = (bf16[64,4]{0,1:T(4,128)(2,1)S(1)}, bf16[64,4]{0,1:T(4,128)(2,1)}, u32[]{:S(2)}) copy-start(bf16[64,4]{0,1:T(4,128)(2,1)} %param.8) | copy-start | bytes 1540
  265.7 167.1 %all-to-all-start.1 = ((bf16[8,64,7168]{2,1,0:T(8,128)(2,1)}), bf16[8,64,7168]{2,1,0:T(8,128)(2,1)}, u32[]{:S(2)}, u32[]{:S(2)}) async-start(bf16[8,64,7168]{2,1,0:T(8,128)(2,1)} %reduce-scatter.2.cloned.1.call-done), calls=%async_computation.2 | async-start | bytes 14680064 | tf_op jit(solution)/shard_map/all_to_all | solution.py:48
  271.6 166.6 %copy-start.1 = (bf16[64,7168]{1,0:T(8,128)(2,1)S(1)}, bf16[64,7168]{1,0:T(8,128)(2,1)}, u32[]{:S(2)}) copy-start(bf16[64,7168]{1,0:T(8,128)(2,1)} %param.6) | copy-start | bytes 2752516
Sparse Core Ops, SparseCore 0:
  179.6 26.0 all-gather.1
  240.6 25.0 reduce-scatter.1
where the time goes:
time: 445 us
  waiting for transfers between devices  212 us (48%)
  blocking collectives  168 us (38%)
  matrix products  42.2 us (9%)
  between operations  13.5 us (3%)
  starting transfers between devices  5.93 us (1%)
    all_to_all x1, blocking collectives, per_device(): lax.all_to_all(outgoing, 'node', split_axis=0, concat_axis=0, tiled=True)  168 us
    all_to_all x1, waiting for transfers between devices, per_device(): lax.all_to_all(own_rows, 'node', split_axis=0, concat_axis=0, tiled=True)  161 us
    all_gather x1, waiting for transfers between devices, per_device(): lax.all_gather(lax.all_to_all(outgoing, 'node', split_axis=0, concat_axis...  26.1 us
    reduce_scatter x1, waiting for transfers between devices, per_device(): lax.psum_scatter(partial_value.astype(jnp.bfloat16), 'local', scatter_dim...  25.2 us
    dot_general x1, matrix products, per_device(): up_act = jnp.dot(rows, w_up[0], preferred_element_type=jnp.float32)  13.4 us
    dot_general x1, matrix products, per_device(): jnp.dot(hidden, w_down[0], preferred_element_type=jnp.float32)  11.1 us
    dot_general x1, matrix products, per_device(): gate_act = jnp.dot(rows, w_gate[0], preferred_element_type=jnp.float32)  10.3 us
  transfers between devices with their start and end apart: 3, of which 3 were waited for; matrix products, arithmetic and copies ran while one was open for 0% of the time, Pallas kernels for 0%

commit v1 on v0

v1 whole, which is shorter than its diff:
```python
import functools

import jax
import jax.numpy as jnp
from jax import lax
from jax.experimental import pallas as pl
from jax.experimental.pallas import tpu as pltpu
from jax.sharding import PartitionSpec as P


def divisor_tile(extent, most, unit):
    best = unit
    for tile in range(unit, most + 1, unit):
        if extent % tile == 0:
            best = tile
    return best


def expert_kernel(count, hidden_steps, hidden_tile, *refs):
    rows_in = refs[:count]
    scale, gate_own, up_own, gate_other, up_other, down_own, down_other = refs[count : count + 7]
    rows_out = refs[count + 7 : 2 * count + 7]
    rows, hidden, arrived = refs[2 * count + 7 :]
    step = pl.program_id(0)
    height = rows_in[0].shape[0]
    half = hidden_steps // 2

    @pl.when(step == 0)
    def load():
        copies = [
            pltpu.make_async_copy(source, rows.at[pl.ds(i * height, height)], arrived.at[i])
            for i, source in enumerate(rows_in)
        ]
        for copy in copies:
            copy.start()
        for copy in copies:
            copy.wait()

    def project(gate, up):
        gate_act = jnp.dot(rows[...], gate[...], preferred_element_type=jnp.float32)
        up_act = jnp.dot(rows[...], up[...], preferred_element_type=jnp.float32)
        value = gate_act / (1.0 + jnp.exp(-gate_act)) * up_act
        hidden[step] = value.astype(jnp.bfloat16)

    @pl.when(step < half)
    def own():
        project(gate_own, up_own)

    @pl.when((step >= half) & (step < hidden_steps))
    def other():
        project(gate_other, up_other)

    @pl.when(step >= hidden_steps)
    def down():
        total = jnp.zeros((rows.shape[0], down_own.shape[1]), jnp.float32)
        for j in range(hidden_steps):
            source = down_own if j < half else down_other
            piece = source[(j % half) * hidden_tile : (j % half + 1) * hidden_tile, :]
            total += jnp.dot(hidden[j], piece, preferred_element_type=jnp.float32)
        total = total * scale[...]
        for i in range(count):
            rows_out[i][...] = total[i * height : (i + 1) * height].astype(jnp.bfloat16)


def expert_rows(blocks, scale, weights):
    count = len(blocks)
    height, width = blocks[0].shape
    depth = weights[0].shape[1]
    hidden_tile = divisor_tile(depth, 256, 128)
    half = depth // hidden_tile
    hidden_steps = 2 * half
    out_tile = divisor_tile(width, 1024, 128)
    out_steps = width // out_tile
    row_count = count * height

    def own_map(j):
        return (0, jnp.minimum(j, half - 1))

    def other_map(j):
        return (0, jnp.clip(j - half, 0, half - 1))

    def out_map(j):
        return (0, jnp.maximum(j - hidden_steps, 0))

    in_specs = (
        [pl.BlockSpec(memory_space=pl.ANY)] * count
        + [pl.BlockSpec((row_count, 1), lambda j: (0, 0))]
        + [pl.BlockSpec((width, hidden_tile), own_map)] * 2
        + [pl.BlockSpec((width, hidden_tile), other_map)] * 2
        + [pl.BlockSpec((depth, out_tile), out_map)] * 2
    )
    flops = 2 * row_count * width * depth * 6
    return pl.pallas_call(
        functools.partial(expert_kernel, count, hidden_steps, hidden_tile),
        grid=(hidden_steps + out_steps,),
        in_specs=in_specs,
        out_specs=[pl.BlockSpec((height, out_tile), out_map)] * count,
        out_shape=[jax.ShapeDtypeStruct((height, width), jnp.bfloat16)] * count,
        scratch_shapes=[
            pltpu.VMEM((row_count, width), jnp.bfloat16),
            pltpu.VMEM((hidden_steps, row_count, hidden_tile), jnp.bfloat16),
            pltpu.SemaphoreType.DMA((count,)),
        ],
        compiler_params=pltpu.CompilerParams(vmem_limit_bytes=48 * 1024 * 1024),
        cost_estimate=pl.CostEstimate(
            flops=flops,
            bytes_accessed=2 * (6 * width * depth + 2 * row_count * width),
            transcendentals=row_count * 2 * depth,
        ),
    )(*blocks, scale, *weights)


def per_device(tokens, gate_ids, gate_values, w_gate, w_up, w_down):
    nodes = lax.axis_size("node")
    node = lax.axis_index("node")

    def cross(array, step):
        return lax.ppermute(array, "node", [(n, n ^ step) for n in range(nodes)])

    def swap(array):
        return lax.ppermute(array, "local", [(0, 1), (1, 0)])

    blocks = {0: tokens}
    for step in range(2, nodes, 2):
        blocks[step] = cross(tokens, step)
    for step in range(0, nodes, 2):
        blocks[step + 1] = cross(blocks[step], 1)

    own = [w_gate[0], w_up[0], w_down[0]]
    other = [swap(w) for w in own]
    weights = [own[0], own[1], other[0], other[1], own[2], other[2]]

    experts = jnp.arange(nodes, dtype=jnp.int32)
    chosen = gate_ids[:, :, None] == experts[None, None, :]
    table = jnp.sum(
        jnp.where(chosen, gate_values.astype(jnp.float32)[:, :, None], 0.0), axis=1
    ).astype(jnp.bfloat16)
    tables = lax.all_gather(table, "node", axis=0)
    mine = jnp.sum(
        jnp.where(experts == node, tables.astype(jnp.float32), 0.0), axis=2
    )
    source = (node ^ experts)[:, None] == experts[None, :]
    scales = jnp.sum(jnp.where(source[:, :, None], mine[None], 0.0), axis=1)

    group = min(nodes, 4)
    shares = {}
    for first in range(0, nodes, group):
        steps = range(first, first + group)
        scale = scales[first : first + group].reshape(-1, 1)
        results = expert_rows([blocks[s] for s in steps], scale, weights)
        shares.update(zip(steps, results))

    total = None
    for step in range(0, nodes, 2):
        part = shares[step].astype(jnp.float32) + cross(shares[step + 1], 1).astype(jnp.float32)
        if step:
            part = cross(part.astype(jnp.bfloat16), step).astype(jnp.float32)
        total = part if total is None else total + part
    return total.astype(jnp.bfloat16)


def solution(mesh):
    return jax.shard_map(
        per_device,
        mesh=mesh,
        in_specs=(
            P(("rep", "node", "local"), None),
            P(("rep", "node", "local"), None),
            P(("rep", "node", "local"), None),
            P("node", None, "local"),
            P("node", None, "local"),
            P("node", "local", None),
        ),
        out_specs=P(("rep", "node", "local"), None),
        check_vma=False,
    )
```

time: 445 us -> 289 us (0.65)
  blocking collectives: 168 us -> 57.1 us
  waiting for transfers between devices: 212 us -> 156 us
  Pallas kernels: 0 us -> 53.1 us
  matrix products: 42.2 us -> 0 us
  between operations: 13.5 us -> 0.12 us
  starting transfers between devices: 5.93 us -> 17.5 us
    all_to_all x1 -> x0, blocking collectives: 168 us -> none  [per_device(): lax.all_to_all(outgoing, 'node', split_axis=0, concat_axis=0, tiled=True)]
    all_to_all x1 -> x0, waiting for transfers between devices: 161 us -> none  [per_device(): lax.all_to_all(own_rows, 'node', split_axis=0, concat_axis=0, tiled=True)]
    ppermute x0 -> x17, waiting for transfers between devices: none -> 156 us  [the longest x14 156 us: cross(): return lax.ppermute(array, 'node', [(n, n ^ step) for n in range(nodes)])]
    all_gather x0 -> x1, blocking collectives: none -> 57.1 us  [per_device(): tables = lax.all_gather(table, 'node', axis=0)]
    pallas_call x0 -> x2, Pallas kernels: none -> 53.1 us  [expert_rows(): pl.pallas_call(functools.partial(expert_kernel, count, hidden_steps, hidd...]
    dot_general x5 -> x0, matrix products: 42.2 us -> none  [the longest x1 13.4 us: per_device(): up_act = jnp.dot(rows, w_up[0], preferred_element_type=jnp.float32)]
    all_gather x1 -> x0, waiting for transfers between devices: 26.1 us -> none  [per_device(): lax.all_gather(lax.all_to_all(outgoing, 'node', split_axis=0, concat_axis...]
    reduce_scatter x1 -> x0, waiting for transfers between devices: 25.2 us -> none  [per_device(): lax.psum_scatter(partial_value.astype(jnp.bfloat16), 'local', scatter_dim...]
  transfers between devices with their start and end apart: 3 -> 17, of which waited for: 3 -> 8; matrix products, arithmetic and copies ran while one was open for 0% -> 1% of each run, Pallas kernels for 0% -> 18%
where the time goes in v1:
time: 289 us
  waiting for transfers between devices  156 us (54%)
  blocking collectives  57.1 us (20%)
  Pallas kernels  53.1 us (18%)
  starting transfers between devices  17.5 us (6%)
  other arithmetic  3.75 us (1%)
    ppermute x14, waiting for transfers between devices, cross(): return lax.ppermute(array, 'node', [(n, n ^ step) for n in range(nodes)])  156 us
    all_gather x1, blocking collectives, per_device(): tables = lax.all_gather(table, 'node', axis=0)  57.1 us
    pallas_call x2, Pallas kernels, expert_rows(): pl.pallas_call(functools.partial(expert_kernel, count, hidden_steps, hidd...  53.1 us
    ppermute x14, starting transfers between devices, cross(): return lax.ppermute(array, 'node', [(n, n ^ step) for n in range(nodes)])  16.5 us
  transfers between devices with their start and end apart: 17, of which 8 were waited for; matrix products, arithmetic and copies ran while one was open for 1% of the time, Pallas kernels for 18%

profile of v1, /device:TPU:0, one launch (start us, length us, event | category | flops | bytes accessed | tf_op | source)
XLA Modules:
  0.0 288.8 jit_solution(12449639295361077789)
XLA Ops:
  0.0 0.5 collective-permute-start.3
  0.5 0.5 collective-permute-start.5
  1.0 3.6 %collective-permute-start.9 = (bf16[64,7168]{1,0:T(8,128)(2,1)}, bf16[64,7168]{1,0:T(8,128)(2,1)S(1)}, u32[]{:S(2)}, u32[]{:S(2)}) collective-permute-start(bf16[64,7168]{1,0:T(8,128)(2,1)} %refs_0_.1), channel_id=1, source_target_pairs={{0,8},{2,10},{4,12},{6,14},{8,0},{10,2},{12,4},{14,6},{1,9},{3,11}... | collective-permute-start | bytes 2752520 | tf_op jit(solution)/shard_map/ppermute | solution.py:118
  4.6 1.3 collective-permute-start.11
  5.9 59.4 %collective-permute-done.9.refs_0_ = bf16[64,7168]{1,0:T(8,128)(2,1)S(1)} collective-permute-done((bf16[64,7168]{1,0:T(8,128)(2,1)}, bf16[64,7168]{1,0:T(8,128)(2,1)S(1)}, u32[]{:S(2)}, u32[]{:S(2)}) %collective-permute-start.9) | collective-permute-done | bytes 917536 | tf_op jit(solution)/shard_map/ppermute | solution.py:118
  65.3 0.7 collective-permute-start.1
  66.0 0.7 convert_element_type.64
  66.7 1.5 collective-permute-start.10
  68.2 19.3 %collective-permute-done.1.refs_2_ = bf16[64,7168]{1,0:T(8,128)(2,1)S(1)} collective-permute-done((bf16[64,7168]{1,0:T(8,128)(2,1)}, bf16[64,7168]{1,0:T(8,128)(2,1)S(1)}, u32[]{:S(2)}, u32[]{:S(2)}) %collective-permute-start.1) | collective-permute-done | bytes 917536 | tf_op jit(solution)/shard_map/ppermute | solution.py:118
  87.5 1.4 collective-permute-start.12
  88.9 0.7 select_reduce_fusion.1
  89.6 57.1 %all-gather.1 = bf16[8,64,8]{1,2,0:T(8,128)(2,1)S(1)} all-gather(bf16[1,64,8]{1,2,0:T(8,128)(2,1)S(1)} %bitcast.15), channel_id=2, replica_groups=mesh['rep'=2,'node'=8,'local'=2] {'node'}, dimensions={0}, use_global_device_ids=true | all-gather | bytes 9216 | tf_op jit(solution)/shard_map/all_gather | solution.py:138
  147.2 1.6 collective-permute-start
  148.9 0.5 collective-permute-start.2
  149.4 26.5 %shard_map.65 = (bf16[64,7168]{1,0:T(8,128)(2,1)S(1)}, bf16[64,7168]{1,0:T(8,128)(2,1)S(1)}, bf16[64,7168]{1,0:T(8,128)(2,1)S(1)}, bf16[64,7168]{1,0:T(8,128)(2,1)S(1)}) custom-call(bf16[64,7168]{1,0:T(8,128)(2,1)S(1)} %collective-permute-done.9.refs_0_, bf16[64,7168]{1,0:T(8,128)(2,1)S(1)} %collective-permute-done.10.refs_1_, ...), custom_call_target="tpu_custom_call" | custom-call | flops 11274289152 | bytes 51380224 | tf_op jit(solution)/shard_map/pallas_call | solution.py:93
  175.9 1.6 collective-permute-start.13
  177.5 0.5 collective-permute-start.15
  178.0 12.5 %collective-permute-done.2.refs_3_ = bf16[64,7168]{1,0:T(8,128)(2,1)S(1)} collective-permute-done((bf16[64,7168]{1,0:T(8,128)(2,1)S(1)}, bf16[64,7168]{1,0:T(8,128)(2,1)S(1)}, u32[]{:S(2)}, u32[]{:S(2)}) %collective-permute-start.2) | collective-permute-done | bytes 917536 | tf_op jit(solution)/shard_map/ppermute | solution.py:118
  190.5 1.0 copy-done.2
  191.4 26.5 %shard_map.64 = (bf16[64,7168]{1,0:T(8,128)(2,1)S(1)}, bf16[64,7168]{1,0:T(8,128)(2,1)S(1)}, bf16[64,7168]{1,0:T(8,128)(2,1)S(1)}, bf16[64,7168]{1,0:T(8,128)(2,1)S(1)}) custom-call(bf16[64,7168]{1,0:T(8,128)(2,1)S(1)} %copy-done, bf16[64,7168]{1,0:T(8,128)(2,1)S(1)} %collective-permute-done.refs_1_, bf16[64,7168]{1,0:T(8,128)(2,1)} %copy-done.1, ...), custom_call_target="tpu_custom_call" | custom-call | flops 11274289152 | bytes 51380224 | tf_op jit(solution)/shard_map/pallas_call | solution.py:93
  218.0 1.6 collective-permute-start.7
  219.6 0.5 collective-permute-start.6
  220.0 0.2 add_convert_fusion.2
  220.3 9.4 %collective-permute-done.15 = bf16[64,7168]{1,0:T(8,128)(2,1)S(1)} collective-permute-done((bf16[64,7168]{1,0:T(8,128)(2,1)S(1)}, bf16[64,7168]{1,0:T(8,128)(2,1)S(1)}, u32[]{:S(2)}, u32[]{:S(2)}) %collective-permute-start.15) | collective-permute-done | bytes 917536 | tf_op jit(solution)/shard_map/ppermute | solution.py:118
  229.8 0.2 add_convert_fusion.1
  230.0 1.3 collective-permute-start.16
  231.3 18.1 %collective-permute-done.7 = bf16[64,7168]{1,0:T(8,128)(2,1)S(1)} collective-permute-done((bf16[64,7168]{1,0:T(8,128)(2,1)S(1)}, bf16[64,7168]{1,0:T(8,128)(2,1)S(1)}, u32[]{:S(2)}, u32[]{:S(2)}) %collective-permute-start.7) | collective-permute-done | bytes 917536 | tf_op jit(solution)/shard_map/ppermute | solution.py:118
  249.7 0.3 collective-permute-start.8
  250.0 12.7 %collective-permute-done.6 = bf16[64,7168]{1,0:T(8,128)(2,1)S(1)} collective-permute-done((bf16[64,7168]{1,0:T(8,128)(2,1)S(1)}, bf16[64,7168]{1,0:T(8,128)(2,1)S(1)}, u32[]{:S(2)}, u32[]{:S(2)}) %collective-permute-start.6) | collective-permute-done | bytes 917536 | tf_op jit(solution)/shard_map/ppermute | solution.py:118
  262.7 8.4 %collective-permute-done.14 = bf16[64,7168]{1,0:T(8,128)(2,1)S(1)} collective-permute-done((bf16[64,7168]{1,0:T(8,128)(2,1)S(1)}, bf16[64,7168]{1,0:T(8,128)(2,1)S(1)}, u32[]{:S(2)}, u32[]{:S(2)}) %collective-permute-start.14) | collective-permute-done | bytes 917536 | tf_op jit(solution)/shard_map/ppermute | solution.py:118
  271.1 16.2 %collective-permute-done.8 = bf16[64,7168]{1,0:T(8,128)(2,1)S(1)} collective-permute-done((bf16[64,7168]{1,0:T(8,128)(2,1)S(1)}, bf16[64,7168]{1,0:T(8,128)(2,1)S(1)}, u32[]{:S(2)}, u32[]{:S(2)}) %collective-permute-start.8) | collective-permute-done | bytes 917536 | tf_op jit(solution)/shard_map/ppermute | solution.py:118
  287.3 1.5 add_convert_fusion
  (25 shorter events, 0.9 us)
Async XLA Ops:
  0.0 149.3 %collective-permute-start.3 = (bf16[7168,512]{1,0:T(8,128)(2,1)}, bf16[7168,512]{1,0:T(8,128)(2,1)}, u32[]{:S(2)}, u32[]{:S(2)}) collective-permute-start(bf16[7168,512]{1,0:T(8,128)(2,1)} %bitcast.6), channel_id=1, source_target_pairs={{0,1},{1,0},{2,3},{3,2},{4,5},{5,4},{6,7},{7,6},{8,9},{9,8},{10,11... | collective-permute-start | bytes 22020104 | tf_op jit(solution)/shard_map/ppermute | solution.py:121
  0.5 148.9 %collective-permute-start.4 = (bf16[7168,512]{1,0:T(8,128)(2,1)}, bf16[7168,512]{1,0:T(8,128)(2,1)}, u32[]{:S(2)}, u32[]{:S(2)}) collective-permute-start(bf16[7168,512]{1,0:T(8,128)(2,1)} %bitcast.9), channel_id=1, source_target_pairs={{0,1},{1,0},{2,3},{3,2},{4,5},{5,4},{6,7},{7,6},{8,9},{9,8},{10,11... | collective-permute-start | bytes 22020104 | tf_op jit(solution)/shard_map/ppermute | solution.py:121
  0.5 148.8 %collective-permute-start.5 = (bf16[512,7168]{1,0:T(8,128)(2,1)}, bf16[512,7168]{1,0:T(8,128)(2,1)}, u32[]{:S(2)}, u32[]{:S(2)}) collective-permute-start(bf16[512,7168]{1,0:T(8,128)(2,1)} %bitcast.12), channel_id=1, source_target_pairs={{0,1},{1,0},{2,3},{3,2},{4,5},{5,4},{6,7},{7,6},{8,9},{9,8},{10,11... | collective-permute-start | bytes 22020104 | tf_op jit(solution)/shard_map/ppermute | solution.py:121
  1.0 64.3 %collective-permute-start.9 = (bf16[64,7168]{1,0:T(8,128)(2,1)}, bf16[64,7168]{1,0:T(8,128)(2,1)S(1)}, u32[]{:S(2)}, u32[]{:S(2)}) collective-permute-start(bf16[64,7168]{1,0:T(8,128)(2,1)} %refs_0_.1), channel_id=1, source_target_pairs={{0,8},{2,10},{4,12},{6,14},{8,0},{10,2},{12,4},{14,6},{1,9},{3,11}... | collective-permute-start | bytes 2752520 | tf_op jit(solution)/shard_map/ppermute | solution.py:118
  4.6 62.1 %collective-permute-start.11 = (bf16[64,7168]{1,0:T(8,128)(2,1)}, bf16[64,7168]{1,0:T(8,128)(2,1)}, u32[]{:S(2)}, u32[]{:S(2)}) collective-permute-start(bf16[64,7168]{1,0:T(8,128)(2,1)} %refs_0_.1), channel_id=1, source_target_pairs={{0,12},{2,14},{4,8},{6,10},{8,4},{10,6},{12,0},{14,2},{1,13},{3,15... | collective-permute-start | bytes 2752520 | tf_op jit(solution)/shard_map/ppermute | solution.py:118
  65.3 22.2 %collective-permute-start.1 = (bf16[64,7168]{1,0:T(8,128)(2,1)}, bf16[64,7168]{1,0:T(8,128)(2,1)S(1)}, u32[]{:S(2)}, u32[]{:S(2)}) collective-permute-start(bf16[64,7168]{1,0:T(8,128)(2,1)} %refs_0_.1), channel_id=1, source_target_pairs={{0,4},{2,6},{4,0},{6,2},{8,12},{10,14},{12,8},{14,10},{1,5},{3,7},... | collective-permute-start | bytes 2752520 | tf_op jit(solution)/shard_map/ppermute | solution.py:118
  66.7 80.6 %collective-permute-start.10 = (bf16[64,7168]{1,0:T(8,128)(2,1)S(1)}, bf16[64,7168]{1,0:T(8,128)(2,1)S(1)}, u32[]{:S(2)}, u32[]{:S(2)}) collective-permute-start(bf16[64,7168]{1,0:T(8,128)(2,1)S(1)} %collective-permute-done.9.refs_0_), channel_id=1, source_target_pairs={{0,2},{2,0},{4,6},{6,4},{8,10},{10,8},{12,14},{14,12},{1,3},{3,1},... | collective-permute-start | bytes 2752520 | tf_op jit(solution)/shard_map/ppermute | solution.py:118
  87.5 88.4 %copy-start.1 = (bf16[64,7168]{1,0:T(8,128)(2,1)}, bf16[64,7168]{1,0:T(8,128)(2,1)S(1)}, u32[]{:S(2)}) copy-start(bf16[64,7168]{1,0:T(8,128)(2,1)S(1)} %collective-permute-done.1.refs_2_) | copy-start | bytes 2752516
  87.5 61.4 %collective-permute-start.12 = (bf16[64,7168]{1,0:T(8,128)(2,1)}, bf16[64,7168]{1,0:T(8,128)(2,1)}, u32[]{:S(2)}, u32[]{:S(2)}) collective-permute-start(bf16[64,7168]{1,0:T(8,128)(2,1)} %collective-permute-done.11.refs_2_), channel_id=1, source_target_pairs={{0,2},{2,0},{4,6},{6,4},{8,10},{10,8},{12,14},{14,12},{1,3},{3,1},... | collective-permute-start | bytes 2752520 | tf_op jit(solution)/shard_map/ppermute | solution.py:118
  147.2 44.2 %copy-start = (bf16[64,7168]{1,0:T(8,128)(2,1)S(1)}, bf16[64,7168]{1,0:T(8,128)(2,1)}, u32[]{:S(2)}) copy-start(bf16[64,7168]{1,0:T(8,128)(2,1)} %refs_0_.1) | copy-start | bytes 2752516
  147.2 30.8 %collective-permute-start = (bf16[64,7168]{1,0:T(8,128)(2,1)}, bf16[64,7168]{1,0:T(8,128)(2,1)S(1)}, u32[]{:S(2)}, u32[]{:S(2)}) collective-permute-start(bf16[64,7168]{1,0:T(8,128)(2,1)} %refs_0_.1), channel_id=1, source_target_pairs={{0,2},{2,0},{4,6},{6,4},{8,10},{10,8},{12,14},{14,12},{1,3},{3,1},... | collective-permute-start | bytes 2752520 | tf_op jit(solution)/shard_map/ppermute | solution.py:118
  148.9 41.6 %collective-permute-start.2 = (bf16[64,7168]{1,0:T(8,128)(2,1)S(1)}, bf16[64,7168]{1,0:T(8,128)(2,1)S(1)}, u32[]{:S(2)}, u32[]{:S(2)}) collective-permute-start(bf16[64,7168]{1,0:T(8,128)(2,1)S(1)} %collective-permute-done.1.refs_2_), channel_id=1, source_target_pairs={{0,2},{2,0},{4,6},{6,4},{8,10},{10,8},{12,14},{14,12},{1,3},{3,1},... | collective-permute-start | bytes 2752520 | tf_op jit(solution)/shard_map/ppermute | solution.py:118
  175.9 44.1 %collective-permute-start.13 = (bf16[64,7168]{1,0:T(8,128)(2,1)S(1)}, bf16[64,7168]{1,0:T(8,128)(2,1)S(1)}, u32[]{:S(2)}, u32[]{:S(2)}) collective-permute-start(bf16[64,7168]{1,0:T(8,128)(2,1)S(1)} %get-tuple-element.18), channel_id=1, source_target_pairs={{0,2},{2,0},{4,6},{6,4},{8,10},{10,8},{12,14},{14,12},{1,3},{3,1},... | collective-permute-start | bytes 2752520 | tf_op jit(solution)/shard_map/ppermute | solution.py:118
  177.5 52.3 %collective-permute-start.15 = (bf16[64,7168]{1,0:T(8,128)(2,1)S(1)}, bf16[64,7168]{1,0:T(8,128)(2,1)S(1)}, u32[]{:S(2)}, u32[]{:S(2)}) collective-permute-start(bf16[64,7168]{1,0:T(8,128)(2,1)S(1)} %get-tuple-element.20), channel_id=1, source_target_pairs={{0,2},{2,0},{4,6},{6,4},{8,10},{10,8},{12,14},{14,12},{1,3},{3,1},... | collective-permute-start | bytes 2752520 | tf_op jit(solution)/shard_map/ppermute | solution.py:118
  190.5 1.0 copy-start.2
  218.0 31.5 %collective-permute-start.7 = (bf16[64,7168]{1,0:T(8,128)(2,1)S(1)}, bf16[64,7168]{1,0:T(8,128)(2,1)S(1)}, u32[]{:S(2)}, u32[]{:S(2)}) collective-permute-start(bf16[64,7168]{1,0:T(8,128)(2,1)S(1)} %get-tuple-element.16), channel_id=1, source_target_pairs={{0,2},{2,0},{4,6},{6,4},{8,10},{10,8},{12,14},{14,12},{1,3},{3,1},... | collective-permute-start | bytes 2752520 | tf_op jit(solution)/shard_map/ppermute | solution.py:118
  219.6 43.1 %collective-permute-start.6 = (bf16[64,7168]{1,0:T(8,128)(2,1)S(1)}, bf16[64,7168]{1,0:T(8,128)(2,1)S(1)}, u32[]{:S(2)}, u32[]{:S(2)}) collective-permute-start(bf16[64,7168]{1,0:T(8,128)(2,1)S(1)} %get-tuple-element.14), channel_id=1, source_target_pairs={{0,2},{2,0},{4,6},{6,4},{8,10},{10,8},{12,14},{14,12},{1,3},{3,1},... | collective-permute-start | bytes 2752520 | tf_op jit(solution)/shard_map/ppermute | solution.py:118
  220.3 50.9 %collective-permute-start.14 = (bf16[64,7168]{1,0:T(8,128)(2,1)S(1)}, bf16[64,7168]{1,0:T(8,128)(2,1)S(1)}, u32[]{:S(2)}, u32[]{:S(2)}) collective-permute-start(bf16[64,7168]{1,0:T(8,128)(2,1)S(1)} %add_convert_fusion.2), channel_id=1, source_target_pairs={{0,8},{2,10},{4,12},{6,14},{8,0},{10,2},{12,4},{14,6},{1,9},{3,11}... | collective-permute-start | bytes 2752520 | tf_op jit(solution)/shard_map/ppermute | solution.py:118
  230.0 41.1 %collective-permute-start.16 = (bf16[64,7168]{1,0:T(8,128)(2,1)S(1)}, bf16[64,7168]{1,0:T(8,128)(2,1)S(1)}, u32[]{:S(2)}, u32[]{:S(2)}) collective-permute-start(bf16[64,7168]{1,0:T(8,128)(2,1)S(1)} %add_convert_fusion.1), channel_id=1, source_target_pairs={{0,12},{2,14},{4,8},{6,10},{8,4},{10,6},{12,0},{14,2},{1,13},{3,15... | collective-permute-start | bytes 2752520 | tf_op jit(solution)/shard_map/ppermute | solution.py:118
  249.7 37.6 %collective-permute-start.8 = (bf16[64,7168]{1,0:T(8,128)(2,1)S(1)}, bf16[64,7168]{1,0:T(8,128)(2,1)S(1)}, u32[]{:S(2)}, u32[]{:S(2)}) collective-permute-start(bf16[64,7168]{1,0:T(8,128)(2,1)S(1)} %add_convert_fusion.3), channel_id=1, source_target_pairs={{0,4},{2,6},{4,0},{6,2},{8,12},{10,14},{12,8},{14,10},{1,5},{3,7},... | collective-permute-start | bytes 2752520 | tf_op jit(solution)/shard_map/ppermute | solution.py:118

commit v2 on v0

v2 whole, which is shorter than its diff:
```python
import functools

import jax
import jax.numpy as jnp
from jax import lax
from jax.experimental import pallas as pl
from jax.experimental.pallas import tpu as pltpu
from jax.sharding import PartitionSpec as P

LANES = 128
RING = 4
KERNEL_VMEM = 54 * 1024 * 1024


def divisor_tile(extent, most, unit):
    best = unit
    for tile in range(unit, most + 1, unit):
        if extent % tile == 0:
            best = tile
    return best


def expert_kernel(count, slab, out_tile, *refs):
    blocks = refs[:count]
    node, gate_own, up_own, gate_other, up_other, down_own, down_other = refs[count : count + 7]
    results = refs[count + 7 : 2 * count + 7]
    rows, gates, ups, downs, gate_sum, up_sum, hidden, staged = refs[2 * count + 7 : 2 * count + 15]
    block_sem, gate_sem, up_sem, down_sem, out_sem = refs[2 * count + 15 :]
    height = blocks[0].shape[0]
    _, width, depth = gate_own.shape
    slabs = width // slab
    tiles = width // out_tile

    def block_copy(i):
        return pltpu.make_async_copy(
            blocks[i], rows.at[pl.ds(i * height, height)], block_sem.at[i]
        )

    def slab_copies(gate, up, index, slot):
        place = pl.ds(pl.multiple_of(index * slab, slab), slab)
        return (
            pltpu.make_async_copy(gate.at[0, place], gates.at[slot], gate_sem.at[slot]),
            pltpu.make_async_copy(up.at[0, place], ups.at[slot], up_sem.at[slot]),
        )

    def down_copies(tile):
        slot = lax.rem(tile, RING)
        place = pl.ds(pl.multiple_of(tile * out_tile, out_tile), out_tile)
        return (
            pltpu.make_async_copy(down_own.at[0, :, place], downs.at[slot, 0], down_sem.at[slot, 0]),
            pltpu.make_async_copy(down_other.at[0, :, place], downs.at[slot, 1], down_sem.at[slot, 1]),
        )

    def start_load(index):
        slot = lax.rem(index, RING)

        @pl.when(index < slabs)
        def own():
            for copy in slab_copies(gate_own, up_own, index, slot):
                copy.start()

        @pl.when((index >= slabs) & (index < 2 * slabs))
        def other():
            for copy in slab_copies(gate_other, up_other, index - slabs, slot):
                copy.start()

        @pl.when((index >= 2 * slabs) & (index < 2 * slabs + tiles))
        def down():
            for copy in down_copies(index - 2 * slabs):
                copy.start()

    def out_copies(tile, slot):
        place = pl.ds(pl.multiple_of(tile * out_tile, out_tile), out_tile)
        return [
            pltpu.make_async_copy(
                staged.at[slot, pl.ds(i * height, height)],
                results[i].at[:, place],
                out_sem.at[slot, i],
            )
            for i in range(count)
        ]

    for i in range(count):
        block_copy(i).start()
    for index in range(RING):
        start_load(jnp.int32(index))
    for i in range(count):
        block_copy(i).wait()

    def project(index, half):
        slot = lax.rem(index, RING)
        local = index - half * slabs
        for copy in slab_copies(gate_own, up_own, local, slot):
            copy.wait()
        piece = rows[:, pl.ds(pl.multiple_of(local * slab, slab), slab)]
        gate_part = jnp.dot(piece, gates[slot], preferred_element_type=jnp.float32)
        up_part = jnp.dot(piece, ups[slot], preferred_element_type=jnp.float32)

        @pl.when(local == 0)
        def first():
            gate_sum[...] = gate_part
            up_sum[...] = up_part

        @pl.when(local > 0)
        def later():
            gate_sum[...] += gate_part
            up_sum[...] += up_part

        start_load(index + RING)

    for half in range(2):
        lax.fori_loop(
            half * slabs, (half + 1) * slabs, lambda i, _, half=half: project(i, half), None
        )
        act = gate_sum[...]
        hidden[half] = (act / (1.0 + jnp.exp(-act)) * up_sum[...]).astype(jnp.bfloat16)

    table = rows[:, width:].astype(jnp.float32)
    lane = lax.broadcasted_iota(jnp.int32, table.shape, 1)
    scale = jnp.sum(jnp.where(lane == node[0], table, 0.0), axis=1, keepdims=True)

    def down(tile, _):
        slot = lax.rem(tile, RING)
        out_slot = lax.rem(tile, 2)
        for copy in down_copies(tile):
            copy.wait()
        total = jnp.dot(hidden[0], downs[slot, 0], preferred_element_type=jnp.float32)
        total += jnp.dot(hidden[1], downs[slot, 1], preferred_element_type=jnp.float32)
        start_load(2 * slabs + tile + RING)

        @pl.when(tile >= 2)
        def free():
            for copy in out_copies(tile - 2, out_slot):
                copy.wait()

        staged[out_slot] = (total * scale).astype(jnp.bfloat16)
        for copy in out_copies(tile, out_slot):
            copy.start()

    lax.fori_loop(0, tiles, down, None)
    for tile in range(max(0, tiles - 2), tiles):
        for copy in out_copies(tile, tile % 2):
            copy.wait()


def expert_rows(blocks, node, weights):
    count = len(blocks)
    height, total_width = blocks[0].shape
    _, width, depth = weights[0].shape
    slab = divisor_tile(width, 1024, 128)
    out_tile = divisor_tile(width, 1024, 128)
    tiles = width // out_tile
    row_count = count * height
    anywhere = pl.BlockSpec(memory_space=pl.ANY)
    return pl.pallas_call(
        functools.partial(expert_kernel, count, slab, out_tile),
        in_specs=[anywhere] * count
        + [pl.BlockSpec(memory_space=pltpu.SMEM)]
        + [pl.BlockSpec(memory_space=pltpu.HBM)] * 6,
        out_specs=[anywhere] * count,
        out_shape=[jax.ShapeDtypeStruct((height, width), jnp.bfloat16)] * count,
        scratch_shapes=[
            pltpu.VMEM((row_count, total_width), jnp.bfloat16),
            pltpu.VMEM((RING, slab, depth), jnp.bfloat16),
            pltpu.VMEM((RING, slab, depth), jnp.bfloat16),
            pltpu.VMEM((RING, 2, depth, out_tile), jnp.bfloat16),
            pltpu.VMEM((row_count, depth), jnp.float32),
            pltpu.VMEM((row_count, depth), jnp.float32),
            pltpu.VMEM((2, row_count, depth), jnp.bfloat16),
            pltpu.VMEM((2, row_count, out_tile), jnp.bfloat16),
            pltpu.SemaphoreType.DMA((count,)),
            pltpu.SemaphoreType.DMA((RING,)),
            pltpu.SemaphoreType.DMA((RING,)),
            pltpu.SemaphoreType.DMA((RING, 2)),
            pltpu.SemaphoreType.DMA((2, count)),
        ],
        compiler_params=pltpu.CompilerParams(vmem_limit_bytes=KERNEL_VMEM),
        cost_estimate=pl.CostEstimate(
            flops=12 * row_count * width * depth,
            bytes_accessed=2 * (6 * width * depth + 2 * row_count * width),
            transcendentals=2 * row_count * depth,
        ),
    )(*blocks, node, *weights)


def joined(*arrays):
    return lax.optimization_barrier(arrays)


def plus(*arrays):
    total = arrays[0].astype(jnp.float32)
    for array in arrays[1:]:
        total = total + array.astype(jnp.float32)
    return total.astype(jnp.bfloat16)


def per_device(tokens, gate_ids, gate_values, w_gate, w_up, w_down):
    nodes = lax.axis_size("node")
    node = lax.axis_index("node")

    def send(array, pairs):
        return lax.ppermute(array, "node", pairs)

    def cross(array, step):
        return send(array, [(n, n ^ step) for n in range(nodes)])

    def swap(array):
        return lax.ppermute(array, "local", [(0, 1), (1, 0)])

    lanes = jnp.arange(LANES, dtype=jnp.int32)
    chosen = gate_ids[:, :, None] == lanes[None, None, :]
    table = jnp.sum(
        jnp.where(chosen, gate_values.astype(jnp.float32)[:, :, None], 0.0), axis=1
    ).astype(jnp.bfloat16)
    mine = jnp.concatenate([tokens, table], axis=1)

    place = node.astype(jnp.int32).reshape(1)

    def experts(others, *blocks):
        weights = [w_gate, w_up, others[0], others[1], w_down, others[2]]
        return expert_rows(blocks, place, weights)

    halves = (w_gate, w_up, w_down)
    if nodes == 8:
        return line_plan(mine, node, send, cross, swap, halves, experts)
    others = [swap(half) for half in halves]
    return direct_plan(mine, nodes, cross, functools.partial(experts, others))


def line_plan(mine, node, send, cross, swap, halves, experts):
    middle = [(2, 4), (4, 2), (3, 5), (5, 3)]
    outward = [(2, 0), (3, 1), (4, 6), (5, 7)]
    inward = [(b, a) for a, b in outward]
    inner = (node >= 2) & (node < 6)

    s0, (w_gate, w_up, w_down) = mine, halves
    s1, m2, t0, v_gate, w_up, w_down = joined(
        cross(s0, 2), send(s0, middle), cross(s0, 1), swap(w_gate), w_up, w_down
    )
    e2, m3, t1, v_up, v_down = joined(
        send(m2, outward), send(s1, middle), cross(s1, 1), swap(w_up), swap(w_down)
    )
    experts = functools.partial(experts, (v_gate, v_up, v_down))
    s2 = jnp.where(inner, m2, e2)
    e3, t2, p0, q0, p1, q1 = joined(send(m3, outward), cross(s2, 1), *experts(s0, t0, s1, t1))
    s3 = jnp.where(inner, m3, e3)
    t3, p2, q2, p3 = joined(cross(s3, 1), *experts(s2, t2, s3))
    q3, y2 = joined(*experts(t3), cross(q2, 1))

    p2 = plus(p2, y2)
    y3, i2 = joined(cross(q3, 1), send(p2, inward))
    p3, p2 = plus(p3, y3), plus(p2, i2)
    i3, f2, y1 = joined(send(p3, inward), send(p2, middle), cross(q1, 1))
    p3, p1 = plus(p3, i3), plus(p1, y1)
    i1, y0 = joined(send(p3, middle), cross(q0, 1))
    p1 = plus(p1, i1)
    return plus(p0, y0, cross(p1, 2), f2)


def direct_plan(mine, nodes, cross, experts):
    blocks = {0: mine}
    for step in range(2, nodes, 2):
        blocks[step] = cross(mine, step)
    for step in range(0, nodes, 2):
        blocks[step + 1] = cross(blocks[step], 1)
    shares = {}
    group = min(nodes, 4)
    for first in range(0, nodes, group):
        steps = range(first, first + group)
        shares.update(zip(steps, experts(*[blocks[s] for s in steps])))
    sums = []
    for step in range(0, nodes, 2):
        part = plus(shares[step], cross(shares[step + 1], 1))
        sums.append(cross(part, step) if step else part)
    return plus(*sums)


def solution(mesh):
    return jax.shard_map(
        per_device,
        mesh=mesh,
        in_specs=(
            P(("rep", "node", "local"), None),
            P(("rep", "node", "local"), None),
            P(("rep", "node", "local"), None),
            P("node", None, "local"),
            P("node", None, "local"),
            P("node", "local", None),
        ),
        out_specs=P(("rep", "node", "local"), None),
        check_vma=False,
    )
```

time: 445 us -> 208 us (0.47)
  blocking collectives: 168 us -> 0 us
  waiting for transfers between devices: 212 us -> 113 us
  Pallas kernels: 0 us -> 57.5 us
  matrix products: 42.2 us -> 0 us
  starting transfers between devices: 5.93 us -> 29.1 us
  between operations: 13.5 us -> 0.31 us
  other arithmetic: 1.69 us -> 6.69 us
    all_to_all x1 -> x0, blocking collectives: 168 us -> none  [per_device(): lax.all_to_all(outgoing, 'node', split_axis=0, concat_axis=0, tiled=True)]
    all_to_all x1 -> x0, waiting for transfers between devices: 161 us -> none  [per_device(): lax.all_to_all(own_rows, 'node', split_axis=0, concat_axis=0, tiled=True)]
    ppermute x0 -> x21, waiting for transfers between devices: none -> 113 us  [the longest x18 113 us: send(): return lax.ppermute(array, 'node', pairs)]
    pallas_call x0 -> x3, Pallas kernels: none -> 57.5 us  [expert_rows(): pl.pallas_call(functools.partial(expert_kernel, count, slab, out_tile), i...]
    dot_general x5 -> x0, matrix products: 42.2 us -> none  [the longest x1 13.4 us: per_device(): up_act = jnp.dot(rows, w_up[0], preferred_element_type=jnp.float32)]
    ppermute x0 -> x21, starting transfers between devices: none -> 29.1 us  [the longest x18 28.2 us: send(): return lax.ppermute(array, 'node', pairs)]
    all_gather x1 -> x0, waiting for transfers between devices: 26.1 us -> none  [per_device(): lax.all_gather(lax.all_to_all(outgoing, 'node', split_axis=0, concat_axis...]
    reduce_scatter x1 -> x0, waiting for transfers between devices: 25.2 us -> none  [per_device(): lax.psum_scatter(partial_value.astype(jnp.bfloat16), 'local', scatter_dim...]
  transfers between devices with their start and end apart: 3 -> 21, of which waited for: 3 -> 11; matrix products, arithmetic and copies ran while one was open for 0% -> 2% of each run, Pallas kernels for 0% -> 28%
where the time goes in v2:
time: 208 us
  waiting for transfers between devices  113 us (54%)
  Pallas kernels  57.5 us (28%)
  starting transfers between devices  29.1 us (14%)
  other arithmetic  6.69 us (3%)
    ppermute x18, waiting for transfers between devices, send(): return lax.ppermute(array, 'node', pairs)  113 us
    pallas_call x3, Pallas kernels, expert_rows(): pl.pallas_call(functools.partial(expert_kernel, count, slab, out_tile), i...  57.5 us
    ppermute x18, starting transfers between devices, send(): return lax.ppermute(array, 'node', pairs)  28.2 us
  transfers between devices with their start and end apart: 21, of which 11 were waited for; matrix products, arithmetic and copies ran while one was open for 2% of the time, Pallas kernels for 28%

profile of v2, /device:TPU:0, one launch (start us, length us, event | category | flops | bytes accessed | tf_op | source)
XLA Modules:
  0.0 207.5 jit_solution(6173801338479668233)
XLA Ops:
  0.5 0.7 convert_element_type.75
  1.1 0.8 select_reduce_fusion
  2.0 1.2 pad_maximum_fusion.refs_0_
  3.2 2.6 %collective-permute-start.2 = (bf16[64,7296]{1,0:T(8,128)(2,1)S(1)}, bf16[64,7296]{1,0:T(8,128)(2,1)S(1)}, u32[]{:S(2)}, u32[]{:S(2)}) collective-permute-start(bf16[64,7296]{1,0:T(8,128)(2,1)S(1)} %pad_maximum_fusion.refs_0_), channel_id=1, source_target_pairs={{0,2},{2,0},{4,6},{6,4},{8,10},{10,8},{12,14},{14,12},{1,3},{3,1},... | collective-permute-start | bytes 2801672 | tf_op jit(solution)/shard_map/ppermute | solution.py:202
  5.8 0.7 collective-permute-start.1
  6.5 4.4 %collective-permute-start = (bf16[64,7296]{1,0:T(8,128)(2,1)S(1)}, bf16[64,7296]{1,0:T(8,128)(2,1)}, u32[]{:S(2)}, u32[]{:S(2)}) collective-permute-start(bf16[64,7296]{1,0:T(8,128)(2,1)S(1)} %pad_maximum_fusion.refs_0_), channel_id=1, source_target_pairs={{0,4},{2,6},{4,0},{6,2},{8,12},{10,14},{12,8},{14,10},{1,5},{3,7},... | collective-permute-start | bytes 2801672 | tf_op jit(solution)/shard_map/ppermute | solution.py:202
  10.9 16.2 %collective-permute-done.2.refs_1_ = bf16[64,7296]{1,0:T(8,128)(2,1)S(1)} collective-permute-done((bf16[64,7296]{1,0:T(8,128)(2,1)S(1)}, bf16[64,7296]{1,0:T(8,128)(2,1)S(1)}, u32[]{:S(2)}, u32[]{:S(2)}) %collective-permute-start.2) | collective-permute-done | bytes 933920 | tf_op jit(solution)/shard_map/ppermute | solution.py:202
  27.2 4.7 %collective-permute-done.refs_2_ = bf16[64,7296]{1,0:T(8,128)(2,1)} collective-permute-done((bf16[64,7296]{1,0:T(8,128)(2,1)S(1)}, bf16[64,7296]{1,0:T(8,128)(2,1)}, u32[]{:S(2)}, u32[]{:S(2)}) %collective-permute-start) | collective-permute-done | bytes 933920 | tf_op jit(solution)/shard_map/ppermute | solution.py:202
  32.3 1.3 collective-permute-start.4
  34.2 0.7 collective-permute-start.5
  34.9 22.0 %collective-permute-done.4 = bf16[64,7296]{1,0:T(8,128)(2,1)} collective-permute-done((bf16[64,7296]{1,0:T(8,128)(2,1)S(1)}, bf16[64,7296]{1,0:T(8,128)(2,1)}, u32[]{:S(2)}, u32[]{:S(2)}) %collective-permute-start.4) | collective-permute-done | bytes 933920 | tf_op jit(solution)/shard_map/ppermute | solution.py:202
  57.0 1.3 broadcast_select_fusion.1.refs_0_
  58.9 1.3 collective-permute-start.9
  60.1 22.2 %shard_map.64 = (bf16[64,7168]{1,0:T(8,128)(2,1)}, bf16[64,7168]{1,0:T(8,128)(2,1)}, bf16[64,7168]{1,0:T(8,128)(2,1)}, bf16[64,7168]{1,0:T(8,128)(2,1)}) custom-call(bf16[64,7296]{1,0:T(8,128)(2,1)} %copy-done.2, bf16[64,7296]{1,0:T(8,128)(2,1)} %copy-done.4, bf16[64,7296]{1,0:T(8,128)(2,1)} %collective-permute-done.refs_2_, ...), custom_call_target="tpu_custom_call" | custom-call | flops 11274289152 | bytes 51380224 | tf_op jit(solution)/shard_map/pallas_call | solution.py:155
  82.4 1.6 collective-permute-done.9
  85.1 18.8 %shard_map.65 = (bf16[64,7168]{1,0:T(8,128)(2,1)}, bf16[64,7168]{1,0:T(8,128)(2,1)}, bf16[64,7168]{1,0:T(8,128)(2,1)}) custom-call(bf16[64,7296]{1,0:T(8,128)(2,1)} %copy-done, bf16[64,7296]{1,0:T(8,128)(2,1)} %copy-done.3, bf16[64,7296]{1,0:T(8,128)(2,1)} %copy-done.1, s32[1]{0:T(128)} %bitcast.refs_4_.refs_3_.refs_1_, bf16[1,7168,512]{2,1,0:T(8,128)(2,1)} %refs_2_.1, ...), custom_call_target="tpu_custom_call" | custom-call | flops 8455716864 | bytes 49545216 | tf_op jit(solution)/shard_map/pallas_call | solution.py:155
  104.4 1.2 collective-permute-start.12
  105.6 16.5 %shard_map.66 = bf16[64,7168]{1,0:T(8,128)(2,1)} custom-call(bf16[64,7296]{1,0:T(8,128)(2,1)} %copy-done.5, s32[1]{0:T(128)} %bitcast.refs_4_.refs_3_.refs_1_, bf16[1,7168,512]{2,1,0:T(8,128)(2,1)} %refs_2_.1, bf16[1,7168,512]{2,1,0:T(8,128)(2,1)} %refs_3_.1, bf16[1,7168,512]{2,1,0:T(8,128)(2,1)} %collective-permute-done.3.refs_7_.refs_6_.refs_4_, ...), custom_call_target="tpu_custom_call" | custom-call | flops 2818572288 | bytes 45875200 | tf_op jit(solution)/shard_map/pallas_call | solution.py:155
  122.2 1.9 collective-permute-done.12
  124.3 6.1 %collective-permute-start.14 = (bf16[64,7168]{1,0:T(8,128)(2,1)S(1)}, bf16[64,7168]{1,0:T(8,128)(2,1)S(1)}, u32[]{:S(2)}, u32[]{:S(2)}) collective-permute-start(bf16[64,7168]{1,0:T(8,128)(2,1)S(1)} %add_convert_fusion.6), channel_id=1, source_target_pairs={{0,4},{2,6},{12,8},{14,10},{1,5},{3,7},{13,9},{15,11},{16,20},{18,... | collective-permute-start | bytes 2752520 | tf_op jit(solution)/shard_map/ppermute | solution.py:202
  130.5 0.8 collective-permute-start.13
  131.2 1.3 collective-permute-start.17
  132.6 14.0 %collective-permute-done.14 = bf16[64,7168]{1,0:T(8,128)(2,1)S(1)} collective-permute-done((bf16[64,7168]{1,0:T(8,128)(2,1)S(1)}, bf16[64,7168]{1,0:T(8,128)(2,1)S(1)}, u32[]{:S(2)}, u32[]{:S(2)}) %collective-permute-start.14) | collective-permute-done | bytes 917536 | tf_op jit(solution)/shard_map/ppermute | solution.py:202
  146.6 7.2 %collective-permute-done.13 = bf16[64,7168]{1,0:T(8,128)(2,1)S(1)} collective-permute-done((bf16[64,7168]{1,0:T(8,128)(2,1)S(1)}, bf16[64,7168]{1,0:T(8,128)(2,1)S(1)}, u32[]{:S(2)}, u32[]{:S(2)}) %collective-permute-start.13) | collective-permute-done | bytes 917536 | tf_op jit(solution)/shard_map/ppermute | solution.py:202
  154.0 0.9 collective-permute-start.16
  155.1 3.1 %collective-permute-start.15 = (bf16[64,7168]{1,0:T(8,128)(2,1)S(1)}, bf16[64,7168]{1,0:T(8,128)(2,1)S(1)}, u32[]{:S(2)}, u32[]{:S(2)}) collective-permute-start(bf16[64,7168]{1,0:T(8,128)(2,1)S(1)} %add_convert_fusion.5), channel_id=1, source_target_pairs={{0,4},{2,6},{12,8},{14,10},{1,5},{3,7},{13,9},{15,11},{16,20},{18,... | collective-permute-start | bytes 2752520 | tf_op jit(solution)/shard_map/ppermute | solution.py:202
  158.2 0.8 collective-permute-start.19
  159.0 14.5 %collective-permute-done.17 = bf16[64,7168]{1,0:T(8,128)(2,1)S(1)} collective-permute-done((bf16[64,7168]{1,0:T(8,128)(2,1)S(1)}, bf16[64,7168]{1,0:T(8,128)(2,1)S(1)}, u32[]{:S(2)}, u32[]{:S(2)}) %collective-permute-start.17) | collective-permute-done | bytes 917536 | tf_op jit(solution)/shard_map/ppermute | solution.py:202
  173.7 0.9 collective-permute-start.18
  174.6 13.7 %collective-permute-done.19 = bf16[64,7168]{1,0:T(8,128)(2,1)S(1)} collective-permute-done((bf16[64,7168]{1,0:T(8,128)(2,1)S(1)}, bf16[64,7168]{1,0:T(8,128)(2,1)S(1)}, u32[]{:S(2)}, u32[]{:S(2)}) %collective-permute-start.19) | collective-permute-done | bytes 917536 | tf_op jit(solution)/shard_map/ppermute | solution.py:202
  189.1 17.0 %collective-permute-done.20 = bf16[64,7168]{1,0:T(8,128)(2,1)S(1)} collective-permute-done((bf16[64,7168]{1,0:T(8,128)(2,1)S(1)}, bf16[64,7168]{1,0:T(8,128)(2,1)S(1)}, u32[]{:S(2)}, u32[]{:S(2)}) %collective-permute-start.20) | collective-permute-done | bytes 917536 | tf_op jit(solution)/shard_map/ppermute | solution.py:202
  206.2 1.4 add_convert_fusion
  (50 shorter events, 5.5 us)
Async XLA Ops:
  0.0 31.8 %collective-permute-start.3 = (bf16[1,7168,512]{2,1,0:T(8,128)(2,1)}, bf16[1,7168,512]{2,1,0:T(8,128)(2,1)}, u32[]{:S(2)}, u32[]{:S(2)}) collective-permute-start(bf16[1,7168,512]{2,1,0:T(8,128)(2,1)} %refs_2_.1), channel_id=1, source_target_pairs={{0,1},{1,0},{2,3},{3,2},{4,5},{5,4},{6,7},{7,6},{8,9},{9,8},{10,11... | collective-permute-start | bytes 22020104 | tf_op jit(solution)/shard_map/ppermute | solution.py:208
  3.2 56.9 %copy-start.2 = (bf16[64,7296]{1,0:T(8,128)(2,1)}, bf16[64,7296]{1,0:T(8,128)(2,1)S(1)}, u32[]{:S(2)}) copy-start(bf16[64,7296]{1,0:T(8,128)(2,1)S(1)} %pad_maximum_fusion.refs_0_) | copy-start | bytes 2801668
  3.2 24.0 %collective-permute-start.2 = (bf16[64,7296]{1,0:T(8,128)(2,1)S(1)}, bf16[64,7296]{1,0:T(8,128)(2,1)S(1)}, u32[]{:S(2)}, u32[]{:S(2)}) collective-permute-start(bf16[64,7296]{1,0:T(8,128)(2,1)S(1)} %pad_maximum_fusion.refs_0_), channel_id=1, source_target_pairs={{0,2},{2,0},{4,6},{6,4},{8,10},{10,8},{12,14},{14,12},{1,3},{3,1},... | collective-permute-start | bytes 2801672 | tf_op jit(solution)/shard_map/ppermute | solution.py:202
  5.8 21.4 %collective-permute-start.1 = (bf16[64,7296]{1,0:T(8,128)(2,1)S(1)}, bf16[64,7296]{1,0:T(8,128)(2,1)S(1)}, u32[]{:S(2)}, u32[]{:S(2)}) collective-permute-start(bf16[64,7296]{1,0:T(8,128)(2,1)S(1)} %pad_maximum_fusion.refs_0_), channel_id=1, source_target_pairs={{4,8},{8,4},{6,10},{10,6},{5,9},{9,5},{7,11},{11,7},{20,24},{24,20... | collective-permute-start | bytes 2801672 | tf_op jit(solution)/shard_map/ppermute | solution.py:202
  6.5 25.3 %collective-permute-start = (bf16[64,7296]{1,0:T(8,128)(2,1)S(1)}, bf16[64,7296]{1,0:T(8,128)(2,1)}, u32[]{:S(2)}, u32[]{:S(2)}) collective-permute-start(bf16[64,7296]{1,0:T(8,128)(2,1)S(1)} %pad_maximum_fusion.refs_0_), channel_id=1, source_target_pairs={{0,4},{2,6},{4,0},{6,2},{8,12},{10,14},{12,8},{14,10},{1,5},{3,7},... | collective-permute-start | bytes 2801672 | tf_op jit(solution)/shard_map/ppermute | solution.py:202
  27.2 6.5 %copy-start.4 = (bf16[64,7296]{1,0:T(8,128)(2,1)}, bf16[64,7296]{1,0:T(8,128)(2,1)S(1)}, u32[]{:S(2)}) copy-start(bf16[64,7296]{1,0:T(8,128)(2,1)S(1)} %collective-permute-done.2.refs_1_) | copy-start | bytes 2801668
  31.8 25.1 %collective-permute-start.7 = (bf16[1,7168,512]{2,1,0:T(8,128)(2,1)}, bf16[1,7168,512]{2,1,0:T(8,128)(2,1)}, u32[]{:S(2)}, u32[]{:S(2)}) collective-permute-start(bf16[1,7168,512]{2,1,0:T(8,128)(2,1)} %refs_3_.1), channel_id=1, source_target_pairs={{0,1},{1,0},{2,3},{3,2},{4,5},{5,4},{6,7},{7,6},{8,9},{9,8},{10,11... | collective-permute-start | bytes 22020104 | tf_op jit(solution)/shard_map/ppermute | solution.py:208
  31.8 25.1 %collective-permute-start.8 = (bf16[1,512,7168]{2,1,0:T(8,128)(2,1)}, bf16[1,512,7168]{2,1,0:T(8,128)(2,1)}, u32[]{:S(2)}, u32[]{:S(2)}) collective-permute-start(bf16[1,512,7168]{2,1,0:T(8,128)(2,1)} %refs_6_.3), channel_id=1, source_target_pairs={{0,1},{1,0},{2,3},{3,2},{4,5},{5,4},{6,7},{7,6},{8,9},{9,8},{10,11... | collective-permute-start | bytes 22020104 | tf_op jit(solution)/shard_map/ppermute | solution.py:208
  32.3 24.6 %collective-permute-start.4 = (bf16[64,7296]{1,0:T(8,128)(2,1)S(1)}, bf16[64,7296]{1,0:T(8,128)(2,1)}, u32[]{:S(2)}, u32[]{:S(2)}) collective-permute-start(bf16[64,7296]{1,0:T(8,128)(2,1)S(1)} %collective-permute-done.1), channel_id=1, source_target_pairs={{4,0},{6,2},{8,12},{10,14},{5,1},{7,3},{9,13},{11,15},{20,16},{22,... | collective-permute-start | bytes 2801672 | tf_op jit(solution)/shard_map/ppermute | solution.py:202
  33.6 23.3 %collective-permute-start.6 = (bf16[64,7296]{1,0:T(8,128)(2,1)}, bf16[64,7296]{1,0:T(8,128)(2,1)}, u32[]{:S(2)}, u32[]{:S(2)}) collective-permute-start(bf16[64,7296]{1,0:T(8,128)(2,1)} %collective-permute-done.refs_2_), channel_id=1, source_target_pairs={{0,2},{2,0},{4,6},{6,4},{8,10},{10,8},{12,14},{14,12},{1,3},{3,1},... | collective-permute-start | bytes 2801672 | tf_op jit(solution)/shard_map/ppermute | solution.py:202
  34.2 22.7 %collective-permute-start.5 = (bf16[64,7296]{1,0:T(8,128)(2,1)}, bf16[64,7296]{1,0:T(8,128)(2,1)S(1)}, u32[]{:S(2)}, u32[]{:S(2)}) collective-permute-start(bf16[64,7296]{1,0:T(8,128)(2,1)} %collective-permute-done.refs_2_), channel_id=1, source_target_pairs={{4,8},{8,4},{6,10},{10,6},{5,9},{9,5},{7,11},{11,7},{20,24},{24,20... | collective-permute-start | bytes 2801672 | tf_op jit(solution)/shard_map/ppermute | solution.py:202
  58.3 24.1 %copy-start = (bf16[64,7296]{1,0:T(8,128)(2,1)}, bf16[64,7296]{1,0:T(8,128)(2,1)S(1)}, u32[]{:S(2)}) copy-start(bf16[64,7296]{1,0:T(8,128)(2,1)S(1)} %broadcast_select_fusion.1.refs_0_) | copy-start | bytes 2801668
  58.3 24.1 %collective-permute-start.10 = (bf16[64,7296]{1,0:T(8,128)(2,1)S(1)}, bf16[64,7296]{1,0:T(8,128)(2,1)S(1)}, u32[]{:S(2)}, u32[]{:S(2)}) collective-permute-start(bf16[64,7296]{1,0:T(8,128)(2,1)S(1)} %broadcast_select_fusion.1.refs_0_), channel_id=1, source_target_pairs={{0,2},{2,0},{4,6},{6,4},{8,10},{10,8},{12,14},{14,12},{1,3},{3,1},... | collective-permute-start | bytes 2801672 | tf_op jit(solution)/shard_map/ppermute | solution.py:202
  58.9 25.2 %collective-permute-start.9 = (bf16[64,7296]{1,0:T(8,128)(2,1)S(1)}, bf16[64,7296]{1,0:T(8,128)(2,1)S(1)}, u32[]{:S(2)}, u32[]{:S(2)}) collective-permute-start(bf16[64,7296]{1,0:T(8,128)(2,1)S(1)} %collective-permute-done.5), channel_id=1, source_target_pairs={{4,0},{6,2},{8,12},{10,14},{5,1},{7,3},{9,13},{11,15},{20,16},{22,... | collective-permute-start | bytes 2801672 | tf_op jit(solution)/shard_map/ppermute | solution.py:202
  82.4 2.3 %copy-start.3 = (bf16[64,7296]{1,0:T(8,128)(2,1)}, bf16[64,7296]{1,0:T(8,128)(2,1)S(1)}, u32[]{:S(2)}) copy-start(bf16[64,7296]{1,0:T(8,128)(2,1)S(1)} %collective-permute-done.10.refs_1_) | copy-start | bytes 2801668
  84.1 20.3 %collective-permute-start.11 = (bf16[64,7296]{1,0:T(8,128)(2,1)S(1)}, bf16[64,7296]{1,0:T(8,128)(2,1)S(1)}, u32[]{:S(2)}, u32[]{:S(2)}) collective-permute-start(bf16[64,7296]{1,0:T(8,128)(2,1)S(1)} %broadcast_select_fusion.refs_2_), channel_id=1, source_target_pairs={{0,2},{2,0},{4,6},{6,4},{8,10},{10,8},{12,14},{14,12},{1,3},{3,1},... | collective-permute-start | bytes 2801672 | tf_op jit(solution)/shard_map/ppermute | solution.py:202
  104.4 19.7 %copy-start.10 = (bf16[64,7168]{1,0:T(8,128)(2,1)S(1)}, bf16[64,7168]{1,0:T(8,128)(2,1)}, u32[]{:S(2)}) copy-start(bf16[64,7168]{1,0:T(8,128)(2,1)} %get-tuple-element.67) | copy-start | bytes 2752516
  104.4 19.7 %collective-permute-start.12 = (bf16[64,7168]{1,0:T(8,128)(2,1)}, bf16[64,7168]{1,0:T(8,128)(2,1)S(1)}, u32[]{:S(2)}, u32[]{:S(2)}) collective-permute-start(bf16[64,7168]{1,0:T(8,128)(2,1)} %get-tuple-element.65), channel_id=1, source_target_pairs={{0,2},{2,0},{4,6},{6,4},{8,10},{10,8},{12,14},{14,12},{1,3},{3,1},... | collective-permute-start | bytes 2752520 | tf_op jit(solution)/shard_map/ppermute | solution.py:202
  122.1 8.3 %copy-start.9 = (bf16[64,7168]{1,0:T(8,128)(2,1)S(1)}, bf16[64,7168]{1,0:T(8,128)(2,1)}, u32[]{:S(2)}) copy-start(bf16[64,7168]{1,0:T(8,128)(2,1)} %shard_map.66) | copy-start | bytes 2752516
  122.2 9.1 %copy-start.12 = (bf16[64,7168]{1,0:T(8,128)(2,1)S(1)}, bf16[64,7168]{1,0:T(8,128)(2,1)}, u32[]{:S(2)}) copy-start(bf16[64,7168]{1,0:T(8,128)(2,1)} %get-tuple-element.71) | copy-start | bytes 2752516
  124.3 30.6 %copy-start.8 = (bf16[64,7168]{1,0:T(8,128)(2,1)S(1)}, bf16[64,7168]{1,0:T(8,128)(2,1)}, u32[]{:S(2)}) copy-start(bf16[64,7168]{1,0:T(8,128)(2,1)} %get-tuple-element.63) | copy-start | bytes 2752516
  124.3 22.3 %collective-permute-start.14 = (bf16[64,7168]{1,0:T(8,128)(2,1)S(1)}, bf16[64,7168]{1,0:T(8,128)(2,1)S(1)}, u32[]{:S(2)}, u32[]{:S(2)}) collective-permute-start(bf16[64,7168]{1,0:T(8,128)(2,1)S(1)} %add_convert_fusion.6), channel_id=1, source_target_pairs={{0,4},{2,6},{12,8},{14,10},{1,5},{3,7},{13,9},{15,11},{16,20},{18,... | collective-permute-start | bytes 2752520 | tf_op jit(solution)/shard_map/ppermute | solution.py:202
  130.5 23.4 %collective-permute-start.13 = (bf16[64,7168]{1,0:T(8,128)(2,1)S(1)}, bf16[64,7168]{1,0:T(8,128)(2,1)S(1)}, u32[]{:S(2)}, u32[]{:S(2)}) collective-permute-start(bf16[64,7168]{1,0:T(8,128)(2,1)S(1)} %copy-done.9), channel_id=1, source_target_pairs={{0,2},{2,0},{4,6},{6,4},{8,10},{10,8},{12,14},{14,12},{1,3},{3,1},... | collective-permute-start | bytes 2752520 | tf_op jit(solution)/shard_map/ppermute | solution.py:202
  131.2 42.3 %collective-permute-start.17 = (bf16[64,7168]{1,0:T(8,128)(2,1)S(1)}, bf16[64,7168]{1,0:T(8,128)(2,1)S(1)}, u32[]{:S(2)}, u32[]{:S(2)}) collective-permute-start(bf16[64,7168]{1,0:T(8,128)(2,1)S(1)} %copy-done.12), channel_id=1, source_target_pairs={{0,2},{2,0},{4,6},{6,4},{8,10},{10,8},{12,14},{14,12},{1,3},{3,1},... | collective-permute-start | bytes 2752520 | tf_op jit(solution)/shard_map/ppermute | solution.py:202
  154.0 4.2 %copy-start.11 = (bf16[64,7168]{1,0:T(8,128)(2,1)S(1)}, bf16[64,7168]{1,0:T(8,128)(2,1)}, u32[]{:S(2)}) copy-start(bf16[64,7168]{1,0:T(8,128)(2,1)} %get-tuple-element.73) | copy-start | bytes 2752516
  154.0 19.4 %collective-permute-start.16 = (bf16[64,7168]{1,0:T(8,128)(2,1)S(1)}, bf16[64,7168]{1,0:T(8,128)(2,1)S(1)}, u32[]{:S(2)}, u32[]{:S(2)}) collective-permute-start(bf16[64,7168]{1,0:T(8,128)(2,1)S(1)} %add_convert_fusion.4), channel_id=1, source_target_pairs={{4,8},{8,4},{6,10},{10,6},{5,9},{9,5},{7,11},{11,7},{20,24},{24,20... | collective-permute-start | bytes 2752520 | tf_op jit(solution)/shard_map/ppermute | solution.py:202
  155.1 33.1 %copy-start.6 = (bf16[64,7168]{1,0:T(8,128)(2,1)S(1)}, bf16[64,7168]{1,0:T(8,128)(2,1)}, u32[]{:S(2)}) copy-start(bf16[64,7168]{1,0:T(8,128)(2,1)} %get-tuple-element.75) | copy-start | bytes 2752516
  155.1 18.3 %collective-permute-start.15 = (bf16[64,7168]{1,0:T(8,128)(2,1)S(1)}, bf16[64,7168]{1,0:T(8,128)(2,1)S(1)}, u32[]{:S(2)}, u32[]{:S(2)}) collective-permute-start(bf16[64,7168]{1,0:T(8,128)(2,1)S(1)} %add_convert_fusion.5), channel_id=1, source_target_pairs={{0,4},{2,6},{12,8},{14,10},{1,5},{3,7},{13,9},{15,11},{16,20},{18,... | collective-permute-start | bytes 2752520 | tf_op jit(solution)/shard_map/ppermute | solution.py:202
  158.2 30.0 %collective-permute-start.19 = (bf16[64,7168]{1,0:T(8,128)(2,1)S(1)}, bf16[64,7168]{1,0:T(8,128)(2,1)S(1)}, u32[]{:S(2)}, u32[]{:S(2)}) collective-permute-start(bf16[64,7168]{1,0:T(8,128)(2,1)S(1)} %copy-done.11), channel_id=1, source_target_pairs={{0,2},{2,0},{4,6},{6,4},{8,10},{10,8},{12,14},{14,12},{1,3},{3,1},... | collective-permute-start | bytes 2752520 | tf_op jit(solution)/shard_map/ppermute | solution.py:202
  173.7 32.5 %copy-start.7 = (bf16[64,7168]{1,0:T(8,128)(2,1)S(1)}, bf16[64,7168]{1,0:T(8,128)(2,1)}, u32[]{:S(2)}) copy-start(bf16[64,7168]{1,0:T(8,128)(2,1)} %get-tuple-element.57) | copy-start | bytes 2752516
  173.7 14.6 %collective-permute-start.18 = (bf16[64,7168]{1,0:T(8,128)(2,1)S(1)}, bf16[64,7168]{1,0:T(8,128)(2,1)S(1)}, u32[]{:S(2)}, u32[]{:S(2)}) collective-permute-start(bf16[64,7168]{1,0:T(8,128)(2,1)S(1)} %add_convert_fusion.3), channel_id=1, source_target_pairs={{4,8},{8,4},{6,10},{10,6},{5,9},{9,5},{7,11},{11,7},{20,24},{24,20... | collective-permute-start | bytes 2752520 | tf_op jit(solution)/shard_map/ppermute | solution.py:202
  188.6 17.6 %collective-permute-start.20 = (bf16[64,7168]{1,0:T(8,128)(2,1)S(1)}, bf16[64,7168]{1,0:T(8,128)(2,1)S(1)}, u32[]{:S(2)}, u32[]{:S(2)}) collective-permute-start(bf16[64,7168]{1,0:T(8,128)(2,1)S(1)} %add_convert_fusion.1), channel_id=1, source_target_pairs={{0,4},{2,6},{4,0},{6,2},{8,12},{10,14},{12,8},{14,10},{1,5},{3,7},... | collective-permute-start | bytes 2752520 | tf_op jit(solution)/shard_map/ppermute | solution.py:202
  (2 other events, 2.1 us)

commit v3 on v2

--- a/solution.py
+++ b/solution.py
@@ -8,7 +8,7 @@
 from jax.sharding import PartitionSpec as P
 
 LANES = 128
-RING = 4
+RING = 3
 KERNEL_VMEM = 54 * 1024 * 1024
 
 
@@ -26,14 +26,15 @@
     results = refs[count + 7 : 2 * count + 7]
     rows, gates, ups, downs, gate_sum, up_sum, hidden, staged = refs[2 * count + 7 : 2 * count + 15]
     block_sem, gate_sem, up_sem, down_sem, out_sem = refs[2 * count + 15 :]
-    height = blocks[0].shape[0]
+    heights = [block.shape[0] for block in blocks]
+    starts = [sum(heights[:i]) for i in range(count)]
     _, width, depth = gate_own.shape
     slabs = width // slab
     tiles = width // out_tile
 
     def block_copy(i):
         return pltpu.make_async_copy(
-            blocks[i], rows.at[pl.ds(i * height, height)], block_sem.at[i]
+            blocks[i], rows.at[pl.ds(starts[i], heights[i])], block_sem.at[i]
         )
 
     def slab_copies(gate, up, index, slot):
@@ -73,7 +74,7 @@
         place = pl.ds(pl.multiple_of(tile * out_tile, out_tile), out_tile)
         return [
             pltpu.make_async_copy(
-                staged.at[slot, pl.ds(i * height, height)],
+                staged.at[slot, pl.ds(starts[i], heights[i])],
                 results[i].at[:, place],
                 out_sem.at[slot, i],
             )
@@ -145,12 +146,12 @@
 
 def expert_rows(blocks, node, weights):
     count = len(blocks)
-    height, total_width = blocks[0].shape
+    total_width = blocks[0].shape[1]
     _, width, depth = weights[0].shape
-    slab = divisor_tile(width, 1024, 128)
+    slab = divisor_tile(width, 1792, 128)
     out_tile = divisor_tile(width, 1024, 128)
     tiles = width // out_tile
-    row_count = count * height
+    row_count = sum(block.shape[0] for block in blocks)
     anywhere = pl.BlockSpec(memory_space=pl.ANY)
     return pl.pallas_call(
         functools.partial(expert_kernel, count, slab, out_tile),
@@ -158,7 +159,7 @@
         + [pl.BlockSpec(memory_space=pltpu.SMEM)]
         + [pl.BlockSpec(memory_space=pltpu.HBM)] * 6,
         out_specs=[anywhere] * count,
-        out_shape=[jax.ShapeDtypeStruct((height, width), jnp.bfloat16)] * count,
+        out_shape=[jax.ShapeDtypeStruct((block.shape[0], width), jnp.bfloat16) for block in blocks],
         scratch_shapes=[
             pltpu.VMEM((row_count, total_width), jnp.bfloat16),
             pltpu.VMEM((RING, slab, depth), jnp.bfloat16),
@@ -234,27 +235,36 @@
     inner = (node >= 2) & (node < 6)
 
     s0, (w_gate, w_up, w_down) = mine, halves
-    s1, m2, t0, v_gate, w_up, w_down = joined(
-        cross(s0, 2), send(s0, middle), cross(s0, 1), swap(w_gate), w_up, w_down
-    )
+    cut = mine.shape[0] // 2
+    v_gate, v_up = swap(w_gate), swap(w_up)
+    s1, m2, t0, w_down = joined(cross(s0, 2), send(s0, middle), cross(s0, 1), w_down)
+    v_gate, w_down = joined(v_gate, w_down)
     e2, m3, t1, v_up, v_down = joined(
-        send(m2, outward), send(s1, middle), cross(s1, 1), swap(w_up), swap(w_down)
+        send(m2, outward), send(s1, middle), cross(s1, 1), v_up, swap(w_down)
     )
     experts = functools.partial(experts, (v_gate, v_up, v_down))
     s2 = jnp.where(inner, m2, e2)
-    e3, t2, p0, q0, p1, q1 = joined(send(m3, outward), cross(s2, 1), *experts(s0, t0, s1, t1))
+    e3, t2, n3, q1, p2 = joined(
+        send(m3, outward), cross(s2, 1), send(t1[cut:], middle), *experts(t1, s2)
+    )
+    t3, o3, m3, e3 = joined(
+        cross(jnp.where(inner, m3[:cut], e3[:cut]), 1), send(n3, outward), m3, e3
+    )
     s3 = jnp.where(inner, m3, e3)
-    t3, p2, q2, p3 = joined(cross(s3, 1), *experts(s2, t2, s3))
-    q3, y2 = joined(*experts(t3), cross(q2, 1))
-
-    p2 = plus(p2, y2)
-    y3, i2 = joined(cross(q3, 1), send(p2, inward))
-    p3, p2 = plus(p3, y3), plus(p2, i2)
-    i3, f2, y1 = joined(send(p3, inward), send(p2, middle), cross(q1, 1))
-    p3, p1 = plus(p3, i3), plus(p1, y1)
-    i1, y0 = joined(send(p3, middle), cross(q0, 1))
-    p1 = plus(p1, i1)
-    return plus(p0, y0, cross(p1, 2), f2)
+    q2, p3, q3, r3, s0, t0, s1 = joined(
+        *experts(t2, s3, t3, jnp.where(inner, n3, o3)), s0, t0, s1
+    )
+
+    y3, v3 = joined(cross(q3, 1), send(r3, inward))
+    p3, r3 = jnp.concatenate([plus(p3[:cut], y3), p3[cut:]]), plus(r3, v3)
+    i3, y2, v1 = joined(send(p3, inward), cross(q2, 1), send(r3, middle))
+    p3, p2, q1 = plus(p3, i3), plus(p2, y2), jnp.concatenate([q1[:cut], plus(q1[cut:], v1)])
+    p3, p2, q1, s0, t0, s1 = joined(p3, p2, q1, s0, t0, s1)
+    i1, i2, y1, p0, q0, p1 = joined(
+        send(p3, middle), send(p2, inward), cross(q1, 1), *experts(s0, t0, s1)
+    )
+    p1, p2 = plus(p1, y1, i1), plus(p2, i2)
+    return plus(p0, cross(q0, 1), cross(p1, 2), send(p2, middle))
 
 
 def direct_plan(mine, nodes, cross, experts):

time: 208 us -> 196 us (0.942)
  waiting for transfers between devices: 113 us -> 93.7 us
  other arithmetic: 6.69 us -> 11 us
  Pallas kernels: 57.5 us -> 54.9 us
  starting transfers between devices: 29.1 us -> 31.3 us
    ppermute x18 -> x22, waiting for transfers between devices: 113 us -> 93.7 us  [send(): return lax.ppermute(array, 'node', pairs)]
    ppermute x18 -> x22, starting transfers between devices: 28.2 us -> 30.9 us  [send(): return lax.ppermute(array, 'node', pairs)]
    pallas_call x3, Pallas kernels: 57.5 us -> 54.9 us  [expert_rows(): pl.pallas_call(functools.partial(expert_kernel, count, slab, out_tile), i...]
    convert_element_type x6 -> x7, other arithmetic: 2.55 us -> 4.9 us  [plus(): return total.astype(jnp.bfloat16)]
  transfers between devices with their start and end apart: 21 -> 25, of which waited for: 11 -> 13; matrix products, arithmetic and copies ran while one was open for 2% -> 3% of each run, Pallas kernels for 28% -> 19%
where the time goes in v3:
time: 196 us; the launch traced here: 194 us
  waiting for transfers between devices  93.7 us (48%)
  Pallas kernels  54.9 us (28%)
  starting transfers between devices  31.3 us (16%)
  other arithmetic  11 us (6%)
  local copies, waits for them, and re-layouts  2.15 us (1%)
    ppermute x22, waiting for transfers between devices, send(): return lax.ppermute(array, 'node', pairs)  93.7 us
    pallas_call x3, Pallas kernels, expert_rows(): pl.pallas_call(functools.partial(expert_kernel, count, slab, out_tile), i...  54.9 us
    ppermute x22, starting transfers between devices, send(): return lax.ppermute(array, 'node', pairs)  30.9 us
    convert_element_type x7, other arithmetic, plus(): return total.astype(jnp.bfloat16)  4.9 us
  transfers between devices with their start and end apart: 25, of which 13 were waited for; matrix products, arithmetic and copies ran while one was open for 3% of the time, Pallas kernels for 19%

profile of v3, /device:TPU:0, one launch (start us, length us, event | category | flops | bytes accessed | tf_op | source)
XLA Modules:
  0.0 193.5 jit_solution(4097352311096801949)
XLA Ops:
  2.0 1.2 pad_maximum_fusion.refs_0_
  3.2 2.6 %collective-permute-start = (bf16[64,7296]{1,0:T(8,128)(2,1)S(1)}, bf16[64,7296]{1,0:T(8,128)(2,1)}, u32[]{:S(2)}, u32[]{:S(2)}) collective-permute-start(bf16[64,7296]{1,0:T(8,128)(2,1)S(1)} %pad_maximum_fusion.refs_0_), channel_id=1, source_target_pairs={{0,4},{2,6},{4,0},{6,2},{8,12},{10,14},{12,8},{14,10},{1,5},{3,7},... | collective-permute-start | bytes 2801672 | tf_op jit(solution)/shard_map/ppermute | solution.py:203
  5.8 1.7 collective-permute-start.1
  7.5 1.5 collective-permute-start.2
  9.1 18.3 %collective-permute-done.refs_2_ = bf16[64,7296]{1,0:T(8,128)(2,1)} collective-permute-done((bf16[64,7296]{1,0:T(8,128)(2,1)S(1)}, bf16[64,7296]{1,0:T(8,128)(2,1)}, u32[]{:S(2)}, u32[]{:S(2)}) %collective-permute-start) | collective-permute-done | bytes 933920 | tf_op jit(solution)/shard_map/ppermute | solution.py:203
  27.3 3.0 %collective-permute-done.2.refs_1_ = bf16[64,7296]{1,0:T(8,128)(2,1)S(1)} collective-permute-done((bf16[64,7296]{1,0:T(8,128)(2,1)S(1)}, bf16[64,7296]{1,0:T(8,128)(2,1)S(1)}, u32[]{:S(2)}, u32[]{:S(2)}) %collective-permute-start.2) | collective-permute-done | bytes 933920 | tf_op jit(solution)/shard_map/ppermute | solution.py:203
  32.1 1.6 collective-permute-start.5
  33.7 1.3 collective-permute-start.3
  35.0 19.5 %collective-permute-done.5.refs_0_ = bf16[64,7296]{1,0:T(8,128)(2,1)S(1)} collective-permute-done((bf16[64,7296]{1,0:T(8,128)(2,1)}, bf16[64,7296]{1,0:T(8,128)(2,1)S(1)}, u32[]{:S(2)}, u32[]{:S(2)}) %collective-permute-start.5) | collective-permute-done | bytes 933920 | tf_op jit(solution)/shard_map/ppermute | solution.py:203
  54.5 5.3 %collective-permute-done.3 = bf16[64,7296]{1,0:T(8,128)(2,1)} collective-permute-done((bf16[64,7296]{1,0:T(8,128)(2,1)}, bf16[64,7296]{1,0:T(8,128)(2,1)}, u32[]{:S(2)}, u32[]{:S(2)}) %collective-permute-start.3) | collective-permute-done | bytes 933920 | tf_op jit(solution)/shard_map/ppermute | solution.py:203
  59.8 1.3 broadcast_select_fusion.1.refs_1_
  61.7 1.3 collective-permute-start.9
  63.7 17.5 %shard_map.64 = (bf16[64,7168]{1,0:T(8,128)(2,1)}, bf16[64,7168]{1,0:T(8,128)(2,1)}) custom-call(bf16[64,7296]{1,0:T(8,128)(2,1)} %copy-done.2, bf16[64,7296]{1,0:T(8,128)(2,1)} %copy-done.1, s32[1]{0:T(128)} %bitcast.refs_2_.refs_4_.refs_3_, bf16[1,7168,512]{2,1,0:T(8,128)(2,1)} %refs_4_.3, bf16[1,7168,512]{2,1,0:T(8,128)(2,1)} %refs_5_.3, ...), custom_call_target="tpu_custom_call" | custom-call | flops 5637144576 | bytes 47710208 | tf_op jit(solution)/shard_map/pallas_call | solution.py:156
  82.2 2.1 %collective-permute-done.9 = bf16[64,7296]{1,0:T(8,128)(2,1)S(1)} collective-permute-done((bf16[64,7296]{1,0:T(8,128)(2,1)S(1)}, bf16[64,7296]{1,0:T(8,128)(2,1)S(1)}, u32[]{:S(2)}, u32[]{:S(2)}) %collective-permute-start.9) | collective-permute-done | bytes 933920 | tf_op jit(solution)/shard_map/ppermute | solution.py:203
  84.3 1.6 collective-permute-start.12
  85.9 1.3 collective-permute-start.13
  87.2 7.0 %collective-permute-done.12.refs_2_ = bf16[32,7296]{1,0:T(8,128)(2,1)S(1)} collective-permute-done((bf16[32,7296]{1,0:T(8,128)(2,1)S(1)}, bf16[32,7296]{1,0:T(8,128)(2,1)S(1)}, u32[]{:S(2)}, u32[]{:S(2)}) %collective-permute-start.12) | collective-permute-done | bytes 466976 | tf_op jit(solution)/shard_map/ppermute | solution.py:203
  94.2 3.7 %collective-permute-done.13 = bf16[32,7296]{1,0:T(8,128)(2,1)S(1)} collective-permute-done((bf16[32,7296]{1,0:T(8,128)(2,1)S(1)}, bf16[32,7296]{1,0:T(8,128)(2,1)S(1)}, u32[]{:S(2)}, u32[]{:S(2)}) %collective-permute-start.13) | collective-permute-done | bytes 466976 | tf_op jit(solution)/shard_map/ppermute | solution.py:203
  99.7 18.7 %shard_map.65 = (bf16[64,7168]{1,0:T(8,128)(2,1)}, bf16[64,7168]{1,0:T(8,128)(2,1)}, bf16[32,7168]{1,0:T(8,128)(2,1)}, bf16[32,7168]{1,0:T(8,128)(2,1)}) custom-call(bf16[64,7296]{1,0:T(8,128)(2,1)} %copy-done.4, bf16[64,7296]{1,0:T(8,128)(2,1)} %broadcast_select_fusion.refs_1_, bf16[32,7296]{1,0:T(8,128)(2,1)} %copy-done.8, ...), custom_call_target="tpu_custom_call" | custom-call | flops 8455716864 | bytes 49545216 | tf_op jit(solution)/shard_map/pallas_call | solution.py:156
  119.0 2.3 %collective-permute-start.15 = (bf16[32,7168]{1,0:T(8,128)(2,1)}, bf16[32,7168]{1,0:T(8,128)(2,1)S(1)}, u32[]{:S(2)}, u32[]{:S(2)}) collective-permute-start(bf16[32,7168]{1,0:T(8,128)(2,1)} %get-tuple-element.84), channel_id=1, source_target_pairs={{0,4},{2,6},{12,8},{14,10},{1,5},{3,7},{13,9},{15,11},{16,20},{18,... | collective-permute-start | bytes 1376264 | tf_op jit(solution)/shard_map/ppermute | solution.py:203
  123.1 9.1 %collective-permute-done.14 = bf16[32,7168]{1,0:T(8,128)(2,1)S(1)} collective-permute-done((bf16[32,7168]{1,0:T(8,128)(2,1)}, bf16[32,7168]{1,0:T(8,128)(2,1)S(1)}, u32[]{:S(2)}, u32[]{:S(2)}) %collective-permute-start.14) | collective-permute-done | bytes 458784 | tf_op jit(solution)/shard_map/ppermute | solution.py:203
  132.1 1.1 add_convert_fusion.7
  133.4 1.6 collective-permute-start.16
  136.0 11.3 %collective-permute-done.17 = bf16[64,7168]{1,0:T(8,128)(2,1)S(1)} collective-permute-done((bf16[64,7168]{1,0:T(8,128)(2,1)}, bf16[64,7168]{1,0:T(8,128)(2,1)S(1)}, u32[]{:S(2)}, u32[]{:S(2)}) %collective-permute-start.17) | collective-permute-done | bytes 917536 | tf_op jit(solution)/shard_map/ppermute | solution.py:203
  147.3 1.2 collective-permute-done.16
  149.9 6.2 %collective-permute-start.20 = (bf16[64,7168]{1,0:T(8,128)(2,1)S(1)}, bf16[64,7168]{1,0:T(8,128)(2,1)S(1)}, u32[]{:S(2)}, u32[]{:S(2)}) collective-permute-start(bf16[64,7168]{1,0:T(8,128)(2,1)S(1)} %get-tuple-element.97), channel_id=1, source_target_pairs={{0,4},{2,6},{12,8},{14,10},{1,5},{3,7},{13,9},{15,11},{16,20},{18,... | collective-permute-start | bytes 2752520 | tf_op jit(solution)/shard_map/ppermute | solution.py:203
  156.9 18.7 %shard_map.66 = (bf16[64,7168]{1,0:T(8,128)(2,1)}, bf16[64,7168]{1,0:T(8,128)(2,1)}, bf16[64,7168]{1,0:T(8,128)(2,1)}) custom-call(bf16[64,7296]{1,0:T(8,128)(2,1)} %copy-done, bf16[64,7296]{1,0:T(8,128)(2,1)} %copy-done.3, bf16[64,7296]{1,0:T(8,128)(2,1)} %collective-permute-done.refs_2_, s32[1]{0:T(128)} %bitcast.refs_2_.refs_4_.refs_3_, ...), custom_call_target="tpu_custom_call" | custom-call | flops 8455716864 | bytes 49545216 | tf_op jit(solution)/shard_map/pallas_call | solution.py:156
  175.7 1.5 add_convert_fusion.2
  178.4 1.3 collective-permute-start.22
  179.7 11.3 %collective-permute-done.23 = bf16[64,7168]{1,0:T(8,128)(2,1)S(1)} collective-permute-done((bf16[64,7168]{1,0:T(8,128)(2,1)S(1)}, bf16[64,7168]{1,0:T(8,128)(2,1)S(1)}, u32[]{:S(2)}, u32[]{:S(2)}) %collective-permute-start.23) | collective-permute-done | bytes 917536 | tf_op jit(solution)/shard_map/ppermute | solution.py:203
  191.0 1.2 collective-permute-done.22
  192.1 1.4 add_convert_fusion
  (62 shorter events, 14.5 us)
Async XLA Ops:
  0.0 30.4 %collective-permute-start.7 = (bf16[1,7168,512]{2,1,0:T(8,128)(2,1)}, bf16[1,7168,512]{2,1,0:T(8,128)(2,1)}, u32[]{:S(2)}, u32[]{:S(2)}) collective-permute-start(bf16[1,7168,512]{2,1,0:T(8,128)(2,1)} %refs_4_.3), channel_id=1, source_target_pairs={{0,1},{1,0},{2,3},{3,2},{4,5},{5,4},{6,7},{7,6},{8,9},{9,8},{10,11... | collective-permute-start | bytes 22020104 | tf_op jit(solution)/shard_map/ppermute | solution.py:209
  3.2 59.8 %copy-start = (bf16[64,7296]{1,0:T(8,128)(2,1)}, bf16[64,7296]{1,0:T(8,128)(2,1)S(1)}, u32[]{:S(2)}) copy-start(bf16[64,7296]{1,0:T(8,128)(2,1)S(1)} %pad_maximum_fusion.refs_0_) | copy-start | bytes 2801668
  3.2 24.1 %collective-permute-start = (bf16[64,7296]{1,0:T(8,128)(2,1)S(1)}, bf16[64,7296]{1,0:T(8,128)(2,1)}, u32[]{:S(2)}, u32[]{:S(2)}) collective-permute-start(bf16[64,7296]{1,0:T(8,128)(2,1)S(1)} %pad_maximum_fusion.refs_0_), channel_id=1, source_target_pairs={{0,4},{2,6},{4,0},{6,2},{8,12},{10,14},{12,8},{14,10},{1,5},{3,7},... | collective-permute-start | bytes 2801672 | tf_op jit(solution)/shard_map/ppermute | solution.py:203
  5.8 21.5 %collective-permute-start.1 = (bf16[64,7296]{1,0:T(8,128)(2,1)S(1)}, bf16[64,7296]{1,0:T(8,128)(2,1)}, u32[]{:S(2)}, u32[]{:S(2)}) collective-permute-start(bf16[64,7296]{1,0:T(8,128)(2,1)S(1)} %pad_maximum_fusion.refs_0_), channel_id=1, source_target_pairs={{4,8},{8,4},{6,10},{10,6},{5,9},{9,5},{7,11},{11,7},{20,24},{24,20... | collective-permute-start | bytes 2801672 | tf_op jit(solution)/shard_map/ppermute | solution.py:203
  7.5 22.8 %collective-permute-start.2 = (bf16[64,7296]{1,0:T(8,128)(2,1)S(1)}, bf16[64,7296]{1,0:T(8,128)(2,1)S(1)}, u32[]{:S(2)}, u32[]{:S(2)}) collective-permute-start(bf16[64,7296]{1,0:T(8,128)(2,1)S(1)} %pad_maximum_fusion.refs_0_), channel_id=1, source_target_pairs={{0,2},{2,0},{4,6},{6,4},{8,10},{10,8},{12,14},{14,12},{1,3},{3,1},... | collective-permute-start | bytes 2801672 | tf_op jit(solution)/shard_map/ppermute | solution.py:203
  9.0 50.7 %collective-permute-start.6 = (bf16[1,7168,512]{2,1,0:T(8,128)(2,1)}, bf16[1,7168,512]{2,1,0:T(8,128)(2,1)}, u32[]{:S(2)}, u32[]{:S(2)}) collective-permute-start(bf16[1,7168,512]{2,1,0:T(8,128)(2,1)} %refs_5_.3), channel_id=1, source_target_pairs={{0,1},{1,0},{2,3},{3,2},{4,5},{5,4},{6,7},{7,6},{8,9},{9,8},{10,11... | collective-permute-start | bytes 22020104 | tf_op jit(solution)/shard_map/ppermute | solution.py:209
  30.4 29.4 %collective-permute-start.8 = (bf16[1,512,7168]{2,1,0:T(8,128)(2,1)}, bf16[1,512,7168]{2,1,0:T(8,128)(2,1)}, u32[]{:S(2)}, u32[]{:S(2)}) collective-permute-start(bf16[1,512,7168]{2,1,0:T(8,128)(2,1)} %refs_8_.1), channel_id=1, source_target_pairs={{0,1},{1,0},{2,3},{3,2},{4,5},{5,4},{6,7},{7,6},{8,9},{9,8},{10,11... | collective-permute-start | bytes 22020104 | tf_op jit(solution)/shard_map/ppermute | solution.py:209
  31.4 3.6 %collective-permute-start.4 = (bf16[64,7296]{1,0:T(8,128)(2,1)}, bf16[64,7296]{1,0:T(8,128)(2,1)S(1)}, u32[]{:S(2)}, u32[]{:S(2)}) collective-permute-start(bf16[64,7296]{1,0:T(8,128)(2,1)} %collective-permute-done.refs_2_), channel_id=1, source_target_pairs={{4,8},{8,4},{6,10},{10,6},{5,9},{9,5},{7,11},{11,7},{20,24},{24,20... | collective-permute-start | bytes 2801672 | tf_op jit(solution)/shard_map/ppermute | solution.py:203
  32.1 22.4 %collective-permute-start.5 = (bf16[64,7296]{1,0:T(8,128)(2,1)}, bf16[64,7296]{1,0:T(8,128)(2,1)S(1)}, u32[]{:S(2)}, u32[]{:S(2)}) collective-permute-start(bf16[64,7296]{1,0:T(8,128)(2,1)} %collective-permute-done.refs_2_), channel_id=1, source_target_pairs={{0,2},{2,0},{4,6},{6,4},{8,10},{10,8},{12,14},{14,12},{1,3},{3,1},... | collective-permute-start | bytes 2801672 | tf_op jit(solution)/shard_map/ppermute | solution.py:203
  33.7 26.1 %collective-permute-start.3 = (bf16[64,7296]{1,0:T(8,128)(2,1)}, bf16[64,7296]{1,0:T(8,128)(2,1)}, u32[]{:S(2)}, u32[]{:S(2)}) collective-permute-start(bf16[64,7296]{1,0:T(8,128)(2,1)} %collective-permute-done.1), channel_id=1, source_target_pairs={{4,0},{6,2},{8,12},{10,14},{5,1},{7,3},{9,13},{11,15},{20,16},{22,... | collective-permute-start | bytes 2801672 | tf_op jit(solution)/shard_map/ppermute | solution.py:203
  54.5 8.5 %copy-start.2 = (bf16[64,7296]{1,0:T(8,128)(2,1)}, bf16[64,7296]{1,0:T(8,128)(2,1)S(1)}, u32[]{:S(2)}) copy-start(bf16[64,7296]{1,0:T(8,128)(2,1)S(1)} %collective-permute-done.5.refs_0_) | copy-start | bytes 2801668
  61.1 21.0 %collective-permute-start.10 = (bf16[64,7296]{1,0:T(8,128)(2,1)S(1)}, bf16[64,7296]{1,0:T(8,128)(2,1)S(1)}, u32[]{:S(2)}, u32[]{:S(2)}) collective-permute-start(bf16[64,7296]{1,0:T(8,128)(2,1)S(1)} %broadcast_select_fusion.1.refs_1_), channel_id=1, source_target_pairs={{0,2},{2,0},{4,6},{6,4},{8,10},{10,8},{12,14},{14,12},{1,3},{3,1},... | collective-permute-start | bytes 2801672 | tf_op jit(solution)/shard_map/ppermute | solution.py:203
  61.7 22.6 %collective-permute-start.9 = (bf16[64,7296]{1,0:T(8,128)(2,1)S(1)}, bf16[64,7296]{1,0:T(8,128)(2,1)S(1)}, u32[]{:S(2)}, u32[]{:S(2)}) collective-permute-start(bf16[64,7296]{1,0:T(8,128)(2,1)S(1)} %collective-permute-done.4), channel_id=1, source_target_pairs={{4,0},{6,2},{8,12},{10,14},{5,1},{7,3},{9,13},{11,15},{20,16},{22,... | collective-permute-start | bytes 2801672 | tf_op jit(solution)/shard_map/ppermute | solution.py:203
  63.0 18.2 %collective-permute-start.11 = (bf16[32,7296]{1,0:T(8,128)(2,1)S(1)}, bf16[32,7296]{1,0:T(8,128)(2,1)S(1)}, u32[]{:S(2)}, u32[]{:S(2)}) collective-permute-start(bf16[32,7296]{1,0:T(8,128)(2,1)S(1)} %slice.21), channel_id=1, source_target_pairs={{4,8},{8,4},{6,10},{10,6},{5,9},{9,5},{7,11},{11,7},{20,24},{24,20... | collective-permute-start | bytes 1400840 | tf_op jit(solution)/shard_map/ppermute | solution.py:203
  82.2 17.5 %copy-start.4 = (bf16[64,7296]{1,0:T(8,128)(2,1)}, bf16[64,7296]{1,0:T(8,128)(2,1)S(1)}, u32[]{:S(2)}) copy-start(bf16[64,7296]{1,0:T(8,128)(2,1)S(1)} %collective-permute-done.10.refs_0_) | copy-start | bytes 2801668
  84.3 9.8 %collective-permute-start.12 = (bf16[32,7296]{1,0:T(8,128)(2,1)S(1)}, bf16[32,7296]{1,0:T(8,128)(2,1)S(1)}, u32[]{:S(2)}, u32[]{:S(2)}) collective-permute-start(bf16[32,7296]{1,0:T(8,128)(2,1)S(1)} %slice_select_fusion), channel_id=1, source_target_pairs={{0,2},{2,0},{4,6},{6,4},{8,10},{10,8},{12,14},{14,12},{1,3},{3,1},... | collective-permute-start | bytes 1400840 | tf_op jit(solution)/shard_map/ppermute | solution.py:203
  85.9 11.9 %collective-permute-start.13 = (bf16[32,7296]{1,0:T(8,128)(2,1)S(1)}, bf16[32,7296]{1,0:T(8,128)(2,1)S(1)}, u32[]{:S(2)}, u32[]{:S(2)}) collective-permute-start(bf16[32,7296]{1,0:T(8,128)(2,1)S(1)} %collective-permute-done.11), channel_id=1, source_target_pairs={{4,0},{6,2},{8,12},{10,14},{5,1},{7,3},{9,13},{11,15},{20,16},{22,... | collective-permute-start | bytes 1400840 | tf_op jit(solution)/shard_map/ppermute | solution.py:203
  94.2 5.5 %copy-start.8 = (bf16[32,7296]{1,0:T(8,128)(2,1)}, bf16[32,7296]{1,0:T(8,128)(2,1)S(1)}, u32[]{:S(2)}) copy-start(bf16[32,7296]{1,0:T(8,128)(2,1)S(1)} %collective-permute-done.12.refs_2_) | copy-start | bytes 1400836
  118.4 16.6 %copy-start.9 = (bf16[32,7168]{1,0:T(8,128)(2,1)S(1)}, bf16[32,7168]{1,0:T(8,128)(2,1)}, u32[]{:S(2)}) copy-start(bf16[32,7168]{1,0:T(8,128)(2,1)} %get-tuple-element.84) | copy-start | bytes 1376260
  118.4 13.7 %collective-permute-start.14 = (bf16[32,7168]{1,0:T(8,128)(2,1)}, bf16[32,7168]{1,0:T(8,128)(2,1)S(1)}, u32[]{:S(2)}, u32[]{:S(2)}) collective-permute-start(bf16[32,7168]{1,0:T(8,128)(2,1)} %get-tuple-element.83), channel_id=1, source_target_pairs={{0,2},{2,0},{4,6},{6,4},{8,10},{10,8},{12,14},{14,12},{1,3},{3,1},... | collective-permute-start | bytes 1376264 | tf_op jit(solution)/shard_map/ppermute | solution.py:203
  119.0 13.2 %collective-permute-start.15 = (bf16[32,7168]{1,0:T(8,128)(2,1)}, bf16[32,7168]{1,0:T(8,128)(2,1)S(1)}, u32[]{:S(2)}, u32[]{:S(2)}) collective-permute-start(bf16[32,7168]{1,0:T(8,128)(2,1)} %get-tuple-element.84), channel_id=1, source_target_pairs={{0,4},{2,6},{12,8},{14,10},{1,5},{3,7},{13,9},{15,11},{16,20},{18,... | collective-permute-start | bytes 1376264 | tf_op jit(solution)/shard_map/ppermute | solution.py:203
  122.3 25.0 %collective-permute-start.17 = (bf16[64,7168]{1,0:T(8,128)(2,1)}, bf16[64,7168]{1,0:T(8,128)(2,1)S(1)}, u32[]{:S(2)}, u32[]{:S(2)}) collective-permute-start(bf16[64,7168]{1,0:T(8,128)(2,1)} %get-tuple-element.86), channel_id=1, source_target_pairs={{0,2},{2,0},{4,6},{6,4},{8,10},{10,8},{12,14},{14,12},{1,3},{3,1},... | collective-permute-start | bytes 2752520 | tf_op jit(solution)/shard_map/ppermute | solution.py:203
  133.4 15.1 %collective-permute-start.16 = (bf16[64,7168]{1,0:T(8,128)(2,1)S(1)}, bf16[64,7168]{1,0:T(8,128)(2,1)S(1)}, u32[]{:S(2)}, u32[]{:S(2)}) collective-permute-start(bf16[64,7168]{1,0:T(8,128)(2,1)S(1)} %pad_maximum_fusion.1), channel_id=1, source_target_pairs={{0,4},{2,6},{12,8},{14,10},{1,5},{3,7},{13,9},{15,11},{16,20},{18,... | collective-permute-start | bytes 2752520 | tf_op jit(solution)/shard_map/ppermute | solution.py:203
  135.1 13.5 %copy-start.6 = (bf16[64,7168]{1,0:T(8,128)(2,1)S(1)}, bf16[64,7168]{1,0:T(8,128)(2,1)}, u32[]{:S(2)}) copy-start(bf16[64,7168]{1,0:T(8,128)(2,1)} %get-tuple-element.89) | copy-start | bytes 2752516
  135.1 0.9 collective-permute-start.18
  149.1 26.5 %collective-permute-start.19 = (bf16[64,7168]{1,0:T(8,128)(2,1)S(1)}, bf16[64,7168]{1,0:T(8,128)(2,1)S(1)}, u32[]{:S(2)}, u32[]{:S(2)}) collective-permute-start(bf16[64,7168]{1,0:T(8,128)(2,1)S(1)} %get-tuple-element.96), channel_id=1, source_target_pairs={{4,8},{8,4},{6,10},{10,6},{5,9},{9,5},{7,11},{11,7},{20,24},{24,20... | collective-permute-start | bytes 2752520 | tf_op jit(solution)/shard_map/ppermute | solution.py:203
  149.9 25.8 %collective-permute-start.20 = (bf16[64,7168]{1,0:T(8,128)(2,1)S(1)}, bf16[64,7168]{1,0:T(8,128)(2,1)S(1)}, u32[]{:S(2)}, u32[]{:S(2)}) collective-permute-start(bf16[64,7168]{1,0:T(8,128)(2,1)S(1)} %get-tuple-element.97), channel_id=1, source_target_pairs={{0,4},{2,6},{12,8},{14,10},{1,5},{3,7},{13,9},{15,11},{16,20},{18,... | collective-permute-start | bytes 2752520 | tf_op jit(solution)/shard_map/ppermute | solution.py:203
  156.1 19.6 %collective-permute-start.21 = (bf16[64,7168]{1,0:T(8,128)(2,1)S(1)}, bf16[64,7168]{1,0:T(8,128)(2,1)S(1)}, u32[]{:S(2)}, u32[]{:S(2)}) collective-permute-start(bf16[64,7168]{1,0:T(8,128)(2,1)S(1)} %pad_maximum_fusion.2), channel_id=1, source_target_pairs={{0,2},{2,0},{4,6},{6,4},{8,10},{10,8},{12,14},{14,12},{1,3},{3,1},... | collective-permute-start | bytes 2752520 | tf_op jit(solution)/shard_map/ppermute | solution.py:203
  177.2 15.0 %copy-start.7 = (bf16[64,7168]{1,0:T(8,128)(2,1)S(1)}, bf16[64,7168]{1,0:T(8,128)(2,1)}, u32[]{:S(2)}) copy-start(bf16[64,7168]{1,0:T(8,128)(2,1)} %get-tuple-element.105) | copy-start | bytes 2752516
  177.2 13.8 %collective-permute-start.23 = (bf16[64,7168]{1,0:T(8,128)(2,1)S(1)}, bf16[64,7168]{1,0:T(8,128)(2,1)S(1)}, u32[]{:S(2)}, u32[]{:S(2)}) collective-permute-start(bf16[64,7168]{1,0:T(8,128)(2,1)S(1)} %add_convert_fusion.2), channel_id=1, source_target_pairs={{0,4},{2,6},{4,0},{6,2},{8,12},{10,14},{12,8},{14,10},{1,5},{3,7},... | collective-permute-start | bytes 2752520 | tf_op jit(solution)/shard_map/ppermute | solution.py:203
  177.5 13.5 %collective-permute-start.24 = (bf16[64,7168]{1,0:T(8,128)(2,1)S(1)}, bf16[64,7168]{1,0:T(8,128)(2,1)S(1)}, u32[]{:S(2)}, u32[]{:S(2)}) collective-permute-start(bf16[64,7168]{1,0:T(8,128)(2,1)S(1)} %add_convert_fusion.1), channel_id=1, source_target_pairs={{4,8},{8,4},{6,10},{10,6},{5,9},{9,5},{7,11},{11,7},{20,24},{24,20... | collective-permute-start | bytes 2752520 | tf_op jit(solution)/shard_map/ppermute | solution.py:203
  178.4 13.8 %collective-permute-start.22 = (bf16[64,7168]{1,0:T(8,128)(2,1)S(1)}, bf16[64,7168]{1,0:T(8,128)(2,1)S(1)}, u32[]{:S(2)}, u32[]{:S(2)}) collective-permute-start(bf16[64,7168]{1,0:T(8,128)(2,1)S(1)} %copy-done.10), channel_id=1, source_target_pairs={{0,2},{2,0},{4,6},{6,4},{8,10},{10,8},{12,14},{14,12},{1,3},{3,1},... | collective-permute-start | bytes 2752520 | tf_op jit(solution)/shard_map/ppermute | solution.py:203
  (4 other events, 7.5 us)

commit v4 on v3

--- a/solution.py
+++ b/solution.py
@@ -9,7 +9,7 @@
 
 LANES = 128
 RING = 3
-KERNEL_VMEM = 54 * 1024 * 1024
+KERNEL_VMEM = 50 * 1024 * 1024
 
 
 def divisor_tile(extent, most, unit):
@@ -239,9 +239,8 @@
     v_gate, v_up = swap(w_gate), swap(w_up)
     s1, m2, t0, w_down = joined(cross(s0, 2), send(s0, middle), cross(s0, 1), w_down)
     v_gate, w_down = joined(v_gate, w_down)
-    e2, m3, t1, v_up, v_down = joined(
-        send(m2, outward), send(s1, middle), cross(s1, 1), v_up, swap(w_down)
-    )
+    m3 = send(s1, middle)
+    e2, t1, v_up, v_down = joined(send(m2, outward), cross(s1, 1), v_up, swap(w_down))
     experts = functools.partial(experts, (v_gate, v_up, v_down))
     s2 = jnp.where(inner, m2, e2)
     e3, t2, n3, q1, p2 = joined(

time: 196 us -> 187 us (0.954)
  Pallas kernels: 54.9 us -> 50.7 us
  other arithmetic: 11 us -> 8.06 us
    pallas_call x3, Pallas kernels: 54.9 us -> 50.7 us  [expert_rows(): pl.pallas_call(functools.partial(expert_kernel, count, slab, out_tile), i...]
    convert_element_type x7, other arithmetic: 4.9 us -> 2.68 us  [plus(): return total.astype(jnp.bfloat16)]
    ppermute x22, starting transfers between devices: 30.9 us -> 28.9 us  [send(): return lax.ppermute(array, 'node', pairs)]
  transfers between devices with their start and end apart: 25 -> 25, of which waited for: 13 -> 13; matrix products, arithmetic and copies ran while one was open for 3% -> 2% of each run, Pallas kernels for 19% -> 18%
where the time goes in v4:
time: 187 us; the launch traced here: 186 us
  waiting for transfers between devices  94.9 us (51%)
  Pallas kernels  50.7 us (27%)
  starting transfers between devices  29.4 us (16%)
  other arithmetic  8.06 us (4%)
  local copies, waits for them, and re-layouts  2.98 us (2%)
    ppermute x22, waiting for transfers between devices, send(): return lax.ppermute(array, 'node', pairs)  94.9 us
    pallas_call x3, Pallas kernels, expert_rows(): pl.pallas_call(functools.partial(expert_kernel, count, slab, out_tile), i...  50.7 us
    ppermute x22, starting transfers between devices, send(): return lax.ppermute(array, 'node', pairs)  28.9 us
  transfers between devices with their start and end apart: 25, of which 13 were waited for; matrix products, arithmetic and copies ran while one was open for 2% of the time, Pallas kernels for 18%

profile of v4, /device:TPU:0, one launch (start us, length us, event | category | flops | bytes accessed | tf_op | source)
XLA Modules:
  0.0 186.3 jit_solution(7892898227549385686)
XLA Ops:
  2.0 1.2 pad_maximum_fusion.refs_0_
  3.2 2.6 %collective-permute-start = (bf16[64,7296]{1,0:T(8,128)(2,1)S(1)}, bf16[64,7296]{1,0:T(8,128)(2,1)}, u32[]{:S(2)}, u32[]{:S(2)}) collective-permute-start(bf16[64,7296]{1,0:T(8,128)(2,1)S(1)} %pad_maximum_fusion.refs_0_), channel_id=1, source_target_pairs={{0,4},{2,6},{4,0},{6,2},{8,12},{10,14},{12,8},{14,10},{1,5},{3,7},... | collective-permute-start | bytes 2801672 | tf_op jit(solution)/shard_map/ppermute | solution.py:203
  5.8 1.6 collective-permute-start.1
  7.5 1.5 collective-permute-start.2
  9.0 18.3 %collective-permute-done.refs_2_ = bf16[64,7296]{1,0:T(8,128)(2,1)} collective-permute-done((bf16[64,7296]{1,0:T(8,128)(2,1)S(1)}, bf16[64,7296]{1,0:T(8,128)(2,1)}, u32[]{:S(2)}, u32[]{:S(2)}) %collective-permute-start) | collective-permute-done | bytes 933920 | tf_op jit(solution)/shard_map/ppermute | solution.py:203
  27.3 3.0 %collective-permute-done.2.refs_1_ = bf16[64,7296]{1,0:T(8,128)(2,1)S(1)} collective-permute-done((bf16[64,7296]{1,0:T(8,128)(2,1)S(1)}, bf16[64,7296]{1,0:T(8,128)(2,1)S(1)}, u32[]{:S(2)}, u32[]{:S(2)}) %collective-permute-start.2) | collective-permute-done | bytes 933920 | tf_op jit(solution)/shard_map/ppermute | solution.py:203
  30.4 2.9 %copy-done = bf16[1,7168,512]{2,1,0:T(8,128)(2,1)} copy-done((bf16[1,7168,512]{2,1,0:T(8,128)(2,1)}, bf16[1,7168,512]{2,1,0:T(8,128)(2,1)S(1)}, u32[]{:S(2)}) %copy-start) | copy-done | bytes 7340056
  34.0 1.6 collective-permute-start.6
  35.6 1.3 collective-permute-start.5
  36.9 1.3 collective-permute-start.4
  38.2 18.1 %collective-permute-done.6.refs_0_ = bf16[64,7296]{1,0:T(8,128)(2,1)S(1)} collective-permute-done((bf16[64,7296]{1,0:T(8,128)(2,1)}, bf16[64,7296]{1,0:T(8,128)(2,1)S(1)}, u32[]{:S(2)}, u32[]{:S(2)}) %collective-permute-start.6) | collective-permute-done | bytes 933920 | tf_op jit(solution)/shard_map/ppermute | solution.py:203
  56.3 6.3 %collective-permute-done.5 = bf16[64,7296]{1,0:T(8,128)(2,1)} collective-permute-done((bf16[64,7296]{1,0:T(8,128)(2,1)}, bf16[64,7296]{1,0:T(8,128)(2,1)}, u32[]{:S(2)}, u32[]{:S(2)}) %collective-permute-start.5) | collective-permute-done | bytes 933920 | tf_op jit(solution)/shard_map/ppermute | solution.py:203
  62.6 1.3 broadcast_select_fusion.1.refs_1_
  64.7 15.9 %shard_map.64 = (bf16[64,7168]{1,0:T(8,128)(2,1)S(1)}, bf16[64,7168]{1,0:T(8,128)(2,1)S(1)}) custom-call(bf16[64,7296]{1,0:T(8,128)(2,1)S(1)} %collective-permute-done.6.refs_0_, bf16[64,7296]{1,0:T(8,128)(2,1)S(1)} %broadcast_select_fusion.1.refs_1_, s32[1]{0:T(128)} %bitcast.refs_2_.refs_4_.refs_3_, bf16[1,7168,512]{2,1,0:T(8,128)(2,1)} %refs_4_.3, ...), custom_call_target="tpu_custom_call" | custom-call | flops 5637144576 | bytes 47710208 | tf_op jit(solution)/shard_map/pallas_call | solution.py:156
  81.6 3.1 %collective-permute-done.10.refs_0_ = bf16[64,7296]{1,0:T(8,128)(2,1)S(1)} collective-permute-done((bf16[64,7296]{1,0:T(8,128)(2,1)S(1)}, bf16[64,7296]{1,0:T(8,128)(2,1)S(1)}, u32[]{:S(2)}, u32[]{:S(2)}) %collective-permute-start.10) | collective-permute-done | bytes 933920 | tf_op jit(solution)/shard_map/ppermute | solution.py:203
  84.9 1.3 collective-permute-start.13
  86.2 7.8 %collective-permute-done.12.refs_2_ = bf16[32,7296]{1,0:T(8,128)(2,1)S(1)} collective-permute-done((bf16[32,7296]{1,0:T(8,128)(2,1)S(1)}, bf16[32,7296]{1,0:T(8,128)(2,1)S(1)}, u32[]{:S(2)}, u32[]{:S(2)}) %collective-permute-start.12) | collective-permute-done | bytes 466976 | tf_op jit(solution)/shard_map/ppermute | solution.py:203
  94.0 1.8 collective-permute-done.13
  95.8 1.1 broadcast_select_fusion.refs_1_
  96.9 16.9 %shard_map.65 = (bf16[64,7168]{1,0:T(8,128)(2,1)S(1)}, bf16[64,7168]{1,0:T(8,128)(2,1)S(1)}, bf16[32,7168]{1,0:T(8,128)(2,1)S(1)}, bf16[32,7168]{1,0:T(8,128)(2,1)S(1)}) custom-call(bf16[64,7296]{1,0:T(8,128)(2,1)} %copy-done.2, bf16[64,7296]{1,0:T(8,128)(2,1)} %broadcast_select_fusion.refs_1_, bf16[32,7296]{1,0:T(8,128)(2,1)S(1)} %collective-permute-done.12.refs_2_, ...), custom_call_target="tpu_custom_call" | custom-call | flops 8455716864 | bytes 49545216 | tf_op jit(solution)/shard_map/pallas_call | solution.py:156
  113.8 1.7 collective-permute-start.14
  115.5 1.5 collective-permute-start.15
  117.5 9.9 %collective-permute-done.14 = bf16[32,7168]{1,0:T(8,128)(2,1)S(1)} collective-permute-done((bf16[32,7168]{1,0:T(8,128)(2,1)S(1)}, bf16[32,7168]{1,0:T(8,128)(2,1)S(1)}, u32[]{:S(2)}, u32[]{:S(2)}) %collective-permute-start.14) | collective-permute-done | bytes 458784 | tf_op jit(solution)/shard_map/ppermute | solution.py:203
  127.5 1.6 collective-permute-start.16
  130.0 11.4 %collective-permute-done.17 = bf16[64,7168]{1,0:T(8,128)(2,1)S(1)} collective-permute-done((bf16[64,7168]{1,0:T(8,128)(2,1)S(1)}, bf16[64,7168]{1,0:T(8,128)(2,1)S(1)}, u32[]{:S(2)}, u32[]{:S(2)}) %collective-permute-start.17) | collective-permute-done | bytes 917536 | tf_op jit(solution)/shard_map/ppermute | solution.py:203
  141.4 1.2 collective-permute-done.16
  143.9 6.6 %collective-permute-start.20 = (bf16[64,7168]{1,0:T(8,128)(2,1)S(1)}, bf16[64,7168]{1,0:T(8,128)(2,1)S(1)}, u32[]{:S(2)}, u32[]{:S(2)}) collective-permute-start(bf16[64,7168]{1,0:T(8,128)(2,1)S(1)} %get-tuple-element.95), channel_id=1, source_target_pairs={{0,4},{2,6},{12,8},{14,10},{1,5},{3,7},{13,9},{15,11},{16,20},{18,... | collective-permute-start | bytes 2752520 | tf_op jit(solution)/shard_map/ppermute | solution.py:203
  151.1 17.8 %shard_map.66 = (bf16[64,7168]{1,0:T(8,128)(2,1)S(1)}, bf16[64,7168]{1,0:T(8,128)(2,1)S(1)}, bf16[64,7168]{1,0:T(8,128)(2,1)S(1)}) custom-call(bf16[64,7296]{1,0:T(8,128)(2,1)S(1)} %pad_maximum_fusion.refs_0_, bf16[64,7296]{1,0:T(8,128)(2,1)} %copy-done.1, bf16[64,7296]{1,0:T(8,128)(2,1)} %collective-permute-done.refs_2_, s32[1]{0:T(128)} %bitcast.refs_2_.refs_4_.refs_3_, ...), custom_call_target="tpu_custom_call" | custom-call | flops 8455716864 | bytes 49545216 | tf_op jit(solution)/shard_map/pallas_call | solution.py:156
  170.4 1.5 collective-permute-start.22
  171.9 11.7 %collective-permute-done.23 = bf16[64,7168]{1,0:T(8,128)(2,1)S(1)} collective-permute-done((bf16[64,7168]{1,0:T(8,128)(2,1)S(1)}, bf16[64,7168]{1,0:T(8,128)(2,1)S(1)}, u32[]{:S(2)}, u32[]{:S(2)}) %collective-permute-start.23) | collective-permute-done | bytes 917536 | tf_op jit(solution)/shard_map/ppermute | solution.py:203
  183.6 1.4 collective-permute-done.22
  185.0 1.4 add_convert_fusion
  (46 shorter events, 9.4 us)
Async XLA Ops:
  0.0 30.3 %collective-permute-start.8 = (bf16[1,7168,512]{2,1,0:T(8,128)(2,1)}, bf16[1,7168,512]{2,1,0:T(8,128)(2,1)S(1)}, u32[]{:S(2)}, u32[]{:S(2)}) collective-permute-start(bf16[1,7168,512]{2,1,0:T(8,128)(2,1)} %refs_4_.3), channel_id=1, source_target_pairs={{0,1},{1,0},{2,3},{3,2},{4,5},{5,4},{6,7},{7,6},{8,9},{9,8},{10,11... | collective-permute-start | bytes 22020104 | tf_op jit(solution)/shard_map/ppermute | solution.py:209
  3.2 24.1 %collective-permute-start = (bf16[64,7296]{1,0:T(8,128)(2,1)S(1)}, bf16[64,7296]{1,0:T(8,128)(2,1)}, u32[]{:S(2)}, u32[]{:S(2)}) collective-permute-start(bf16[64,7296]{1,0:T(8,128)(2,1)S(1)} %pad_maximum_fusion.refs_0_), channel_id=1, source_target_pairs={{0,4},{2,6},{4,0},{6,2},{8,12},{10,14},{12,8},{14,10},{1,5},{3,7},... | collective-permute-start | bytes 2801672 | tf_op jit(solution)/shard_map/ppermute | solution.py:203
  5.8 21.5 %collective-permute-start.1 = (bf16[64,7296]{1,0:T(8,128)(2,1)S(1)}, bf16[64,7296]{1,0:T(8,128)(2,1)}, u32[]{:S(2)}, u32[]{:S(2)}) collective-permute-start(bf16[64,7296]{1,0:T(8,128)(2,1)S(1)} %pad_maximum_fusion.refs_0_), channel_id=1, source_target_pairs={{4,8},{8,4},{6,10},{10,6},{5,9},{9,5},{7,11},{11,7},{20,24},{24,20... | collective-permute-start | bytes 2801672 | tf_op jit(solution)/shard_map/ppermute | solution.py:203
  7.5 22.8 %collective-permute-start.2 = (bf16[64,7296]{1,0:T(8,128)(2,1)S(1)}, bf16[64,7296]{1,0:T(8,128)(2,1)S(1)}, u32[]{:S(2)}, u32[]{:S(2)}) collective-permute-start(bf16[64,7296]{1,0:T(8,128)(2,1)S(1)} %pad_maximum_fusion.refs_0_), channel_id=1, source_target_pairs={{0,2},{2,0},{4,6},{6,4},{8,10},{10,8},{12,14},{14,12},{1,3},{3,1},... | collective-permute-start | bytes 2801672 | tf_op jit(solution)/shard_map/ppermute | solution.py:203
  9.0 53.6 %collective-permute-start.7 = (bf16[1,7168,512]{2,1,0:T(8,128)(2,1)}, bf16[1,7168,512]{2,1,0:T(8,128)(2,1)}, u32[]{:S(2)}, u32[]{:S(2)}) collective-permute-start(bf16[1,7168,512]{2,1,0:T(8,128)(2,1)} %refs_5_.3), channel_id=1, source_target_pairs={{0,1},{1,0},{2,3},{3,2},{4,5},{5,4},{6,7},{7,6},{8,9},{9,8},{10,11... | collective-permute-start | bytes 22020104 | tf_op jit(solution)/shard_map/ppermute | solution.py:209
  30.3 3.7 %copy-start.1 = (bf16[64,7296]{1,0:T(8,128)(2,1)}, bf16[64,7296]{1,0:T(8,128)(2,1)S(1)}, u32[]{:S(2)}) copy-start(bf16[64,7296]{1,0:T(8,128)(2,1)S(1)} %collective-permute-done.2.refs_1_) | copy-start | bytes 2801668
  30.3 3.0 %copy-start = (bf16[1,7168,512]{2,1,0:T(8,128)(2,1)}, bf16[1,7168,512]{2,1,0:T(8,128)(2,1)S(1)}, u32[]{:S(2)}) copy-start(bf16[1,7168,512]{2,1,0:T(8,128)(2,1)S(1)} %collective-permute-done.8.refs_5_.refs_7_.refs_6_) | copy-start | bytes 22020100
  30.3 32.3 %collective-permute-start.9 = (bf16[1,512,7168]{2,1,0:T(8,128)(2,1)}, bf16[1,512,7168]{2,1,0:T(8,128)(2,1)}, u32[]{:S(2)}, u32[]{:S(2)}) collective-permute-start(bf16[1,512,7168]{2,1,0:T(8,128)(2,1)} %refs_8_.1), channel_id=1, source_target_pairs={{0,1},{1,0},{2,3},{3,2},{4,5},{5,4},{6,7},{7,6},{8,9},{9,8},{10,11... | collective-permute-start | bytes 22020104 | tf_op jit(solution)/shard_map/ppermute | solution.py:209
  33.3 3.6 %collective-permute-start.3 = (bf16[64,7296]{1,0:T(8,128)(2,1)}, bf16[64,7296]{1,0:T(8,128)(2,1)S(1)}, u32[]{:S(2)}, u32[]{:S(2)}) collective-permute-start(bf16[64,7296]{1,0:T(8,128)(2,1)} %collective-permute-done.refs_2_), channel_id=1, source_target_pairs={{4,8},{8,4},{6,10},{10,6},{5,9},{9,5},{7,11},{11,7},{20,24},{24,20... | collective-permute-start | bytes 2801672 | tf_op jit(solution)/shard_map/ppermute | solution.py:203
  34.0 22.3 %collective-permute-start.6 = (bf16[64,7296]{1,0:T(8,128)(2,1)}, bf16[64,7296]{1,0:T(8,128)(2,1)S(1)}, u32[]{:S(2)}, u32[]{:S(2)}) collective-permute-start(bf16[64,7296]{1,0:T(8,128)(2,1)} %collective-permute-done.refs_2_), channel_id=1, source_target_pairs={{0,2},{2,0},{4,6},{6,4},{8,10},{10,8},{12,14},{14,12},{1,3},{3,1},... | collective-permute-start | bytes 2801672 | tf_op jit(solution)/shard_map/ppermute | solution.py:203
  35.6 27.0 %collective-permute-start.5 = (bf16[64,7296]{1,0:T(8,128)(2,1)}, bf16[64,7296]{1,0:T(8,128)(2,1)}, u32[]{:S(2)}, u32[]{:S(2)}) collective-permute-start(bf16[64,7296]{1,0:T(8,128)(2,1)} %collective-permute-done.1), channel_id=1, source_target_pairs={{4,0},{6,2},{8,12},{10,14},{5,1},{7,3},{9,13},{11,15},{20,16},{22,... | collective-permute-start | bytes 2801672 | tf_op jit(solution)/shard_map/ppermute | solution.py:203
  36.9 44.7 %collective-permute-start.4 = (bf16[64,7296]{1,0:T(8,128)(2,1)S(1)}, bf16[64,7296]{1,0:T(8,128)(2,1)S(1)}, u32[]{:S(2)}, u32[]{:S(2)}) collective-permute-start(bf16[64,7296]{1,0:T(8,128)(2,1)S(1)} %collective-permute-done.3), channel_id=1, source_target_pairs={{4,0},{6,2},{8,12},{10,14},{5,1},{7,3},{9,13},{11,15},{20,16},{22,... | collective-permute-start | bytes 2801672 | tf_op jit(solution)/shard_map/ppermute | solution.py:203
  63.9 20.8 %collective-permute-start.10 = (bf16[64,7296]{1,0:T(8,128)(2,1)S(1)}, bf16[64,7296]{1,0:T(8,128)(2,1)S(1)}, u32[]{:S(2)}, u32[]{:S(2)}) collective-permute-start(bf16[64,7296]{1,0:T(8,128)(2,1)S(1)} %broadcast_select_fusion.1.refs_1_), channel_id=1, source_target_pairs={{0,2},{2,0},{4,6},{6,4},{8,10},{10,8},{12,14},{14,12},{1,3},{3,1},... | collective-permute-start | bytes 2801672 | tf_op jit(solution)/shard_map/ppermute | solution.py:203
  64.0 17.5 %collective-permute-start.11 = (bf16[32,7296]{1,0:T(8,128)(2,1)S(1)}, bf16[32,7296]{1,0:T(8,128)(2,1)S(1)}, u32[]{:S(2)}, u32[]{:S(2)}) collective-permute-start(bf16[32,7296]{1,0:T(8,128)(2,1)S(1)} %slice.21), channel_id=1, source_target_pairs={{4,8},{8,4},{6,10},{10,6},{5,9},{9,5},{7,11},{11,7},{20,24},{24,20... | collective-permute-start | bytes 1400840 | tf_op jit(solution)/shard_map/ppermute | solution.py:203
  84.7 12.2 %copy-start.2 = (bf16[64,7296]{1,0:T(8,128)(2,1)}, bf16[64,7296]{1,0:T(8,128)(2,1)S(1)}, u32[]{:S(2)}) copy-start(bf16[64,7296]{1,0:T(8,128)(2,1)S(1)} %collective-permute-done.10.refs_0_) | copy-start | bytes 2801668
  84.8 9.2 %collective-permute-start.12 = (bf16[32,7296]{1,0:T(8,128)(2,1)S(1)}, bf16[32,7296]{1,0:T(8,128)(2,1)S(1)}, u32[]{:S(2)}, u32[]{:S(2)}) collective-permute-start(bf16[32,7296]{1,0:T(8,128)(2,1)S(1)} %slice_select_fusion), channel_id=1, source_target_pairs={{0,2},{2,0},{4,6},{6,4},{8,10},{10,8},{12,14},{14,12},{1,3},{3,1},... | collective-permute-start | bytes 1400840 | tf_op jit(solution)/shard_map/ppermute | solution.py:203
  84.9 10.8 %collective-permute-start.13 = (bf16[32,7296]{1,0:T(8,128)(2,1)S(1)}, bf16[32,7296]{1,0:T(8,128)(2,1)S(1)}, u32[]{:S(2)}, u32[]{:S(2)}) collective-permute-start(bf16[32,7296]{1,0:T(8,128)(2,1)S(1)} %collective-permute-done.11), channel_id=1, source_target_pairs={{4,0},{6,2},{8,12},{10,14},{5,1},{7,3},{9,13},{11,15},{20,16},{22,... | collective-permute-start | bytes 1400840 | tf_op jit(solution)/shard_map/ppermute | solution.py:203
  113.8 13.5 %collective-permute-start.14 = (bf16[32,7168]{1,0:T(8,128)(2,1)S(1)}, bf16[32,7168]{1,0:T(8,128)(2,1)S(1)}, u32[]{:S(2)}, u32[]{:S(2)}) collective-permute-start(bf16[32,7168]{1,0:T(8,128)(2,1)S(1)} %get-tuple-element.81), channel_id=1, source_target_pairs={{0,2},{2,0},{4,6},{6,4},{8,10},{10,8},{12,14},{14,12},{1,3},{3,1},... | collective-permute-start | bytes 1376264 | tf_op jit(solution)/shard_map/ppermute | solution.py:203
  115.5 11.8 %collective-permute-start.15 = (bf16[32,7168]{1,0:T(8,128)(2,1)S(1)}, bf16[32,7168]{1,0:T(8,128)(2,1)S(1)}, u32[]{:S(2)}, u32[]{:S(2)}) collective-permute-start(bf16[32,7168]{1,0:T(8,128)(2,1)S(1)} %get-tuple-element.82), channel_id=1, source_target_pairs={{0,4},{2,6},{12,8},{14,10},{1,5},{3,7},{13,9},{15,11},{16,20},{18,... | collective-permute-start | bytes 1376264 | tf_op jit(solution)/shard_map/ppermute | solution.py:203
  117.0 24.4 %collective-permute-start.17 = (bf16[64,7168]{1,0:T(8,128)(2,1)S(1)}, bf16[64,7168]{1,0:T(8,128)(2,1)S(1)}, u32[]{:S(2)}, u32[]{:S(2)}) collective-permute-start(bf16[64,7168]{1,0:T(8,128)(2,1)S(1)} %get-tuple-element.84), channel_id=1, source_target_pairs={{0,2},{2,0},{4,6},{6,4},{8,10},{10,8},{12,14},{14,12},{1,3},{3,1},... | collective-permute-start | bytes 2752520 | tf_op jit(solution)/shard_map/ppermute | solution.py:203
  127.5 15.1 %collective-permute-start.16 = (bf16[64,7168]{1,0:T(8,128)(2,1)S(1)}, bf16[64,7168]{1,0:T(8,128)(2,1)S(1)}, u32[]{:S(2)}, u32[]{:S(2)}) collective-permute-start(bf16[64,7168]{1,0:T(8,128)(2,1)S(1)} %pad_maximum_fusion.1), channel_id=1, source_target_pairs={{0,4},{2,6},{12,8},{14,10},{1,5},{3,7},{13,9},{15,11},{16,20},{18,... | collective-permute-start | bytes 2752520 | tf_op jit(solution)/shard_map/ppermute | solution.py:203
  129.3 0.7 collective-permute-start.18
  143.2 25.8 %collective-permute-start.19 = (bf16[64,7168]{1,0:T(8,128)(2,1)S(1)}, bf16[64,7168]{1,0:T(8,128)(2,1)S(1)}, u32[]{:S(2)}, u32[]{:S(2)}) collective-permute-start(bf16[64,7168]{1,0:T(8,128)(2,1)S(1)} %get-tuple-element.94), channel_id=1, source_target_pairs={{4,8},{8,4},{6,10},{10,6},{5,9},{9,5},{7,11},{11,7},{20,24},{24,20... | collective-permute-start | bytes 2752520 | tf_op jit(solution)/shard_map/ppermute | solution.py:203
  143.9 25.0 %collective-permute-start.20 = (bf16[64,7168]{1,0:T(8,128)(2,1)S(1)}, bf16[64,7168]{1,0:T(8,128)(2,1)S(1)}, u32[]{:S(2)}, u32[]{:S(2)}) collective-permute-start(bf16[64,7168]{1,0:T(8,128)(2,1)S(1)} %get-tuple-element.95), channel_id=1, source_target_pairs={{0,4},{2,6},{12,8},{14,10},{1,5},{3,7},{13,9},{15,11},{16,20},{18,... | collective-permute-start | bytes 2752520 | tf_op jit(solution)/shard_map/ppermute | solution.py:203
  150.5 18.5 %collective-permute-start.21 = (bf16[64,7168]{1,0:T(8,128)(2,1)S(1)}, bf16[64,7168]{1,0:T(8,128)(2,1)S(1)}, u32[]{:S(2)}, u32[]{:S(2)}) collective-permute-start(bf16[64,7168]{1,0:T(8,128)(2,1)S(1)} %pad_maximum_fusion.2), channel_id=1, source_target_pairs={{0,2},{2,0},{4,6},{6,4},{8,10},{10,8},{12,14},{14,12},{1,3},{3,1},... | collective-permute-start | bytes 2752520 | tf_op jit(solution)/shard_map/ppermute | solution.py:203
  169.3 14.3 %collective-permute-start.23 = (bf16[64,7168]{1,0:T(8,128)(2,1)S(1)}, bf16[64,7168]{1,0:T(8,128)(2,1)S(1)}, u32[]{:S(2)}, u32[]{:S(2)}) collective-permute-start(bf16[64,7168]{1,0:T(8,128)(2,1)S(1)} %add_convert_fusion.2), channel_id=1, source_target_pairs={{0,4},{2,6},{4,0},{6,2},{8,12},{10,14},{12,8},{14,10},{1,5},{3,7},... | collective-permute-start | bytes 2752520 | tf_op jit(solution)/shard_map/ppermute | solution.py:203
  169.6 14.0 %collective-permute-start.24 = (bf16[64,7168]{1,0:T(8,128)(2,1)S(1)}, bf16[64,7168]{1,0:T(8,128)(2,1)S(1)}, u32[]{:S(2)}, u32[]{:S(2)}) collective-permute-start(bf16[64,7168]{1,0:T(8,128)(2,1)S(1)} %add_convert_fusion.1), channel_id=1, source_target_pairs={{4,8},{8,4},{6,10},{10,6},{5,9},{9,5},{7,11},{11,7},{20,24},{24,20... | collective-permute-start | bytes 2752520 | tf_op jit(solution)/shard_map/ppermute | solution.py:203
  170.4 14.6 %collective-permute-start.22 = (bf16[64,7168]{1,0:T(8,128)(2,1)S(1)}, bf16[64,7168]{1,0:T(8,128)(2,1)S(1)}, u32[]{:S(2)}, u32[]{:S(2)}) collective-permute-start(bf16[64,7168]{1,0:T(8,128)(2,1)S(1)} %get-tuple-element.104), channel_id=1, source_target_pairs={{0,2},{2,0},{4,6},{6,4},{8,10},{10,8},{12,14},{14,12},{1,3},{3,1},... | collective-permute-start | bytes 2752520 | tf_op jit(solution)/shard_map/ppermute | solution.py:203

commit v5 on v4

--- a/solution.py
+++ b/solution.py
@@ -246,10 +246,9 @@
     e3, t2, n3, q1, p2 = joined(
         send(m3, outward), cross(s2, 1), send(t1[cut:], middle), *experts(t1, s2)
     )
-    t3, o3, m3, e3 = joined(
-        cross(jnp.where(inner, m3[:cut], e3[:cut]), 1), send(n3, outward), m3, e3
-    )
-    s3 = jnp.where(inner, m3, e3)
+    t3, o3, s3 = joined(
+        cross(jnp.where(inner, m3[:cut], e3[:cut]), 1), send(n3, outward), jnp.where(inner, m3, e3)
+    )
     q2, p3, q3, r3, s0, t0, s1 = joined(
         *experts(t2, s3, t3, jnp.where(inner, n3, o3)), s0, t0, s1
     )

time: 187 us -> 186 us (level)
  transfers between devices with their start and end apart: 25 -> 25, of which waited for: 13 -> 13; matrix products, arithmetic and copies ran while one was open for 2% -> 3% of each run, Pallas kernels for 18% -> 18%
where the time goes in v5:
time: 186 us; the launch traced here: 185 us
  waiting for transfers between devices  93.7 us (50%)
  Pallas kernels  50.7 us (27%)
  starting transfers between devices  29.4 us (16%)
  other arithmetic  8.15 us (4%)
  local copies, waits for them, and re-layouts  2.98 us (2%)
    ppermute x22, waiting for transfers between devices, send(): return lax.ppermute(array, 'node', pairs)  93.7 us
    pallas_call x3, Pallas kernels, expert_rows(): pl.pallas_call(functools.partial(expert_kernel, count, slab, out_tile), i...  50.7 us
    ppermute x22, starting transfers between devices, send(): return lax.ppermute(array, 'node', pairs)  28.9 us
  transfers between devices with their start and end apart: 25, of which 13 were waited for; matrix products, arithmetic and copies ran while one was open for 3% of the time, Pallas kernels for 18%

profile of v5, /device:TPU:0, one launch (start us, length us, event | category | flops | bytes accessed | tf_op | source)
XLA Modules:
  0.0 185.2 jit_solution(11780930183854740932)
XLA Ops:
  2.0 1.2 pad_maximum_fusion.refs_0_
  3.2 2.6 %collective-permute-start = (bf16[64,7296]{1,0:T(8,128)(2,1)S(1)}, bf16[64,7296]{1,0:T(8,128)(2,1)}, u32[]{:S(2)}, u32[]{:S(2)}) collective-permute-start(bf16[64,7296]{1,0:T(8,128)(2,1)S(1)} %pad_maximum_fusion.refs_0_), channel_id=1, source_target_pairs={{0,4},{2,6},{4,0},{6,2},{8,12},{10,14},{12,8},{14,10},{1,5},{3,7},... | collective-permute-start | bytes 2801672 | tf_op jit(solution)/shard_map/ppermute | solution.py:203
  5.8 1.6 collective-permute-start.1
  7.5 1.5 collective-permute-start.2
  9.0 18.3 %collective-permute-done.refs_2_ = bf16[64,7296]{1,0:T(8,128)(2,1)} collective-permute-done((bf16[64,7296]{1,0:T(8,128)(2,1)S(1)}, bf16[64,7296]{1,0:T(8,128)(2,1)}, u32[]{:S(2)}, u32[]{:S(2)}) %collective-permute-start) | collective-permute-done | bytes 933920 | tf_op jit(solution)/shard_map/ppermute | solution.py:203
  27.3 3.0 %collective-permute-done.2.refs_1_ = bf16[64,7296]{1,0:T(8,128)(2,1)S(1)} collective-permute-done((bf16[64,7296]{1,0:T(8,128)(2,1)S(1)}, bf16[64,7296]{1,0:T(8,128)(2,1)S(1)}, u32[]{:S(2)}, u32[]{:S(2)}) %collective-permute-start.2) | collective-permute-done | bytes 933920 | tf_op jit(solution)/shard_map/ppermute | solution.py:203
  30.4 2.9 %copy-done = bf16[1,7168,512]{2,1,0:T(8,128)(2,1)} copy-done((bf16[1,7168,512]{2,1,0:T(8,128)(2,1)}, bf16[1,7168,512]{2,1,0:T(8,128)(2,1)S(1)}, u32[]{:S(2)}) %copy-start) | copy-done | bytes 7340056
  34.0 1.6 collective-permute-start.6
  35.6 1.3 collective-permute-start.5
  36.9 1.3 collective-permute-start.4
  38.2 18.1 %collective-permute-done.6.refs_0_ = bf16[64,7296]{1,0:T(8,128)(2,1)S(1)} collective-permute-done((bf16[64,7296]{1,0:T(8,128)(2,1)}, bf16[64,7296]{1,0:T(8,128)(2,1)S(1)}, u32[]{:S(2)}, u32[]{:S(2)}) %collective-permute-start.6) | collective-permute-done | bytes 933920 | tf_op jit(solution)/shard_map/ppermute | solution.py:203
  56.3 6.3 %collective-permute-done.5 = bf16[64,7296]{1,0:T(8,128)(2,1)} collective-permute-done((bf16[64,7296]{1,0:T(8,128)(2,1)}, bf16[64,7296]{1,0:T(8,128)(2,1)}, u32[]{:S(2)}, u32[]{:S(2)}) %collective-permute-start.5) | collective-permute-done | bytes 933920 | tf_op jit(solution)/shard_map/ppermute | solution.py:203
  62.6 1.3 broadcast_select_fusion.1.refs_1_
  64.7 15.9 %shard_map.64 = (bf16[64,7168]{1,0:T(8,128)(2,1)S(1)}, bf16[64,7168]{1,0:T(8,128)(2,1)S(1)}) custom-call(bf16[64,7296]{1,0:T(8,128)(2,1)S(1)} %collective-permute-done.6.refs_0_, bf16[64,7296]{1,0:T(8,128)(2,1)S(1)} %broadcast_select_fusion.1.refs_1_, s32[1]{0:T(128)} %bitcast.refs_2_.refs_4_.refs_3_, bf16[1,7168,512]{2,1,0:T(8,128)(2,1)} %refs_4_.3, ...), custom_call_target="tpu_custom_call" | custom-call | flops 5637144576 | bytes 47710208 | tf_op jit(solution)/shard_map/pallas_call | solution.py:156
  81.6 3.1 %collective-permute-done.10.refs_0_ = bf16[64,7296]{1,0:T(8,128)(2,1)S(1)} collective-permute-done((bf16[64,7296]{1,0:T(8,128)(2,1)S(1)}, bf16[64,7296]{1,0:T(8,128)(2,1)S(1)}, u32[]{:S(2)}, u32[]{:S(2)}) %collective-permute-start.10) | collective-permute-done | bytes 933920 | tf_op jit(solution)/shard_map/ppermute | solution.py:203
  84.9 1.3 collective-permute-start.13
  86.2 1.2 broadcast_select_fusion.refs_1_
  87.3 6.6 %collective-permute-done.12.refs_2_ = bf16[32,7296]{1,0:T(8,128)(2,1)S(1)} collective-permute-done((bf16[32,7296]{1,0:T(8,128)(2,1)S(1)}, bf16[32,7296]{1,0:T(8,128)(2,1)S(1)}, u32[]{:S(2)}, u32[]{:S(2)}) %collective-permute-start.12) | collective-permute-done | bytes 466976 | tf_op jit(solution)/shard_map/ppermute | solution.py:203
  94.0 1.8 collective-permute-done.13
  95.8 16.9 %shard_map.65 = (bf16[64,7168]{1,0:T(8,128)(2,1)S(1)}, bf16[64,7168]{1,0:T(8,128)(2,1)S(1)}, bf16[32,7168]{1,0:T(8,128)(2,1)S(1)}, bf16[32,7168]{1,0:T(8,128)(2,1)S(1)}) custom-call(bf16[64,7296]{1,0:T(8,128)(2,1)} %copy-done.2, bf16[64,7296]{1,0:T(8,128)(2,1)} %broadcast_select_fusion.refs_1_, bf16[32,7296]{1,0:T(8,128)(2,1)S(1)} %collective-permute-done.12.refs_2_, ...), custom_call_target="tpu_custom_call" | custom-call | flops 8455716864 | bytes 49545216 | tf_op jit(solution)/shard_map/pallas_call | solution.py:156
  112.7 1.7 collective-permute-start.14
  114.4 1.5 collective-permute-start.15
  116.4 9.9 %collective-permute-done.14 = bf16[32,7168]{1,0:T(8,128)(2,1)S(1)} collective-permute-done((bf16[32,7168]{1,0:T(8,128)(2,1)S(1)}, bf16[32,7168]{1,0:T(8,128)(2,1)S(1)}, u32[]{:S(2)}, u32[]{:S(2)}) %collective-permute-start.14) | collective-permute-done | bytes 458784 | tf_op jit(solution)/shard_map/ppermute | solution.py:203
  126.5 1.6 collective-permute-start.16
  128.9 11.4 %collective-permute-done.17 = bf16[64,7168]{1,0:T(8,128)(2,1)S(1)} collective-permute-done((bf16[64,7168]{1,0:T(8,128)(2,1)S(1)}, bf16[64,7168]{1,0:T(8,128)(2,1)S(1)}, u32[]{:S(2)}, u32[]{:S(2)}) %collective-permute-start.17) | collective-permute-done | bytes 917536 | tf_op jit(solution)/shard_map/ppermute | solution.py:203
  140.3 1.1 collective-permute-done.16
  142.8 6.6 %collective-permute-start.20 = (bf16[64,7168]{1,0:T(8,128)(2,1)S(1)}, bf16[64,7168]{1,0:T(8,128)(2,1)S(1)}, u32[]{:S(2)}, u32[]{:S(2)}) collective-permute-start(bf16[64,7168]{1,0:T(8,128)(2,1)S(1)} %get-tuple-element.93), channel_id=1, source_target_pairs={{0,4},{2,6},{12,8},{14,10},{1,5},{3,7},{13,9},{15,11},{16,20},{18,... | collective-permute-start | bytes 2752520 | tf_op jit(solution)/shard_map/ppermute | solution.py:203
  150.0 17.8 %shard_map.66 = (bf16[64,7168]{1,0:T(8,128)(2,1)S(1)}, bf16[64,7168]{1,0:T(8,128)(2,1)S(1)}, bf16[64,7168]{1,0:T(8,128)(2,1)S(1)}) custom-call(bf16[64,7296]{1,0:T(8,128)(2,1)S(1)} %pad_maximum_fusion.refs_0_, bf16[64,7296]{1,0:T(8,128)(2,1)} %copy-done.1, bf16[64,7296]{1,0:T(8,128)(2,1)} %collective-permute-done.refs_2_, s32[1]{0:T(128)} %bitcast.refs_2_.refs_4_.refs_3_, ...), custom_call_target="tpu_custom_call" | custom-call | flops 8455716864 | bytes 49545216 | tf_op jit(solution)/shard_map/pallas_call | solution.py:156
  169.2 1.6 collective-permute-start.22
  170.8 11.7 %collective-permute-done.23 = bf16[64,7168]{1,0:T(8,128)(2,1)S(1)} collective-permute-done((bf16[64,7168]{1,0:T(8,128)(2,1)S(1)}, bf16[64,7168]{1,0:T(8,128)(2,1)S(1)}, u32[]{:S(2)}, u32[]{:S(2)}) %collective-permute-start.23) | collective-permute-done | bytes 917536 | tf_op jit(solution)/shard_map/ppermute | solution.py:203
  182.5 1.4 collective-permute-done.22
  183.9 1.4 add_convert_fusion
  (46 shorter events, 9.5 us)
Async XLA Ops:
  0.0 30.3 %collective-permute-start.8 = (bf16[1,7168,512]{2,1,0:T(8,128)(2,1)}, bf16[1,7168,512]{2,1,0:T(8,128)(2,1)S(1)}, u32[]{:S(2)}, u32[]{:S(2)}) collective-permute-start(bf16[1,7168,512]{2,1,0:T(8,128)(2,1)} %refs_4_.3), channel_id=1, source_target_pairs={{0,1},{1,0},{2,3},{3,2},{4,5},{5,4},{6,7},{7,6},{8,9},{9,8},{10,11... | collective-permute-start | bytes 22020104 | tf_op jit(solution)/shard_map/ppermute | solution.py:209
  3.2 24.1 %collective-permute-start = (bf16[64,7296]{1,0:T(8,128)(2,1)S(1)}, bf16[64,7296]{1,0:T(8,128)(2,1)}, u32[]{:S(2)}, u32[]{:S(2)}) collective-permute-start(bf16[64,7296]{1,0:T(8,128)(2,1)S(1)} %pad_maximum_fusion.refs_0_), channel_id=1, source_target_pairs={{0,4},{2,6},{4,0},{6,2},{8,12},{10,14},{12,8},{14,10},{1,5},{3,7},... | collective-permute-start | bytes 2801672 | tf_op jit(solution)/shard_map/ppermute | solution.py:203
  5.8 21.5 %collective-permute-start.1 = (bf16[64,7296]{1,0:T(8,128)(2,1)S(1)}, bf16[64,7296]{1,0:T(8,128)(2,1)}, u32[]{:S(2)}, u32[]{:S(2)}) collective-permute-start(bf16[64,7296]{1,0:T(8,128)(2,1)S(1)} %pad_maximum_fusion.refs_0_), channel_id=1, source_target_pairs={{4,8},{8,4},{6,10},{10,6},{5,9},{9,5},{7,11},{11,7},{20,24},{24,20... | collective-permute-start | bytes 2801672 | tf_op jit(solution)/shard_map/ppermute | solution.py:203
  7.5 22.8 %collective-permute-start.2 = (bf16[64,7296]{1,0:T(8,128)(2,1)S(1)}, bf16[64,7296]{1,0:T(8,128)(2,1)S(1)}, u32[]{:S(2)}, u32[]{:S(2)}) collective-permute-start(bf16[64,7296]{1,0:T(8,128)(2,1)S(1)} %pad_maximum_fusion.refs_0_), channel_id=1, source_target_pairs={{0,2},{2,0},{4,6},{6,4},{8,10},{10,8},{12,14},{14,12},{1,3},{3,1},... | collective-permute-start | bytes 2801672 | tf_op jit(solution)/shard_map/ppermute | solution.py:203
  9.0 53.6 %collective-permute-start.7 = (bf16[1,7168,512]{2,1,0:T(8,128)(2,1)}, bf16[1,7168,512]{2,1,0:T(8,128)(2,1)}, u32[]{:S(2)}, u32[]{:S(2)}) collective-permute-start(bf16[1,7168,512]{2,1,0:T(8,128)(2,1)} %refs_5_.3), channel_id=1, source_target_pairs={{0,1},{1,0},{2,3},{3,2},{4,5},{5,4},{6,7},{7,6},{8,9},{9,8},{10,11... | collective-permute-start | bytes 22020104 | tf_op jit(solution)/shard_map/ppermute | solution.py:209
  30.3 3.7 %copy-start.1 = (bf16[64,7296]{1,0:T(8,128)(2,1)}, bf16[64,7296]{1,0:T(8,128)(2,1)S(1)}, u32[]{:S(2)}) copy-start(bf16[64,7296]{1,0:T(8,128)(2,1)S(1)} %collective-permute-done.2.refs_1_) | copy-start | bytes 2801668
  30.3 3.0 %copy-start = (bf16[1,7168,512]{2,1,0:T(8,128)(2,1)}, bf16[1,7168,512]{2,1,0:T(8,128)(2,1)S(1)}, u32[]{:S(2)}) copy-start(bf16[1,7168,512]{2,1,0:T(8,128)(2,1)S(1)} %collective-permute-done.8.refs_5_.refs_7_.refs_6_) | copy-start | bytes 22020100
  30.3 32.3 %collective-permute-start.9 = (bf16[1,512,7168]{2,1,0:T(8,128)(2,1)}, bf16[1,512,7168]{2,1,0:T(8,128)(2,1)}, u32[]{:S(2)}, u32[]{:S(2)}) collective-permute-start(bf16[1,512,7168]{2,1,0:T(8,128)(2,1)} %refs_8_.1), channel_id=1, source_target_pairs={{0,1},{1,0},{2,3},{3,2},{4,5},{5,4},{6,7},{7,6},{8,9},{9,8},{10,11... | collective-permute-start | bytes 22020104 | tf_op jit(solution)/shard_map/ppermute | solution.py:209
  33.3 3.6 %collective-permute-start.3 = (bf16[64,7296]{1,0:T(8,128)(2,1)}, bf16[64,7296]{1,0:T(8,128)(2,1)S(1)}, u32[]{:S(2)}, u32[]{:S(2)}) collective-permute-start(bf16[64,7296]{1,0:T(8,128)(2,1)} %collective-permute-done.refs_2_), channel_id=1, source_target_pairs={{4,8},{8,4},{6,10},{10,6},{5,9},{9,5},{7,11},{11,7},{20,24},{24,20... | collective-permute-start | bytes 2801672 | tf_op jit(solution)/shard_map/ppermute | solution.py:203
  34.0 22.3 %collective-permute-start.6 = (bf16[64,7296]{1,0:T(8,128)(2,1)}, bf16[64,7296]{1,0:T(8,128)(2,1)S(1)}, u32[]{:S(2)}, u32[]{:S(2)}) collective-permute-start(bf16[64,7296]{1,0:T(8,128)(2,1)} %collective-permute-done.refs_2_), channel_id=1, source_target_pairs={{0,2},{2,0},{4,6},{6,4},{8,10},{10,8},{12,14},{14,12},{1,3},{3,1},... | collective-permute-start | bytes 2801672 | tf_op jit(solution)/shard_map/ppermute | solution.py:203
  35.6 27.0 %collective-permute-start.5 = (bf16[64,7296]{1,0:T(8,128)(2,1)}, bf16[64,7296]{1,0:T(8,128)(2,1)}, u32[]{:S(2)}, u32[]{:S(2)}) collective-permute-start(bf16[64,7296]{1,0:T(8,128)(2,1)} %collective-permute-done.1), channel_id=1, source_target_pairs={{4,0},{6,2},{8,12},{10,14},{5,1},{7,3},{9,13},{11,15},{20,16},{22,... | collective-permute-start | bytes 2801672 | tf_op jit(solution)/shard_map/ppermute | solution.py:203
  36.9 44.7 %collective-permute-start.4 = (bf16[64,7296]{1,0:T(8,128)(2,1)S(1)}, bf16[64,7296]{1,0:T(8,128)(2,1)S(1)}, u32[]{:S(2)}, u32[]{:S(2)}) collective-permute-start(bf16[64,7296]{1,0:T(8,128)(2,1)S(1)} %collective-permute-done.3), channel_id=1, source_target_pairs={{4,0},{6,2},{8,12},{10,14},{5,1},{7,3},{9,13},{11,15},{20,16},{22,... | collective-permute-start | bytes 2801672 | tf_op jit(solution)/shard_map/ppermute | solution.py:203
  63.9 20.8 %collective-permute-start.10 = (bf16[64,7296]{1,0:T(8,128)(2,1)S(1)}, bf16[64,7296]{1,0:T(8,128)(2,1)S(1)}, u32[]{:S(2)}, u32[]{:S(2)}) collective-permute-start(bf16[64,7296]{1,0:T(8,128)(2,1)S(1)} %broadcast_select_fusion.1.refs_1_), channel_id=1, source_target_pairs={{0,2},{2,0},{4,6},{6,4},{8,10},{10,8},{12,14},{14,12},{1,3},{3,1},... | collective-permute-start | bytes 2801672 | tf_op jit(solution)/shard_map/ppermute | solution.py:203
  64.0 17.5 %collective-permute-start.11 = (bf16[32,7296]{1,0:T(8,128)(2,1)S(1)}, bf16[32,7296]{1,0:T(8,128)(2,1)S(1)}, u32[]{:S(2)}, u32[]{:S(2)}) collective-permute-start(bf16[32,7296]{1,0:T(8,128)(2,1)S(1)} %slice.21), channel_id=1, source_target_pairs={{4,8},{8,4},{6,10},{10,6},{5,9},{9,5},{7,11},{11,7},{20,24},{24,20... | collective-permute-start | bytes 1400840 | tf_op jit(solution)/shard_map/ppermute | solution.py:203
  84.7 2.6 %copy-start.2 = (bf16[64,7296]{1,0:T(8,128)(2,1)}, bf16[64,7296]{1,0:T(8,128)(2,1)S(1)}, u32[]{:S(2)}) copy-start(bf16[64,7296]{1,0:T(8,128)(2,1)S(1)} %collective-permute-done.10.refs_0_) | copy-start | bytes 2801668
  84.8 9.2 %collective-permute-start.12 = (bf16[32,7296]{1,0:T(8,128)(2,1)S(1)}, bf16[32,7296]{1,0:T(8,128)(2,1)S(1)}, u32[]{:S(2)}, u32[]{:S(2)}) collective-permute-start(bf16[32,7296]{1,0:T(8,128)(2,1)S(1)} %slice_select_fusion), channel_id=1, source_target_pairs={{0,2},{2,0},{4,6},{6,4},{8,10},{10,8},{12,14},{14,12},{1,3},{3,1},... | collective-permute-start | bytes 1400840 | tf_op jit(solution)/shard_map/ppermute | solution.py:203
  84.9 10.9 %collective-permute-start.13 = (bf16[32,7296]{1,0:T(8,128)(2,1)S(1)}, bf16[32,7296]{1,0:T(8,128)(2,1)S(1)}, u32[]{:S(2)}, u32[]{:S(2)}) collective-permute-start(bf16[32,7296]{1,0:T(8,128)(2,1)S(1)} %collective-permute-done.11), channel_id=1, source_target_pairs={{4,0},{6,2},{8,12},{10,14},{5,1},{7,3},{9,13},{11,15},{20,16},{22,... | collective-permute-start | bytes 1400840 | tf_op jit(solution)/shard_map/ppermute | solution.py:203
  112.7 13.5 %collective-permute-start.14 = (bf16[32,7168]{1,0:T(8,128)(2,1)S(1)}, bf16[32,7168]{1,0:T(8,128)(2,1)S(1)}, u32[]{:S(2)}, u32[]{:S(2)}) collective-permute-start(bf16[32,7168]{1,0:T(8,128)(2,1)S(1)} %get-tuple-element.79), channel_id=1, source_target_pairs={{0,2},{2,0},{4,6},{6,4},{8,10},{10,8},{12,14},{14,12},{1,3},{3,1},... | collective-permute-start | bytes 1376264 | tf_op jit(solution)/shard_map/ppermute | solution.py:203
  114.4 11.9 %collective-permute-start.15 = (bf16[32,7168]{1,0:T(8,128)(2,1)S(1)}, bf16[32,7168]{1,0:T(8,128)(2,1)S(1)}, u32[]{:S(2)}, u32[]{:S(2)}) collective-permute-start(bf16[32,7168]{1,0:T(8,128)(2,1)S(1)} %get-tuple-element.80), channel_id=1, source_target_pairs={{0,4},{2,6},{12,8},{14,10},{1,5},{3,7},{13,9},{15,11},{16,20},{18,... | collective-permute-start | bytes 1376264 | tf_op jit(solution)/shard_map/ppermute | solution.py:203
  115.9 24.4 %collective-permute-start.17 = (bf16[64,7168]{1,0:T(8,128)(2,1)S(1)}, bf16[64,7168]{1,0:T(8,128)(2,1)S(1)}, u32[]{:S(2)}, u32[]{:S(2)}) collective-permute-start(bf16[64,7168]{1,0:T(8,128)(2,1)S(1)} %get-tuple-element.82), channel_id=1, source_target_pairs={{0,2},{2,0},{4,6},{6,4},{8,10},{10,8},{12,14},{14,12},{1,3},{3,1},... | collective-permute-start | bytes 2752520 | tf_op jit(solution)/shard_map/ppermute | solution.py:203
  126.5 15.0 %collective-permute-start.16 = (bf16[64,7168]{1,0:T(8,128)(2,1)S(1)}, bf16[64,7168]{1,0:T(8,128)(2,1)S(1)}, u32[]{:S(2)}, u32[]{:S(2)}) collective-permute-start(bf16[64,7168]{1,0:T(8,128)(2,1)S(1)} %pad_maximum_fusion.1), channel_id=1, source_target_pairs={{0,4},{2,6},{12,8},{14,10},{1,5},{3,7},{13,9},{15,11},{16,20},{18,... | collective-permute-start | bytes 2752520 | tf_op jit(solution)/shard_map/ppermute | solution.py:203
  128.2 0.7 collective-permute-start.18
  142.1 25.7 %collective-permute-start.19 = (bf16[64,7168]{1,0:T(8,128)(2,1)S(1)}, bf16[64,7168]{1,0:T(8,128)(2,1)S(1)}, u32[]{:S(2)}, u32[]{:S(2)}) collective-permute-start(bf16[64,7168]{1,0:T(8,128)(2,1)S(1)} %get-tuple-element.92), channel_id=1, source_target_pairs={{4,8},{8,4},{6,10},{10,6},{5,9},{9,5},{7,11},{11,7},{20,24},{24,20... | collective-permute-start | bytes 2752520 | tf_op jit(solution)/shard_map/ppermute | solution.py:203
  142.8 25.0 %collective-permute-start.20 = (bf16[64,7168]{1,0:T(8,128)(2,1)S(1)}, bf16[64,7168]{1,0:T(8,128)(2,1)S(1)}, u32[]{:S(2)}, u32[]{:S(2)}) collective-permute-start(bf16[64,7168]{1,0:T(8,128)(2,1)S(1)} %get-tuple-element.93), channel_id=1, source_target_pairs={{0,4},{2,6},{12,8},{14,10},{1,5},{3,7},{13,9},{15,11},{16,20},{18,... | collective-permute-start | bytes 2752520 | tf_op jit(solution)/shard_map/ppermute | solution.py:203
  149.4 18.5 %collective-permute-start.21 = (bf16[64,7168]{1,0:T(8,128)(2,1)S(1)}, bf16[64,7168]{1,0:T(8,128)(2,1)S(1)}, u32[]{:S(2)}, u32[]{:S(2)}) collective-permute-start(bf16[64,7168]{1,0:T(8,128)(2,1)S(1)} %pad_maximum_fusion.2), channel_id=1, source_target_pairs={{0,2},{2,0},{4,6},{6,4},{8,10},{10,8},{12,14},{14,12},{1,3},{3,1},... | collective-permute-start | bytes 2752520 | tf_op jit(solution)/shard_map/ppermute | solution.py:203
  168.2 14.3 %collective-permute-start.23 = (bf16[64,7168]{1,0:T(8,128)(2,1)S(1)}, bf16[64,7168]{1,0:T(8,128)(2,1)S(1)}, u32[]{:S(2)}, u32[]{:S(2)}) collective-permute-start(bf16[64,7168]{1,0:T(8,128)(2,1)S(1)} %add_convert_fusion.2), channel_id=1, source_target_pairs={{0,4},{2,6},{4,0},{6,2},{8,12},{10,14},{12,8},{14,10},{1,5},{3,7},... | collective-permute-start | bytes 2752520 | tf_op jit(solution)/shard_map/ppermute | solution.py:203
  168.5 14.0 %collective-permute-start.24 = (bf16[64,7168]{1,0:T(8,128)(2,1)S(1)}, bf16[64,7168]{1,0:T(8,128)(2,1)S(1)}, u32[]{:S(2)}, u32[]{:S(2)}) collective-permute-start(bf16[64,7168]{1,0:T(8,128)(2,1)S(1)} %add_convert_fusion.1), channel_id=1, source_target_pairs={{4,8},{8,4},{6,10},{10,6},{5,9},{9,5},{7,11},{11,7},{20,24},{24,20... | collective-permute-start | bytes 2752520 | tf_op jit(solution)/shard_map/ppermute | solution.py:203
  169.2 14.6 %collective-permute-start.22 = (bf16[64,7168]{1,0:T(8,128)(2,1)S(1)}, bf16[64,7168]{1,0:T(8,128)(2,1)S(1)}, u32[]{:S(2)}, u32[]{:S(2)}) collective-permute-start(bf16[64,7168]{1,0:T(8,128)(2,1)S(1)} %get-tuple-element.102), channel_id=1, source_target_pairs={{0,2},{2,0},{4,6},{6,4},{8,10},{10,8},{12,14},{14,12},{1,3},{3,1},... | collective-permute-start | bytes 2752520 | tf_op jit(solution)/shard_map/ppermute | solution.py:203

commit v6 on v5

--- a/solution.py
+++ b/solution.py
@@ -81,9 +81,10 @@
             for i in range(count)
         ]
 
+    start_load(jnp.int32(0))
     for i in range(count):
         block_copy(i).start()
-    for index in range(RING):
+    for index in range(1, RING):
         start_load(jnp.int32(index))
     for i in range(count):
         block_copy(i).wait()
@@ -149,7 +150,7 @@
     total_width = blocks[0].shape[1]
     _, width, depth = weights[0].shape
     slab = divisor_tile(width, 1792, 128)
-    out_tile = divisor_tile(width, 1024, 128)
+    out_tile = divisor_tile(width, 1792, 128)
     tiles = width // out_tile
     row_count = sum(block.shape[0] for block in blocks)
     anywhere = pl.BlockSpec(memory_space=pl.ANY)

time: 186 us -> 185 us (level)
  Pallas kernels: 50.7 us -> 47.9 us
  waiting for transfers between devices: 93.7 us -> 95.7 us
    pallas_call x3, Pallas kernels: 50.7 us -> 47.9 us  [expert_rows(): pl.pallas_call(functools.partial(expert_kernel, count, slab, out_tile), i...]
    ppermute x22, waiting for transfers between devices: 93.7 us -> 95.7 us  [send(): return lax.ppermute(array, 'node', pairs)]
  transfers between devices with their start and end apart: 25 -> 25, of which waited for: 13 -> 13; matrix products, arithmetic and copies ran while one was open for 3% -> 3% of each run, Pallas kernels for 18% -> 17%
where the time goes in v6:
time: 185 us
  waiting for transfers between devices  95.7 us (52%)
  Pallas kernels  47.9 us (26%)
  starting transfers between devices  29.5 us (16%)
  other arithmetic  8.15 us (4%)
  local copies, waits for them, and re-layouts  2.98 us (2%)
    ppermute x22, waiting for transfers between devices, send(): return lax.ppermute(array, 'node', pairs)  95.7 us
    pallas_call x3, Pallas kernels, expert_rows(): pl.pallas_call(functools.partial(expert_kernel, count, slab, out_tile), i...  47.9 us
    ppermute x22, starting transfers between devices, send(): return lax.ppermute(array, 'node', pairs)  28.9 us
  transfers between devices with their start and end apart: 25, of which 13 were waited for; matrix products, arithmetic and copies ran while one was open for 3% of the time, Pallas kernels for 17%

profile of v6, /device:TPU:0, one launch (start us, length us, event | category | flops | bytes accessed | tf_op | source)
XLA Modules:
  0.0 184.5 jit_solution(6934625296062213483)
XLA Ops:
  2.0 1.2 pad_maximum_fusion.refs_0_
  3.2 2.6 %collective-permute-start = (bf16[64,7296]{1,0:T(8,128)(2,1)S(1)}, bf16[64,7296]{1,0:T(8,128)(2,1)}, u32[]{:S(2)}, u32[]{:S(2)}) collective-permute-start(bf16[64,7296]{1,0:T(8,128)(2,1)S(1)} %pad_maximum_fusion.refs_0_), channel_id=1, source_target_pairs={{0,4},{2,6},{4,0},{6,2},{8,12},{10,14},{12,8},{14,10},{1,5},{3,7},... | collective-permute-start | bytes 2801672 | tf_op jit(solution)/shard_map/ppermute | solution.py:204
  5.8 1.6 collective-permute-start.1
  7.5 1.5 collective-permute-start.2
  9.0 18.3 %collective-permute-done.refs_2_ = bf16[64,7296]{1,0:T(8,128)(2,1)} collective-permute-done((bf16[64,7296]{1,0:T(8,128)(2,1)S(1)}, bf16[64,7296]{1,0:T(8,128)(2,1)}, u32[]{:S(2)}, u32[]{:S(2)}) %collective-permute-start) | collective-permute-done | bytes 933920 | tf_op jit(solution)/shard_map/ppermute | solution.py:204
  27.3 3.0 %collective-permute-done.2.refs_1_ = bf16[64,7296]{1,0:T(8,128)(2,1)S(1)} collective-permute-done((bf16[64,7296]{1,0:T(8,128)(2,1)S(1)}, bf16[64,7296]{1,0:T(8,128)(2,1)S(1)}, u32[]{:S(2)}, u32[]{:S(2)}) %collective-permute-start.2) | collective-permute-done | bytes 933920 | tf_op jit(solution)/shard_map/ppermute | solution.py:204
  30.4 2.9 %copy-done = bf16[1,7168,512]{2,1,0:T(8,128)(2,1)} copy-done((bf16[1,7168,512]{2,1,0:T(8,128)(2,1)}, bf16[1,7168,512]{2,1,0:T(8,128)(2,1)S(1)}, u32[]{:S(2)}) %copy-start) | copy-done | bytes 7340056
  34.0 1.6 collective-permute-start.6
  35.6 1.3 collective-permute-start.5
  36.9 1.3 collective-permute-start.4
  38.2 18.1 %collective-permute-done.6.refs_0_ = bf16[64,7296]{1,0:T(8,128)(2,1)S(1)} collective-permute-done((bf16[64,7296]{1,0:T(8,128)(2,1)}, bf16[64,7296]{1,0:T(8,128)(2,1)S(1)}, u32[]{:S(2)}, u32[]{:S(2)}) %collective-permute-start.6) | collective-permute-done | bytes 933920 | tf_op jit(solution)/shard_map/ppermute | solution.py:204
  56.3 6.3 %collective-permute-done.5 = bf16[64,7296]{1,0:T(8,128)(2,1)} collective-permute-done((bf16[64,7296]{1,0:T(8,128)(2,1)}, bf16[64,7296]{1,0:T(8,128)(2,1)}, u32[]{:S(2)}, u32[]{:S(2)}) %collective-permute-start.5) | collective-permute-done | bytes 933920 | tf_op jit(solution)/shard_map/ppermute | solution.py:204
  62.6 1.3 broadcast_select_fusion.1.refs_1_
  64.7 14.8 %shard_map.64 = (bf16[64,7168]{1,0:T(8,128)(2,1)S(1)}, bf16[64,7168]{1,0:T(8,128)(2,1)S(1)}) custom-call(bf16[64,7296]{1,0:T(8,128)(2,1)S(1)} %collective-permute-done.6.refs_0_, bf16[64,7296]{1,0:T(8,128)(2,1)S(1)} %broadcast_select_fusion.1.refs_1_, s32[1]{0:T(128)} %bitcast.refs_2_.refs_4_.refs_3_, bf16[1,7168,512]{2,1,0:T(8,128)(2,1)} %refs_4_.3, ...), custom_call_target="tpu_custom_call" | custom-call | flops 5637144576 | bytes 47710208 | tf_op jit(solution)/shard_map/pallas_call | solution.py:157
  79.5 2.0 %collective-permute-done.4 = bf16[64,7296]{1,0:T(8,128)(2,1)S(1)} collective-permute-done((bf16[64,7296]{1,0:T(8,128)(2,1)S(1)}, bf16[64,7296]{1,0:T(8,128)(2,1)S(1)}, u32[]{:S(2)}, u32[]{:S(2)}) %collective-permute-start.4) | collective-permute-done | bytes 933920 | tf_op jit(solution)/shard_map/ppermute | solution.py:204
  81.6 3.1 %collective-permute-done.10.refs_0_ = bf16[64,7296]{1,0:T(8,128)(2,1)S(1)} collective-permute-done((bf16[64,7296]{1,0:T(8,128)(2,1)S(1)}, bf16[64,7296]{1,0:T(8,128)(2,1)S(1)}, u32[]{:S(2)}, u32[]{:S(2)}) %collective-permute-start.10) | collective-permute-done | bytes 933920 | tf_op jit(solution)/shard_map/ppermute | solution.py:204
  84.9 1.3 collective-permute-start.13
  86.2 1.2 broadcast_select_fusion.refs_1_
  87.3 6.6 %collective-permute-done.12.refs_2_ = bf16[32,7296]{1,0:T(8,128)(2,1)S(1)} collective-permute-done((bf16[32,7296]{1,0:T(8,128)(2,1)S(1)}, bf16[32,7296]{1,0:T(8,128)(2,1)S(1)}, u32[]{:S(2)}, u32[]{:S(2)}) %collective-permute-start.12) | collective-permute-done | bytes 466976 | tf_op jit(solution)/shard_map/ppermute | solution.py:204
  94.0 1.8 collective-permute-done.13
  95.8 16.2 %shard_map.65 = (bf16[64,7168]{1,0:T(8,128)(2,1)S(1)}, bf16[64,7168]{1,0:T(8,128)(2,1)S(1)}, bf16[32,7168]{1,0:T(8,128)(2,1)S(1)}, bf16[32,7168]{1,0:T(8,128)(2,1)S(1)}) custom-call(bf16[64,7296]{1,0:T(8,128)(2,1)} %copy-done.2, bf16[64,7296]{1,0:T(8,128)(2,1)} %broadcast_select_fusion.refs_1_, bf16[32,7296]{1,0:T(8,128)(2,1)S(1)} %collective-permute-done.12.refs_2_, ...), custom_call_target="tpu_custom_call" | custom-call | flops 8455716864 | bytes 49545216 | tf_op jit(solution)/shard_map/pallas_call | solution.py:157
  112.0 1.7 collective-permute-start.14
  113.7 1.5 collective-permute-start.15
  115.7 9.8 %collective-permute-done.14 = bf16[32,7168]{1,0:T(8,128)(2,1)S(1)} collective-permute-done((bf16[32,7168]{1,0:T(8,128)(2,1)S(1)}, bf16[32,7168]{1,0:T(8,128)(2,1)S(1)}, u32[]{:S(2)}, u32[]{:S(2)}) %collective-permute-start.14) | collective-permute-done | bytes 458784 | tf_op jit(solution)/shard_map/ppermute | solution.py:204
  125.7 1.6 collective-permute-start.16
  128.2 11.4 %collective-permute-done.17 = bf16[64,7168]{1,0:T(8,128)(2,1)S(1)} collective-permute-done((bf16[64,7168]{1,0:T(8,128)(2,1)S(1)}, bf16[64,7168]{1,0:T(8,128)(2,1)S(1)}, u32[]{:S(2)}, u32[]{:S(2)}) %collective-permute-start.17) | collective-permute-done | bytes 917536 | tf_op jit(solution)/shard_map/ppermute | solution.py:204
  142.1 6.6 %collective-permute-start.20 = (bf16[64,7168]{1,0:T(8,128)(2,1)S(1)}, bf16[64,7168]{1,0:T(8,128)(2,1)S(1)}, u32[]{:S(2)}, u32[]{:S(2)}) collective-permute-start(bf16[64,7168]{1,0:T(8,128)(2,1)S(1)} %get-tuple-element.93), channel_id=1, source_target_pairs={{0,4},{2,6},{12,8},{14,10},{1,5},{3,7},{13,9},{15,11},{16,20},{18,... | collective-permute-start | bytes 2752520 | tf_op jit(solution)/shard_map/ppermute | solution.py:204
  149.3 16.9 %shard_map.66 = (bf16[64,7168]{1,0:T(8,128)(2,1)S(1)}, bf16[64,7168]{1,0:T(8,128)(2,1)S(1)}, bf16[64,7168]{1,0:T(8,128)(2,1)S(1)}) custom-call(bf16[64,7296]{1,0:T(8,128)(2,1)S(1)} %pad_maximum_fusion.refs_0_, bf16[64,7296]{1,0:T(8,128)(2,1)} %copy-done.1, bf16[64,7296]{1,0:T(8,128)(2,1)} %collective-permute-done.refs_2_, s32[1]{0:T(128)} %bitcast.refs_2_.refs_4_.refs_3_, ...), custom_call_target="tpu_custom_call" | custom-call | flops 8455716864 | bytes 49545216 | tf_op jit(solution)/shard_map/pallas_call | solution.py:157
  167.5 1.6 collective-permute-start.22
  169.1 11.7 %collective-permute-done.23 = bf16[64,7168]{1,0:T(8,128)(2,1)S(1)} collective-permute-done((bf16[64,7168]{1,0:T(8,128)(2,1)S(1)}, bf16[64,7168]{1,0:T(8,128)(2,1)S(1)}, u32[]{:S(2)}, u32[]{:S(2)}) %collective-permute-start.23) | collective-permute-done | bytes 917536 | tf_op jit(solution)/shard_map/ppermute | solution.py:204
  180.8 2.3 %collective-permute-done.22 = bf16[64,7168]{1,0:T(8,128)(2,1)S(1)} collective-permute-done((bf16[64,7168]{1,0:T(8,128)(2,1)S(1)}, bf16[64,7168]{1,0:T(8,128)(2,1)S(1)}, u32[]{:S(2)}, u32[]{:S(2)}) %collective-permute-start.22) | collective-permute-done | bytes 917536 | tf_op jit(solution)/shard_map/ppermute | solution.py:204
  183.1 1.4 add_convert_fusion
  (46 shorter events, 9.7 us)
Async XLA Ops:
  0.0 30.3 %collective-permute-start.8 = (bf16[1,7168,512]{2,1,0:T(8,128)(2,1)}, bf16[1,7168,512]{2,1,0:T(8,128)(2,1)S(1)}, u32[]{:S(2)}, u32[]{:S(2)}) collective-permute-start(bf16[1,7168,512]{2,1,0:T(8,128)(2,1)} %refs_4_.3), channel_id=1, source_target_pairs={{0,1},{1,0},{2,3},{3,2},{4,5},{5,4},{6,7},{7,6},{8,9},{9,8},{10,11... | collective-permute-start | bytes 22020104 | tf_op jit(solution)/shard_map/ppermute | solution.py:210
  3.2 24.1 %collective-permute-start = (bf16[64,7296]{1,0:T(8,128)(2,1)S(1)}, bf16[64,7296]{1,0:T(8,128)(2,1)}, u32[]{:S(2)}, u32[]{:S(2)}) collective-permute-start(bf16[64,7296]{1,0:T(8,128)(2,1)S(1)} %pad_maximum_fusion.refs_0_), channel_id=1, source_target_pairs={{0,4},{2,6},{4,0},{6,2},{8,12},{10,14},{12,8},{14,10},{1,5},{3,7},... | collective-permute-start | bytes 2801672 | tf_op jit(solution)/shard_map/ppermute | solution.py:204
  5.8 21.5 %collective-permute-start.1 = (bf16[64,7296]{1,0:T(8,128)(2,1)S(1)}, bf16[64,7296]{1,0:T(8,128)(2,1)}, u32[]{:S(2)}, u32[]{:S(2)}) collective-permute-start(bf16[64,7296]{1,0:T(8,128)(2,1)S(1)} %pad_maximum_fusion.refs_0_), channel_id=1, source_target_pairs={{4,8},{8,4},{6,10},{10,6},{5,9},{9,5},{7,11},{11,7},{20,24},{24,20... | collective-permute-start | bytes 2801672 | tf_op jit(solution)/shard_map/ppermute | solution.py:204
  7.5 22.8 %collective-permute-start.2 = (bf16[64,7296]{1,0:T(8,128)(2,1)S(1)}, bf16[64,7296]{1,0:T(8,128)(2,1)S(1)}, u32[]{:S(2)}, u32[]{:S(2)}) collective-permute-start(bf16[64,7296]{1,0:T(8,128)(2,1)S(1)} %pad_maximum_fusion.refs_0_), channel_id=1, source_target_pairs={{0,2},{2,0},{4,6},{6,4},{8,10},{10,8},{12,14},{14,12},{1,3},{3,1},... | collective-permute-start | bytes 2801672 | tf_op jit(solution)/shard_map/ppermute | solution.py:204
  9.0 53.6 %collective-permute-start.7 = (bf16[1,7168,512]{2,1,0:T(8,128)(2,1)}, bf16[1,7168,512]{2,1,0:T(8,128)(2,1)}, u32[]{:S(2)}, u32[]{:S(2)}) collective-permute-start(bf16[1,7168,512]{2,1,0:T(8,128)(2,1)} %refs_5_.3), channel_id=1, source_target_pairs={{0,1},{1,0},{2,3},{3,2},{4,5},{5,4},{6,7},{7,6},{8,9},{9,8},{10,11... | collective-permute-start | bytes 22020104 | tf_op jit(solution)/shard_map/ppermute | solution.py:210
  30.3 3.7 %copy-start.1 = (bf16[64,7296]{1,0:T(8,128)(2,1)}, bf16[64,7296]{1,0:T(8,128)(2,1)S(1)}, u32[]{:S(2)}) copy-start(bf16[64,7296]{1,0:T(8,128)(2,1)S(1)} %collective-permute-done.2.refs_1_) | copy-start | bytes 2801668
  30.3 3.0 %copy-start = (bf16[1,7168,512]{2,1,0:T(8,128)(2,1)}, bf16[1,7168,512]{2,1,0:T(8,128)(2,1)S(1)}, u32[]{:S(2)}) copy-start(bf16[1,7168,512]{2,1,0:T(8,128)(2,1)S(1)} %collective-permute-done.8.refs_5_.refs_7_.refs_6_) | copy-start | bytes 22020100
  30.3 32.3 %collective-permute-start.9 = (bf16[1,512,7168]{2,1,0:T(8,128)(2,1)}, bf16[1,512,7168]{2,1,0:T(8,128)(2,1)}, u32[]{:S(2)}, u32[]{:S(2)}) collective-permute-start(bf16[1,512,7168]{2,1,0:T(8,128)(2,1)} %refs_8_.1), channel_id=1, source_target_pairs={{0,1},{1,0},{2,3},{3,2},{4,5},{5,4},{6,7},{7,6},{8,9},{9,8},{10,11... | collective-permute-start | bytes 22020104 | tf_op jit(solution)/shard_map/ppermute | solution.py:210
  33.3 3.6 %collective-permute-start.3 = (bf16[64,7296]{1,0:T(8,128)(2,1)}, bf16[64,7296]{1,0:T(8,128)(2,1)S(1)}, u32[]{:S(2)}, u32[]{:S(2)}) collective-permute-start(bf16[64,7296]{1,0:T(8,128)(2,1)} %collective-permute-done.refs_2_), channel_id=1, source_target_pairs={{4,8},{8,4},{6,10},{10,6},{5,9},{9,5},{7,11},{11,7},{20,24},{24,20... | collective-permute-start | bytes 2801672 | tf_op jit(solution)/shard_map/ppermute | solution.py:204
  34.0 22.3 %collective-permute-start.6 = (bf16[64,7296]{1,0:T(8,128)(2,1)}, bf16[64,7296]{1,0:T(8,128)(2,1)S(1)}, u32[]{:S(2)}, u32[]{:S(2)}) collective-permute-start(bf16[64,7296]{1,0:T(8,128)(2,1)} %collective-permute-done.refs_2_), channel_id=1, source_target_pairs={{0,2},{2,0},{4,6},{6,4},{8,10},{10,8},{12,14},{14,12},{1,3},{3,1},... | collective-permute-start | bytes 2801672 | tf_op jit(solution)/shard_map/ppermute | solution.py:204
  35.6 27.0 %collective-permute-start.5 = (bf16[64,7296]{1,0:T(8,128)(2,1)}, bf16[64,7296]{1,0:T(8,128)(2,1)}, u32[]{:S(2)}, u32[]{:S(2)}) collective-permute-start(bf16[64,7296]{1,0:T(8,128)(2,1)} %collective-permute-done.1), channel_id=1, source_target_pairs={{4,0},{6,2},{8,12},{10,14},{5,1},{7,3},{9,13},{11,15},{20,16},{22,... | collective-permute-start | bytes 2801672 | tf_op jit(solution)/shard_map/ppermute | solution.py:204
  36.9 44.7 %collective-permute-start.4 = (bf16[64,7296]{1,0:T(8,128)(2,1)S(1)}, bf16[64,7296]{1,0:T(8,128)(2,1)S(1)}, u32[]{:S(2)}, u32[]{:S(2)}) collective-permute-start(bf16[64,7296]{1,0:T(8,128)(2,1)S(1)} %collective-permute-done.3), channel_id=1, source_target_pairs={{4,0},{6,2},{8,12},{10,14},{5,1},{7,3},{9,13},{11,15},{20,16},{22,... | collective-permute-start | bytes 2801672 | tf_op jit(solution)/shard_map/ppermute | solution.py:204
  63.9 20.8 %collective-permute-start.10 = (bf16[64,7296]{1,0:T(8,128)(2,1)S(1)}, bf16[64,7296]{1,0:T(8,128)(2,1)S(1)}, u32[]{:S(2)}, u32[]{:S(2)}) collective-permute-start(bf16[64,7296]{1,0:T(8,128)(2,1)S(1)} %broadcast_select_fusion.1.refs_1_), channel_id=1, source_target_pairs={{0,2},{2,0},{4,6},{6,4},{8,10},{10,8},{12,14},{14,12},{1,3},{3,1},... | collective-permute-start | bytes 2801672 | tf_op jit(solution)/shard_map/ppermute | solution.py:204
  64.0 17.5 %collective-permute-start.11 = (bf16[32,7296]{1,0:T(8,128)(2,1)S(1)}, bf16[32,7296]{1,0:T(8,128)(2,1)S(1)}, u32[]{:S(2)}, u32[]{:S(2)}) collective-permute-start(bf16[32,7296]{1,0:T(8,128)(2,1)S(1)} %slice.21), channel_id=1, source_target_pairs={{4,8},{8,4},{6,10},{10,6},{5,9},{9,5},{7,11},{11,7},{20,24},{24,20... | collective-permute-start | bytes 1400840 | tf_op jit(solution)/shard_map/ppermute | solution.py:204
  84.7 2.6 %copy-start.2 = (bf16[64,7296]{1,0:T(8,128)(2,1)}, bf16[64,7296]{1,0:T(8,128)(2,1)S(1)}, u32[]{:S(2)}) copy-start(bf16[64,7296]{1,0:T(8,128)(2,1)S(1)} %collective-permute-done.10.refs_0_) | copy-start | bytes 2801668
  84.8 9.2 %collective-permute-start.12 = (bf16[32,7296]{1,0:T(8,128)(2,1)S(1)}, bf16[32,7296]{1,0:T(8,128)(2,1)S(1)}, u32[]{:S(2)}, u32[]{:S(2)}) collective-permute-start(bf16[32,7296]{1,0:T(8,128)(2,1)S(1)} %slice_select_fusion), channel_id=1, source_target_pairs={{0,2},{2,0},{4,6},{6,4},{8,10},{10,8},{12,14},{14,12},{1,3},{3,1},... | collective-permute-start | bytes 1400840 | tf_op jit(solution)/shard_map/ppermute | solution.py:204
  84.9 10.9 %collective-permute-start.13 = (bf16[32,7296]{1,0:T(8,128)(2,1)S(1)}, bf16[32,7296]{1,0:T(8,128)(2,1)S(1)}, u32[]{:S(2)}, u32[]{:S(2)}) collective-permute-start(bf16[32,7296]{1,0:T(8,128)(2,1)S(1)} %collective-permute-done.11), channel_id=1, source_target_pairs={{4,0},{6,2},{8,12},{10,14},{5,1},{7,3},{9,13},{11,15},{20,16},{22,... | collective-permute-start | bytes 1400840 | tf_op jit(solution)/shard_map/ppermute | solution.py:204
  112.0 13.5 %collective-permute-start.14 = (bf16[32,7168]{1,0:T(8,128)(2,1)S(1)}, bf16[32,7168]{1,0:T(8,128)(2,1)S(1)}, u32[]{:S(2)}, u32[]{:S(2)}) collective-permute-start(bf16[32,7168]{1,0:T(8,128)(2,1)S(1)} %get-tuple-element.79), channel_id=1, source_target_pairs={{0,2},{2,0},{4,6},{6,4},{8,10},{10,8},{12,14},{14,12},{1,3},{3,1},... | collective-permute-start | bytes 1376264 | tf_op jit(solution)/shard_map/ppermute | solution.py:204
  113.7 11.9 %collective-permute-start.15 = (bf16[32,7168]{1,0:T(8,128)(2,1)S(1)}, bf16[32,7168]{1,0:T(8,128)(2,1)S(1)}, u32[]{:S(2)}, u32[]{:S(2)}) collective-permute-start(bf16[32,7168]{1,0:T(8,128)(2,1)S(1)} %get-tuple-element.80), channel_id=1, source_target_pairs={{0,4},{2,6},{12,8},{14,10},{1,5},{3,7},{13,9},{15,11},{16,20},{18,... | collective-permute-start | bytes 1376264 | tf_op jit(solution)/shard_map/ppermute | solution.py:204
  115.2 24.4 %collective-permute-start.17 = (bf16[64,7168]{1,0:T(8,128)(2,1)S(1)}, bf16[64,7168]{1,0:T(8,128)(2,1)S(1)}, u32[]{:S(2)}, u32[]{:S(2)}) collective-permute-start(bf16[64,7168]{1,0:T(8,128)(2,1)S(1)} %get-tuple-element.82), channel_id=1, source_target_pairs={{0,2},{2,0},{4,6},{6,4},{8,10},{10,8},{12,14},{14,12},{1,3},{3,1},... | collective-permute-start | bytes 2752520 | tf_op jit(solution)/shard_map/ppermute | solution.py:204
  125.7 15.0 %collective-permute-start.16 = (bf16[64,7168]{1,0:T(8,128)(2,1)S(1)}, bf16[64,7168]{1,0:T(8,128)(2,1)S(1)}, u32[]{:S(2)}, u32[]{:S(2)}) collective-permute-start(bf16[64,7168]{1,0:T(8,128)(2,1)S(1)} %pad_maximum_fusion.1), channel_id=1, source_target_pairs={{0,4},{2,6},{12,8},{14,10},{1,5},{3,7},{13,9},{15,11},{16,20},{18,... | collective-permute-start | bytes 2752520 | tf_op jit(solution)/shard_map/ppermute | solution.py:204
  127.4 0.7 collective-permute-start.18
  141.4 24.8 %collective-permute-start.19 = (bf16[64,7168]{1,0:T(8,128)(2,1)S(1)}, bf16[64,7168]{1,0:T(8,128)(2,1)S(1)}, u32[]{:S(2)}, u32[]{:S(2)}) collective-permute-start(bf16[64,7168]{1,0:T(8,128)(2,1)S(1)} %get-tuple-element.92), channel_id=1, source_target_pairs={{4,8},{8,4},{6,10},{10,6},{5,9},{9,5},{7,11},{11,7},{20,24},{24,20... | collective-permute-start | bytes 2752520 | tf_op jit(solution)/shard_map/ppermute | solution.py:204
  142.1 24.0 %collective-permute-start.20 = (bf16[64,7168]{1,0:T(8,128)(2,1)S(1)}, bf16[64,7168]{1,0:T(8,128)(2,1)S(1)}, u32[]{:S(2)}, u32[]{:S(2)}) collective-permute-start(bf16[64,7168]{1,0:T(8,128)(2,1)S(1)} %get-tuple-element.93), channel_id=1, source_target_pairs={{0,4},{2,6},{12,8},{14,10},{1,5},{3,7},{13,9},{15,11},{16,20},{18,... | collective-permute-start | bytes 2752520 | tf_op jit(solution)/shard_map/ppermute | solution.py:204
  148.7 17.5 %collective-permute-start.21 = (bf16[64,7168]{1,0:T(8,128)(2,1)S(1)}, bf16[64,7168]{1,0:T(8,128)(2,1)S(1)}, u32[]{:S(2)}, u32[]{:S(2)}) collective-permute-start(bf16[64,7168]{1,0:T(8,128)(2,1)S(1)} %pad_maximum_fusion.2), channel_id=1, source_target_pairs={{0,2},{2,0},{4,6},{6,4},{8,10},{10,8},{12,14},{14,12},{1,3},{3,1},... | collective-permute-start | bytes 2752520 | tf_op jit(solution)/shard_map/ppermute | solution.py:204
  166.5 14.3 %collective-permute-start.23 = (bf16[64,7168]{1,0:T(8,128)(2,1)S(1)}, bf16[64,7168]{1,0:T(8,128)(2,1)S(1)}, u32[]{:S(2)}, u32[]{:S(2)}) collective-permute-start(bf16[64,7168]{1,0:T(8,128)(2,1)S(1)} %add_convert_fusion.2), channel_id=1, source_target_pairs={{0,4},{2,6},{4,0},{6,2},{8,12},{10,14},{12,8},{14,10},{1,5},{3,7},... | collective-permute-start | bytes 2752520 | tf_op jit(solution)/shard_map/ppermute | solution.py:204
  166.8 14.0 %collective-permute-start.24 = (bf16[64,7168]{1,0:T(8,128)(2,1)S(1)}, bf16[64,7168]{1,0:T(8,128)(2,1)S(1)}, u32[]{:S(2)}, u32[]{:S(2)}) collective-permute-start(bf16[64,7168]{1,0:T(8,128)(2,1)S(1)} %add_convert_fusion.1), channel_id=1, source_target_pairs={{4,8},{8,4},{6,10},{10,6},{5,9},{9,5},{7,11},{11,7},{20,24},{24,20... | collective-permute-start | bytes 2752520 | tf_op jit(solution)/shard_map/ppermute | solution.py:204
  167.5 15.6 %collective-permute-start.22 = (bf16[64,7168]{1,0:T(8,128)(2,1)S(1)}, bf16[64,7168]{1,0:T(8,128)(2,1)S(1)}, u32[]{:S(2)}, u32[]{:S(2)}) collective-permute-start(bf16[64,7168]{1,0:T(8,128)(2,1)S(1)} %get-tuple-element.102), channel_id=1, source_target_pairs={{0,2},{2,0},{4,6},{6,4},{8,10},{10,8},{12,14},{14,12},{1,3},{3,1},... | collective-permute-start | bytes 2752520 | tf_op jit(solution)/shard_map/ppermute | solution.py:204

commit v7 on v6

--- a/solution.py
+++ b/solution.py
@@ -8,7 +8,7 @@
 from jax.sharding import PartitionSpec as P
 
 LANES = 128
-RING = 3
+RING = 4
 KERNEL_VMEM = 50 * 1024 * 1024
 
 
@@ -89,6 +89,10 @@
     for i in range(count):
         block_copy(i).wait()
 
+    table = rows[:, width:].astype(jnp.float32)
+    lane = lax.broadcasted_iota(jnp.int32, table.shape, 1)
+    scale = jnp.sum(jnp.where(lane == node[0], table, 0.0), axis=1, keepdims=True)
+
     def project(index, half):
         slot = lax.rem(index, RING)
         local = index - half * slabs
@@ -116,10 +120,6 @@
         )
         act = gate_sum[...]
         hidden[half] = (act / (1.0 + jnp.exp(-act)) * up_sum[...]).astype(jnp.bfloat16)
-
-    table = rows[:, width:].astype(jnp.float32)
-    lane = lax.broadcasted_iota(jnp.int32, table.shape, 1)
-    scale = jnp.sum(jnp.where(lane == node[0], table, 0.0), axis=1, keepdims=True)
 
     def down(tile, _):
         slot = lax.rem(tile, RING)

time: 185 us -> 185 us (level)
  no operation moved by 1% of the time
where the time goes in v7:
time: 185 us; the launch traced here: 184 us
  waiting for transfers between devices  95.1 us (51%)
  Pallas kernels  48.4 us (26%)
  starting transfers between devices  29.5 us (16%)
  other arithmetic  8.15 us (4%)
  local copies, waits for them, and re-layouts  2.98 us (2%)
    ppermute x22, waiting for transfers between devices, send(): return lax.ppermute(array, 'node', pairs)  95.1 us
    pallas_call x3, Pallas kernels, expert_rows(): pl.pallas_call(functools.partial(expert_kernel, count, slab, out_tile), i...  48.4 us
    ppermute x22, starting transfers between devices, send(): return lax.ppermute(array, 'node', pairs)  28.9 us
  transfers between devices with their start and end apart: 25, of which 13 were waited for; matrix products, arithmetic and copies ran while one was open for 3% of the time, Pallas kernels for 17%

profile of v7, /device:TPU:0, one launch (start us, length us, event | category | flops | bytes accessed | tf_op | source)
XLA Modules:
  0.0 184.4 jit_solution(16774109741406797043)
XLA Ops:
  2.0 1.2 pad_maximum_fusion.refs_0_
  3.2 2.6 %collective-permute-start = (bf16[64,7296]{1,0:T(8,128)(2,1)S(1)}, bf16[64,7296]{1,0:T(8,128)(2,1)}, u32[]{:S(2)}, u32[]{:S(2)}) collective-permute-start(bf16[64,7296]{1,0:T(8,128)(2,1)S(1)} %pad_maximum_fusion.refs_0_), channel_id=1, source_target_pairs={{0,4},{2,6},{4,0},{6,2},{8,12},{10,14},{12,8},{14,10},{1,5},{3,7},... | collective-permute-start | bytes 2801672 | tf_op jit(solution)/shard_map/ppermute | solution.py:204
  5.8 1.6 collective-permute-start.1
  7.5 1.5 collective-permute-start.2
  9.0 18.3 %collective-permute-done.refs_2_ = bf16[64,7296]{1,0:T(8,128)(2,1)} collective-permute-done((bf16[64,7296]{1,0:T(8,128)(2,1)S(1)}, bf16[64,7296]{1,0:T(8,128)(2,1)}, u32[]{:S(2)}, u32[]{:S(2)}) %collective-permute-start) | collective-permute-done | bytes 933920 | tf_op jit(solution)/shard_map/ppermute | solution.py:204
  27.3 3.0 %collective-permute-done.2.refs_1_ = bf16[64,7296]{1,0:T(8,128)(2,1)S(1)} collective-permute-done((bf16[64,7296]{1,0:T(8,128)(2,1)S(1)}, bf16[64,7296]{1,0:T(8,128)(2,1)S(1)}, u32[]{:S(2)}, u32[]{:S(2)}) %collective-permute-start.2) | collective-permute-done | bytes 933920 | tf_op jit(solution)/shard_map/ppermute | solution.py:204
  30.4 2.9 %copy-done = bf16[1,7168,512]{2,1,0:T(8,128)(2,1)} copy-done((bf16[1,7168,512]{2,1,0:T(8,128)(2,1)}, bf16[1,7168,512]{2,1,0:T(8,128)(2,1)S(1)}, u32[]{:S(2)}) %copy-start) | copy-done | bytes 7340056
  34.0 1.6 collective-permute-start.6
  35.6 1.3 collective-permute-start.5
  36.9 1.3 collective-permute-start.4
  38.2 18.1 %collective-permute-done.6.refs_0_ = bf16[64,7296]{1,0:T(8,128)(2,1)S(1)} collective-permute-done((bf16[64,7296]{1,0:T(8,128)(2,1)}, bf16[64,7296]{1,0:T(8,128)(2,1)S(1)}, u32[]{:S(2)}, u32[]{:S(2)}) %collective-permute-start.6) | collective-permute-done | bytes 933920 | tf_op jit(solution)/shard_map/ppermute | solution.py:204
  56.3 6.3 %collective-permute-done.5 = bf16[64,7296]{1,0:T(8,128)(2,1)} collective-permute-done((bf16[64,7296]{1,0:T(8,128)(2,1)}, bf16[64,7296]{1,0:T(8,128)(2,1)}, u32[]{:S(2)}, u32[]{:S(2)}) %collective-permute-start.5) | collective-permute-done | bytes 933920 | tf_op jit(solution)/shard_map/ppermute | solution.py:204
  62.6 1.3 broadcast_select_fusion.1.refs_1_
  64.7 14.8 %shard_map.64 = (bf16[64,7168]{1,0:T(8,128)(2,1)S(1)}, bf16[64,7168]{1,0:T(8,128)(2,1)S(1)}) custom-call(bf16[64,7296]{1,0:T(8,128)(2,1)S(1)} %collective-permute-done.6.refs_0_, bf16[64,7296]{1,0:T(8,128)(2,1)S(1)} %broadcast_select_fusion.1.refs_1_, s32[1]{0:T(128)} %bitcast.refs_2_.refs_4_.refs_3_, bf16[1,7168,512]{2,1,0:T(8,128)(2,1)} %refs_4_.3, ...), custom_call_target="tpu_custom_call" | custom-call | flops 5637144576 | bytes 47710208 | tf_op jit(solution)/shard_map/pallas_call | solution.py:157
  79.6 2.0 %collective-permute-done.4 = bf16[64,7296]{1,0:T(8,128)(2,1)S(1)} collective-permute-done((bf16[64,7296]{1,0:T(8,128)(2,1)S(1)}, bf16[64,7296]{1,0:T(8,128)(2,1)S(1)}, u32[]{:S(2)}, u32[]{:S(2)}) %collective-permute-start.4) | collective-permute-done | bytes 933920 | tf_op jit(solution)/shard_map/ppermute | solution.py:204
  81.6 3.1 %collective-permute-done.10.refs_0_ = bf16[64,7296]{1,0:T(8,128)(2,1)S(1)} collective-permute-done((bf16[64,7296]{1,0:T(8,128)(2,1)S(1)}, bf16[64,7296]{1,0:T(8,128)(2,1)S(1)}, u32[]{:S(2)}, u32[]{:S(2)}) %collective-permute-start.10) | collective-permute-done | bytes 933920 | tf_op jit(solution)/shard_map/ppermute | solution.py:204
  84.9 1.3 collective-permute-start.13
  86.2 1.2 broadcast_select_fusion.refs_1_
  87.3 6.6 %collective-permute-done.12.refs_2_ = bf16[32,7296]{1,0:T(8,128)(2,1)S(1)} collective-permute-done((bf16[32,7296]{1,0:T(8,128)(2,1)S(1)}, bf16[32,7296]{1,0:T(8,128)(2,1)S(1)}, u32[]{:S(2)}, u32[]{:S(2)}) %collective-permute-start.12) | collective-permute-done | bytes 466976 | tf_op jit(solution)/shard_map/ppermute | solution.py:204
  94.0 1.8 collective-permute-done.13
  95.8 16.1 %shard_map.65 = (bf16[64,7168]{1,0:T(8,128)(2,1)S(1)}, bf16[64,7168]{1,0:T(8,128)(2,1)S(1)}, bf16[32,7168]{1,0:T(8,128)(2,1)S(1)}, bf16[32,7168]{1,0:T(8,128)(2,1)S(1)}) custom-call(bf16[64,7296]{1,0:T(8,128)(2,1)} %copy-done.2, bf16[64,7296]{1,0:T(8,128)(2,1)} %broadcast_select_fusion.refs_1_, bf16[32,7296]{1,0:T(8,128)(2,1)S(1)} %collective-permute-done.12.refs_2_, ...), custom_call_target="tpu_custom_call" | custom-call | flops 8455716864 | bytes 49545216 | tf_op jit(solution)/shard_map/pallas_call | solution.py:157
  111.9 1.7 collective-permute-start.14
  113.6 1.5 collective-permute-start.15
  115.6 9.9 %collective-permute-done.14 = bf16[32,7168]{1,0:T(8,128)(2,1)S(1)} collective-permute-done((bf16[32,7168]{1,0:T(8,128)(2,1)S(1)}, bf16[32,7168]{1,0:T(8,128)(2,1)S(1)}, u32[]{:S(2)}, u32[]{:S(2)}) %collective-permute-start.14) | collective-permute-done | bytes 458784 | tf_op jit(solution)/shard_map/ppermute | solution.py:204
  125.6 1.6 collective-permute-start.16
  128.1 11.4 %collective-permute-done.17 = bf16[64,7168]{1,0:T(8,128)(2,1)S(1)} collective-permute-done((bf16[64,7168]{1,0:T(8,128)(2,1)S(1)}, bf16[64,7168]{1,0:T(8,128)(2,1)S(1)}, u32[]{:S(2)}, u32[]{:S(2)}) %collective-permute-start.17) | collective-permute-done | bytes 917536 | tf_op jit(solution)/shard_map/ppermute | solution.py:204
  142.0 6.6 %collective-permute-start.20 = (bf16[64,7168]{1,0:T(8,128)(2,1)S(1)}, bf16[64,7168]{1,0:T(8,128)(2,1)S(1)}, u32[]{:S(2)}, u32[]{:S(2)}) collective-permute-start(bf16[64,7168]{1,0:T(8,128)(2,1)S(1)} %get-tuple-element.93), channel_id=1, source_target_pairs={{0,4},{2,6},{12,8},{14,10},{1,5},{3,7},{13,9},{15,11},{16,20},{18,... | collective-permute-start | bytes 2752520 | tf_op jit(solution)/shard_map/ppermute | solution.py:204
  149.2 17.4 %shard_map.66 = (bf16[64,7168]{1,0:T(8,128)(2,1)S(1)}, bf16[64,7168]{1,0:T(8,128)(2,1)S(1)}, bf16[64,7168]{1,0:T(8,128)(2,1)S(1)}) custom-call(bf16[64,7296]{1,0:T(8,128)(2,1)S(1)} %pad_maximum_fusion.refs_0_, bf16[64,7296]{1,0:T(8,128)(2,1)} %copy-done.1, bf16[64,7296]{1,0:T(8,128)(2,1)} %collective-permute-done.refs_2_, s32[1]{0:T(128)} %bitcast.refs_2_.refs_4_.refs_3_, ...), custom_call_target="tpu_custom_call" | custom-call | flops 8455716864 | bytes 49545216 | tf_op jit(solution)/shard_map/pallas_call | solution.py:157
  168.0 1.6 collective-permute-start.22
  169.5 11.7 %collective-permute-done.23 = bf16[64,7168]{1,0:T(8,128)(2,1)S(1)} collective-permute-done((bf16[64,7168]{1,0:T(8,128)(2,1)S(1)}, bf16[64,7168]{1,0:T(8,128)(2,1)S(1)}, u32[]{:S(2)}, u32[]{:S(2)}) %collective-permute-start.23) | collective-permute-done | bytes 917536 | tf_op jit(solution)/shard_map/ppermute | solution.py:204
  181.2 1.8 collective-permute-done.22
  183.0 1.4 add_convert_fusion
  (46 shorter events, 9.7 us)
Async XLA Ops:
  0.0 30.3 %collective-permute-start.8 = (bf16[1,7168,512]{2,1,0:T(8,128)(2,1)}, bf16[1,7168,512]{2,1,0:T(8,128)(2,1)S(1)}, u32[]{:S(2)}, u32[]{:S(2)}) collective-permute-start(bf16[1,7168,512]{2,1,0:T(8,128)(2,1)} %refs_4_.3), channel_id=1, source_target_pairs={{0,1},{1,0},{2,3},{3,2},{4,5},{5,4},{6,7},{7,6},{8,9},{9,8},{10,11... | collective-permute-start | bytes 22020104 | tf_op jit(solution)/shard_map/ppermute | solution.py:210
  3.2 24.1 %collective-permute-start = (bf16[64,7296]{1,0:T(8,128)(2,1)S(1)}, bf16[64,7296]{1,0:T(8,128)(2,1)}, u32[]{:S(2)}, u32[]{:S(2)}) collective-permute-start(bf16[64,7296]{1,0:T(8,128)(2,1)S(1)} %pad_maximum_fusion.refs_0_), channel_id=1, source_target_pairs={{0,4},{2,6},{4,0},{6,2},{8,12},{10,14},{12,8},{14,10},{1,5},{3,7},... | collective-permute-start | bytes 2801672 | tf_op jit(solution)/shard_map/ppermute | solution.py:204
  5.8 21.5 %collective-permute-start.1 = (bf16[64,7296]{1,0:T(8,128)(2,1)S(1)}, bf16[64,7296]{1,0:T(8,128)(2,1)}, u32[]{:S(2)}, u32[]{:S(2)}) collective-permute-start(bf16[64,7296]{1,0:T(8,128)(2,1)S(1)} %pad_maximum_fusion.refs_0_), channel_id=1, source_target_pairs={{4,8},{8,4},{6,10},{10,6},{5,9},{9,5},{7,11},{11,7},{20,24},{24,20... | collective-permute-start | bytes 2801672 | tf_op jit(solution)/shard_map/ppermute | solution.py:204
  7.5 22.8 %collective-permute-start.2 = (bf16[64,7296]{1,0:T(8,128)(2,1)S(1)}, bf16[64,7296]{1,0:T(8,128)(2,1)S(1)}, u32[]{:S(2)}, u32[]{:S(2)}) collective-permute-start(bf16[64,7296]{1,0:T(8,128)(2,1)S(1)} %pad_maximum_fusion.refs_0_), channel_id=1, source_target_pairs={{0,2},{2,0},{4,6},{6,4},{8,10},{10,8},{12,14},{14,12},{1,3},{3,1},... | collective-permute-start | bytes 2801672 | tf_op jit(solution)/shard_map/ppermute | solution.py:204
  9.0 53.6 %collective-permute-start.7 = (bf16[1,7168,512]{2,1,0:T(8,128)(2,1)}, bf16[1,7168,512]{2,1,0:T(8,128)(2,1)}, u32[]{:S(2)}, u32[]{:S(2)}) collective-permute-start(bf16[1,7168,512]{2,1,0:T(8,128)(2,1)} %refs_5_.3), channel_id=1, source_target_pairs={{0,1},{1,0},{2,3},{3,2},{4,5},{5,4},{6,7},{7,6},{8,9},{9,8},{10,11... | collective-permute-start | bytes 22020104 | tf_op jit(solution)/shard_map/ppermute | solution.py:210
  30.3 3.7 %copy-start.1 = (bf16[64,7296]{1,0:T(8,128)(2,1)}, bf16[64,7296]{1,0:T(8,128)(2,1)S(1)}, u32[]{:S(2)}) copy-start(bf16[64,7296]{1,0:T(8,128)(2,1)S(1)} %collective-permute-done.2.refs_1_) | copy-start | bytes 2801668
  30.3 3.0 %copy-start = (bf16[1,7168,512]{2,1,0:T(8,128)(2,1)}, bf16[1,7168,512]{2,1,0:T(8,128)(2,1)S(1)}, u32[]{:S(2)}) copy-start(bf16[1,7168,512]{2,1,0:T(8,128)(2,1)S(1)} %collective-permute-done.8.refs_5_.refs_7_.refs_6_) | copy-start | bytes 22020100
  30.3 32.3 %collective-permute-start.9 = (bf16[1,512,7168]{2,1,0:T(8,128)(2,1)}, bf16[1,512,7168]{2,1,0:T(8,128)(2,1)}, u32[]{:S(2)}, u32[]{:S(2)}) collective-permute-start(bf16[1,512,7168]{2,1,0:T(8,128)(2,1)} %refs_8_.1), channel_id=1, source_target_pairs={{0,1},{1,0},{2,3},{3,2},{4,5},{5,4},{6,7},{7,6},{8,9},{9,8},{10,11... | collective-permute-start | bytes 22020104 | tf_op jit(solution)/shard_map/ppermute | solution.py:210
  33.3 3.6 %collective-permute-start.3 = (bf16[64,7296]{1,0:T(8,128)(2,1)}, bf16[64,7296]{1,0:T(8,128)(2,1)S(1)}, u32[]{:S(2)}, u32[]{:S(2)}) collective-permute-start(bf16[64,7296]{1,0:T(8,128)(2,1)} %collective-permute-done.refs_2_), channel_id=1, source_target_pairs={{4,8},{8,4},{6,10},{10,6},{5,9},{9,5},{7,11},{11,7},{20,24},{24,20... | collective-permute-start | bytes 2801672 | tf_op jit(solution)/shard_map/ppermute | solution.py:204
  34.0 22.3 %collective-permute-start.6 = (bf16[64,7296]{1,0:T(8,128)(2,1)}, bf16[64,7296]{1,0:T(8,128)(2,1)S(1)}, u32[]{:S(2)}, u32[]{:S(2)}) collective-permute-start(bf16[64,7296]{1,0:T(8,128)(2,1)} %collective-permute-done.refs_2_), channel_id=1, source_target_pairs={{0,2},{2,0},{4,6},{6,4},{8,10},{10,8},{12,14},{14,12},{1,3},{3,1},... | collective-permute-start | bytes 2801672 | tf_op jit(solution)/shard_map/ppermute | solution.py:204
  35.6 27.0 %collective-permute-start.5 = (bf16[64,7296]{1,0:T(8,128)(2,1)}, bf16[64,7296]{1,0:T(8,128)(2,1)}, u32[]{:S(2)}, u32[]{:S(2)}) collective-permute-start(bf16[64,7296]{1,0:T(8,128)(2,1)} %collective-permute-done.1), channel_id=1, source_target_pairs={{4,0},{6,2},{8,12},{10,14},{5,1},{7,3},{9,13},{11,15},{20,16},{22,... | collective-permute-start | bytes 2801672 | tf_op jit(solution)/shard_map/ppermute | solution.py:204
  36.9 44.7 %collective-permute-start.4 = (bf16[64,7296]{1,0:T(8,128)(2,1)S(1)}, bf16[64,7296]{1,0:T(8,128)(2,1)S(1)}, u32[]{:S(2)}, u32[]{:S(2)}) collective-permute-start(bf16[64,7296]{1,0:T(8,128)(2,1)S(1)} %collective-permute-done.3), channel_id=1, source_target_pairs={{4,0},{6,2},{8,12},{10,14},{5,1},{7,3},{9,13},{11,15},{20,16},{22,... | collective-permute-start | bytes 2801672 | tf_op jit(solution)/shard_map/ppermute | solution.py:204
  63.9 20.8 %collective-permute-start.10 = (bf16[64,7296]{1,0:T(8,128)(2,1)S(1)}, bf16[64,7296]{1,0:T(8,128)(2,1)S(1)}, u32[]{:S(2)}, u32[]{:S(2)}) collective-permute-start(bf16[64,7296]{1,0:T(8,128)(2,1)S(1)} %broadcast_select_fusion.1.refs_1_), channel_id=1, source_target_pairs={{0,2},{2,0},{4,6},{6,4},{8,10},{10,8},{12,14},{14,12},{1,3},{3,1},... | collective-permute-start | bytes 2801672 | tf_op jit(solution)/shard_map/ppermute | solution.py:204
  64.0 17.5 %collective-permute-start.11 = (bf16[32,7296]{1,0:T(8,128)(2,1)S(1)}, bf16[32,7296]{1,0:T(8,128)(2,1)S(1)}, u32[]{:S(2)}, u32[]{:S(2)}) collective-permute-start(bf16[32,7296]{1,0:T(8,128)(2,1)S(1)} %slice.21), channel_id=1, source_target_pairs={{4,8},{8,4},{6,10},{10,6},{5,9},{9,5},{7,11},{11,7},{20,24},{24,20... | collective-permute-start | bytes 1400840 | tf_op jit(solution)/shard_map/ppermute | solution.py:204
  84.7 2.6 %copy-start.2 = (bf16[64,7296]{1,0:T(8,128)(2,1)}, bf16[64,7296]{1,0:T(8,128)(2,1)S(1)}, u32[]{:S(2)}) copy-start(bf16[64,7296]{1,0:T(8,128)(2,1)S(1)} %collective-permute-done.10.refs_0_) | copy-start | bytes 2801668
  84.8 9.2 %collective-permute-start.12 = (bf16[32,7296]{1,0:T(8,128)(2,1)S(1)}, bf16[32,7296]{1,0:T(8,128)(2,1)S(1)}, u32[]{:S(2)}, u32[]{:S(2)}) collective-permute-start(bf16[32,7296]{1,0:T(8,128)(2,1)S(1)} %slice_select_fusion), channel_id=1, source_target_pairs={{0,2},{2,0},{4,6},{6,4},{8,10},{10,8},{12,14},{14,12},{1,3},{3,1},... | collective-permute-start | bytes 1400840 | tf_op jit(solution)/shard_map/ppermute | solution.py:204
  84.9 10.9 %collective-permute-start.13 = (bf16[32,7296]{1,0:T(8,128)(2,1)S(1)}, bf16[32,7296]{1,0:T(8,128)(2,1)S(1)}, u32[]{:S(2)}, u32[]{:S(2)}) collective-permute-start(bf16[32,7296]{1,0:T(8,128)(2,1)S(1)} %collective-permute-done.11), channel_id=1, source_target_pairs={{4,0},{6,2},{8,12},{10,14},{5,1},{7,3},{9,13},{11,15},{20,16},{22,... | collective-permute-start | bytes 1400840 | tf_op jit(solution)/shard_map/ppermute | solution.py:204
  111.9 13.5 %collective-permute-start.14 = (bf16[32,7168]{1,0:T(8,128)(2,1)S(1)}, bf16[32,7168]{1,0:T(8,128)(2,1)S(1)}, u32[]{:S(2)}, u32[]{:S(2)}) collective-permute-start(bf16[32,7168]{1,0:T(8,128)(2,1)S(1)} %get-tuple-element.79), channel_id=1, source_target_pairs={{0,2},{2,0},{4,6},{6,4},{8,10},{10,8},{12,14},{14,12},{1,3},{3,1},... | collective-permute-start | bytes 1376264 | tf_op jit(solution)/shard_map/ppermute | solution.py:204
  113.6 11.9 %collective-permute-start.15 = (bf16[32,7168]{1,0:T(8,128)(2,1)S(1)}, bf16[32,7168]{1,0:T(8,128)(2,1)S(1)}, u32[]{:S(2)}, u32[]{:S(2)}) collective-permute-start(bf16[32,7168]{1,0:T(8,128)(2,1)S(1)} %get-tuple-element.80), channel_id=1, source_target_pairs={{0,4},{2,6},{12,8},{14,10},{1,5},{3,7},{13,9},{15,11},{16,20},{18,... | collective-permute-start | bytes 1376264 | tf_op jit(solution)/shard_map/ppermute | solution.py:204
  115.1 24.4 %collective-permute-start.17 = (bf16[64,7168]{1,0:T(8,128)(2,1)S(1)}, bf16[64,7168]{1,0:T(8,128)(2,1)S(1)}, u32[]{:S(2)}, u32[]{:S(2)}) collective-permute-start(bf16[64,7168]{1,0:T(8,128)(2,1)S(1)} %get-tuple-element.82), channel_id=1, source_target_pairs={{0,2},{2,0},{4,6},{6,4},{8,10},{10,8},{12,14},{14,12},{1,3},{3,1},... | collective-permute-start | bytes 2752520 | tf_op jit(solution)/shard_map/ppermute | solution.py:204
  125.6 15.0 %collective-permute-start.16 = (bf16[64,7168]{1,0:T(8,128)(2,1)S(1)}, bf16[64,7168]{1,0:T(8,128)(2,1)S(1)}, u32[]{:S(2)}, u32[]{:S(2)}) collective-permute-start(bf16[64,7168]{1,0:T(8,128)(2,1)S(1)} %pad_maximum_fusion.1), channel_id=1, source_target_pairs={{0,4},{2,6},{12,8},{14,10},{1,5},{3,7},{13,9},{15,11},{16,20},{18,... | collective-permute-start | bytes 2752520 | tf_op jit(solution)/shard_map/ppermute | solution.py:204
  127.3 0.7 collective-permute-start.18
  141.3 25.3 %collective-permute-start.19 = (bf16[64,7168]{1,0:T(8,128)(2,1)S(1)}, bf16[64,7168]{1,0:T(8,128)(2,1)S(1)}, u32[]{:S(2)}, u32[]{:S(2)}) collective-permute-start(bf16[64,7168]{1,0:T(8,128)(2,1)S(1)} %get-tuple-element.92), channel_id=1, source_target_pairs={{4,8},{8,4},{6,10},{10,6},{5,9},{9,5},{7,11},{11,7},{20,24},{24,20... | collective-permute-start | bytes 2752520 | tf_op jit(solution)/shard_map/ppermute | solution.py:204
  142.0 24.6 %collective-permute-start.20 = (bf16[64,7168]{1,0:T(8,128)(2,1)S(1)}, bf16[64,7168]{1,0:T(8,128)(2,1)S(1)}, u32[]{:S(2)}, u32[]{:S(2)}) collective-permute-start(bf16[64,7168]{1,0:T(8,128)(2,1)S(1)} %get-tuple-element.93), channel_id=1, source_target_pairs={{0,4},{2,6},{12,8},{14,10},{1,5},{3,7},{13,9},{15,11},{16,20},{18,... | collective-permute-start | bytes 2752520 | tf_op jit(solution)/shard_map/ppermute | solution.py:204
  148.6 18.1 %collective-permute-start.21 = (bf16[64,7168]{1,0:T(8,128)(2,1)S(1)}, bf16[64,7168]{1,0:T(8,128)(2,1)S(1)}, u32[]{:S(2)}, u32[]{:S(2)}) collective-permute-start(bf16[64,7168]{1,0:T(8,128)(2,1)S(1)} %pad_maximum_fusion.2), channel_id=1, source_target_pairs={{0,2},{2,0},{4,6},{6,4},{8,10},{10,8},{12,14},{14,12},{1,3},{3,1},... | collective-permute-start | bytes 2752520 | tf_op jit(solution)/shard_map/ppermute | solution.py:204
  167.0 14.3 %collective-permute-start.23 = (bf16[64,7168]{1,0:T(8,128)(2,1)S(1)}, bf16[64,7168]{1,0:T(8,128)(2,1)S(1)}, u32[]{:S(2)}, u32[]{:S(2)}) collective-permute-start(bf16[64,7168]{1,0:T(8,128)(2,1)S(1)} %add_convert_fusion.2), channel_id=1, source_target_pairs={{0,4},{2,6},{4,0},{6,2},{8,12},{10,14},{12,8},{14,10},{1,5},{3,7},... | collective-permute-start | bytes 2752520 | tf_op jit(solution)/shard_map/ppermute | solution.py:204
  167.3 14.0 %collective-permute-start.24 = (bf16[64,7168]{1,0:T(8,128)(2,1)S(1)}, bf16[64,7168]{1,0:T(8,128)(2,1)S(1)}, u32[]{:S(2)}, u32[]{:S(2)}) collective-permute-start(bf16[64,7168]{1,0:T(8,128)(2,1)S(1)} %add_convert_fusion.1), channel_id=1, source_target_pairs={{4,8},{8,4},{6,10},{10,6},{5,9},{9,5},{7,11},{11,7},{20,24},{24,20... | collective-permute-start | bytes 2752520 | tf_op jit(solution)/shard_map/ppermute | solution.py:204
  168.0 15.0 %collective-permute-start.22 = (bf16[64,7168]{1,0:T(8,128)(2,1)S(1)}, bf16[64,7168]{1,0:T(8,128)(2,1)S(1)}, u32[]{:S(2)}, u32[]{:S(2)}) collective-permute-start(bf16[64,7168]{1,0:T(8,128)(2,1)S(1)} %get-tuple-element.102), channel_id=1, source_target_pairs={{0,2},{2,0},{4,6},{6,4},{8,10},{10,8},{12,14},{14,12},{1,3},{3,1},... | collective-permute-start | bytes 2752520 | tf_op jit(solution)/shard_map/ppermute | solution.py:204

commit v8 on v6

--- a/solution.py
+++ b/solution.py
@@ -256,13 +256,14 @@
 
     y3, v3 = joined(cross(q3, 1), send(r3, inward))
     p3, r3 = jnp.concatenate([plus(p3[:cut], y3), p3[cut:]]), plus(r3, v3)
+    near = q1[:cut]
     i3, y2, v1 = joined(send(p3, inward), cross(q2, 1), send(r3, middle))
-    p3, p2, q1 = plus(p3, i3), plus(p2, y2), jnp.concatenate([q1[:cut], plus(q1[cut:], v1)])
+    p3, p2, q1 = plus(p3, i3), plus(p2, y2), plus(q1[cut:], v1)
     p3, p2, q1, s0, t0, s1 = joined(p3, p2, q1, s0, t0, s1)
-    i1, i2, y1, p0, q0, p1 = joined(
-        send(p3, middle), send(p2, inward), cross(q1, 1), *experts(s0, t0, s1)
-    )
-    p1, p2 = plus(p1, y1, i1), plus(p2, i2)
+    i1, i2, y1, z1, p0, q0, p1 = joined(
+        send(p3, middle), send(p2, inward), cross(near, 1), cross(q1, 1), *experts(s0, t0, s1)
+    )
+    p1, p2 = plus(p1, jnp.concatenate([y1, z1]), i1), plus(p2, i2)
     return plus(p0, cross(q0, 1), cross(p1, 2), send(p2, middle))
 
 

time: 185 us -> 186 us (level)
    ppermute x22 -> x23, starting transfers between devices: 28.9 us -> 29.5 us  [send(): return lax.ppermute(array, 'node', pairs)]
    ppermute x22 -> x23, waiting for transfers between devices: 95.7 us -> 95.3 us  [send(): return lax.ppermute(array, 'node', pairs)]
  transfers between devices with their start and end apart: 25 -> 26, of which waited for: 13 -> 13; matrix products, arithmetic and copies ran while one was open for 3% -> 3% of each run, Pallas kernels for 17% -> 17%
where the time goes in v8:
time: 186 us; the launch traced here: 185 us
  waiting for transfers between devices  95.4 us (51%)
  Pallas kernels  47.9 us (26%)
  starting transfers between devices  30 us (16%)
  other arithmetic  8.08 us (4%)
  local copies, waits for them, and re-layouts  2.98 us (2%)
    ppermute x23, waiting for transfers between devices, send(): return lax.ppermute(array, 'node', pairs)  95.3 us
    pallas_call x3, Pallas kernels, expert_rows(): pl.pallas_call(functools.partial(expert_kernel, count, slab, out_tile), i...  47.9 us
    ppermute x23, starting transfers between devices, send(): return lax.ppermute(array, 'node', pairs)  29.5 us
  transfers between devices with their start and end apart: 26, of which 13 were waited for; matrix products, arithmetic and copies ran while one was open for 3% of the time, Pallas kernels for 17%

profile of v8, /device:TPU:0, one launch (start us, length us, event | category | flops | bytes accessed | tf_op | source)
XLA Modules:
  0.0 184.6 jit_solution(1346162282335945363)
XLA Ops:
  2.0 1.2 pad_maximum_fusion.refs_0_
  3.2 2.6 %collective-permute-start = (bf16[64,7296]{1,0:T(8,128)(2,1)S(1)}, bf16[64,7296]{1,0:T(8,128)(2,1)}, u32[]{:S(2)}, u32[]{:S(2)}) collective-permute-start(bf16[64,7296]{1,0:T(8,128)(2,1)S(1)} %pad_maximum_fusion.refs_0_), channel_id=1, source_target_pairs={{0,4},{2,6},{4,0},{6,2},{8,12},{10,14},{12,8},{14,10},{1,5},{3,7},... | collective-permute-start | bytes 2801672 | tf_op jit(solution)/shard_map/ppermute | solution.py:204
  5.8 1.6 collective-permute-start.1
  7.5 1.5 collective-permute-start.2
  9.0 18.3 %collective-permute-done.refs_2_ = bf16[64,7296]{1,0:T(8,128)(2,1)} collective-permute-done((bf16[64,7296]{1,0:T(8,128)(2,1)S(1)}, bf16[64,7296]{1,0:T(8,128)(2,1)}, u32[]{:S(2)}, u32[]{:S(2)}) %collective-permute-start) | collective-permute-done | bytes 933920 | tf_op jit(solution)/shard_map/ppermute | solution.py:204
  27.3 3.0 %collective-permute-done.2.refs_1_ = bf16[64,7296]{1,0:T(8,128)(2,1)S(1)} collective-permute-done((bf16[64,7296]{1,0:T(8,128)(2,1)S(1)}, bf16[64,7296]{1,0:T(8,128)(2,1)S(1)}, u32[]{:S(2)}, u32[]{:S(2)}) %collective-permute-start.2) | collective-permute-done | bytes 933920 | tf_op jit(solution)/shard_map/ppermute | solution.py:204
  30.4 2.9 %copy-done = bf16[1,7168,512]{2,1,0:T(8,128)(2,1)} copy-done((bf16[1,7168,512]{2,1,0:T(8,128)(2,1)}, bf16[1,7168,512]{2,1,0:T(8,128)(2,1)S(1)}, u32[]{:S(2)}) %copy-start) | copy-done | bytes 7340056
  34.0 1.6 collective-permute-start.6
  35.6 1.3 collective-permute-start.5
  36.9 1.3 collective-permute-start.4
  38.2 18.1 %collective-permute-done.6.refs_0_ = bf16[64,7296]{1,0:T(8,128)(2,1)S(1)} collective-permute-done((bf16[64,7296]{1,0:T(8,128)(2,1)}, bf16[64,7296]{1,0:T(8,128)(2,1)S(1)}, u32[]{:S(2)}, u32[]{:S(2)}) %collective-permute-start.6) | collective-permute-done | bytes 933920 | tf_op jit(solution)/shard_map/ppermute | solution.py:204
  56.3 6.3 %collective-permute-done.5 = bf16[64,7296]{1,0:T(8,128)(2,1)} collective-permute-done((bf16[64,7296]{1,0:T(8,128)(2,1)}, bf16[64,7296]{1,0:T(8,128)(2,1)}, u32[]{:S(2)}, u32[]{:S(2)}) %collective-permute-start.5) | collective-permute-done | bytes 933920 | tf_op jit(solution)/shard_map/ppermute | solution.py:204
  62.6 1.3 broadcast_select_fusion.1.refs_1_
  64.7 14.8 %shard_map.64 = (bf16[64,7168]{1,0:T(8,128)(2,1)S(1)}, bf16[64,7168]{1,0:T(8,128)(2,1)S(1)}) custom-call(bf16[64,7296]{1,0:T(8,128)(2,1)S(1)} %collective-permute-done.6.refs_0_, bf16[64,7296]{1,0:T(8,128)(2,1)S(1)} %broadcast_select_fusion.1.refs_1_, s32[1]{0:T(128)} %bitcast.refs_2_.refs_4_.refs_3_, bf16[1,7168,512]{2,1,0:T(8,128)(2,1)} %refs_4_.3, ...), custom_call_target="tpu_custom_call" | custom-call | flops 5637144576 | bytes 47710208 | tf_op jit(solution)/shard_map/pallas_call | solution.py:157
  79.5 2.0 %collective-permute-done.4 = bf16[64,7296]{1,0:T(8,128)(2,1)S(1)} collective-permute-done((bf16[64,7296]{1,0:T(8,128)(2,1)S(1)}, bf16[64,7296]{1,0:T(8,128)(2,1)S(1)}, u32[]{:S(2)}, u32[]{:S(2)}) %collective-permute-start.4) | collective-permute-done | bytes 933920 | tf_op jit(solution)/shard_map/ppermute | solution.py:204
  81.6 3.1 %collective-permute-done.10.refs_0_ = bf16[64,7296]{1,0:T(8,128)(2,1)S(1)} collective-permute-done((bf16[64,7296]{1,0:T(8,128)(2,1)S(1)}, bf16[64,7296]{1,0:T(8,128)(2,1)S(1)}, u32[]{:S(2)}, u32[]{:S(2)}) %collective-permute-start.10) | collective-permute-done | bytes 933920 | tf_op jit(solution)/shard_map/ppermute | solution.py:204
  84.9 1.3 collective-permute-start.13
  86.2 1.2 broadcast_select_fusion.refs_1_
  87.3 6.6 %collective-permute-done.12.refs_2_ = bf16[32,7296]{1,0:T(8,128)(2,1)S(1)} collective-permute-done((bf16[32,7296]{1,0:T(8,128)(2,1)S(1)}, bf16[32,7296]{1,0:T(8,128)(2,1)S(1)}, u32[]{:S(2)}, u32[]{:S(2)}) %collective-permute-start.12) | collective-permute-done | bytes 466976 | tf_op jit(solution)/shard_map/ppermute | solution.py:204
  94.0 1.8 collective-permute-done.13
  95.8 16.2 %shard_map.65 = (bf16[64,7168]{1,0:T(8,128)(2,1)S(1)}, bf16[64,7168]{1,0:T(8,128)(2,1)S(1)}, bf16[32,7168]{1,0:T(8,128)(2,1)S(1)}, bf16[32,7168]{1,0:T(8,128)(2,1)S(1)}) custom-call(bf16[64,7296]{1,0:T(8,128)(2,1)} %copy-done.2, bf16[64,7296]{1,0:T(8,128)(2,1)} %broadcast_select_fusion.refs_1_, bf16[32,7296]{1,0:T(8,128)(2,1)S(1)} %collective-permute-done.12.refs_2_, ...), custom_call_target="tpu_custom_call" | custom-call | flops 8455716864 | bytes 49545216 | tf_op jit(solution)/shard_map/pallas_call | solution.py:157
  112.0 1.7 collective-permute-start.14
  113.7 1.5 collective-permute-start.15
  115.7 9.8 %collective-permute-done.14 = bf16[32,7168]{1,0:T(8,128)(2,1)S(1)} collective-permute-done((bf16[32,7168]{1,0:T(8,128)(2,1)S(1)}, bf16[32,7168]{1,0:T(8,128)(2,1)S(1)}, u32[]{:S(2)}, u32[]{:S(2)}) %collective-permute-start.14) | collective-permute-done | bytes 458784 | tf_op jit(solution)/shard_map/ppermute | solution.py:204
  125.7 1.6 collective-permute-start.16
  128.2 11.5 %collective-permute-done.17 = bf16[64,7168]{1,0:T(8,128)(2,1)S(1)} collective-permute-done((bf16[64,7168]{1,0:T(8,128)(2,1)S(1)}, bf16[64,7168]{1,0:T(8,128)(2,1)S(1)}, u32[]{:S(2)}, u32[]{:S(2)}) %collective-permute-start.17) | collective-permute-done | bytes 917536 | tf_op jit(solution)/shard_map/ppermute | solution.py:204
  139.6 1.1 collective-permute-done.16
  142.0 6.6 %collective-permute-start.20 = (bf16[64,7168]{1,0:T(8,128)(2,1)S(1)}, bf16[64,7168]{1,0:T(8,128)(2,1)S(1)}, u32[]{:S(2)}, u32[]{:S(2)}) collective-permute-start(bf16[64,7168]{1,0:T(8,128)(2,1)S(1)} %add_convert_fusion.3), channel_id=1, source_target_pairs={{0,4},{2,6},{12,8},{14,10},{1,5},{3,7},{13,9},{15,11},{16,20},{18,... | collective-permute-start | bytes 2752520 | tf_op jit(solution)/shard_map/ppermute | solution.py:204
  149.3 1.4 collective-permute-start.22
  150.8 16.9 %shard_map.66 = (bf16[64,7168]{1,0:T(8,128)(2,1)S(1)}, bf16[64,7168]{1,0:T(8,128)(2,1)S(1)}, bf16[64,7168]{1,0:T(8,128)(2,1)S(1)}) custom-call(bf16[64,7296]{1,0:T(8,128)(2,1)S(1)} %pad_maximum_fusion.refs_0_, bf16[64,7296]{1,0:T(8,128)(2,1)} %copy-done.1, bf16[64,7296]{1,0:T(8,128)(2,1)} %collective-permute-done.refs_2_, s32[1]{0:T(128)} %bitcast.refs_2_.refs_4_.refs_3_, ...), custom_call_target="tpu_custom_call" | custom-call | flops 8455716864 | bytes 49545216 | tf_op jit(solution)/shard_map/pallas_call | solution.py:157
  169.7 12.6 %collective-permute-done.24 = bf16[64,7168]{1,0:T(8,128)(2,1)S(1)} collective-permute-done((bf16[64,7168]{1,0:T(8,128)(2,1)S(1)}, bf16[64,7168]{1,0:T(8,128)(2,1)S(1)}, u32[]{:S(2)}, u32[]{:S(2)}) %collective-permute-start.24) | collective-permute-done | bytes 917536 | tf_op jit(solution)/shard_map/ppermute | solution.py:204
  183.3 1.4 add_convert_fusion
  (48 shorter events, 10.2 us)
Async XLA Ops:
  0.0 30.3 %collective-permute-start.8 = (bf16[1,7168,512]{2,1,0:T(8,128)(2,1)}, bf16[1,7168,512]{2,1,0:T(8,128)(2,1)S(1)}, u32[]{:S(2)}, u32[]{:S(2)}) collective-permute-start(bf16[1,7168,512]{2,1,0:T(8,128)(2,1)} %refs_4_.3), channel_id=1, source_target_pairs={{0,1},{1,0},{2,3},{3,2},{4,5},{5,4},{6,7},{7,6},{8,9},{9,8},{10,11... | collective-permute-start | bytes 22020104 | tf_op jit(solution)/shard_map/ppermute | solution.py:210
  3.2 24.1 %collective-permute-start = (bf16[64,7296]{1,0:T(8,128)(2,1)S(1)}, bf16[64,7296]{1,0:T(8,128)(2,1)}, u32[]{:S(2)}, u32[]{:S(2)}) collective-permute-start(bf16[64,7296]{1,0:T(8,128)(2,1)S(1)} %pad_maximum_fusion.refs_0_), channel_id=1, source_target_pairs={{0,4},{2,6},{4,0},{6,2},{8,12},{10,14},{12,8},{14,10},{1,5},{3,7},... | collective-permute-start | bytes 2801672 | tf_op jit(solution)/shard_map/ppermute | solution.py:204
  5.8 21.5 %collective-permute-start.1 = (bf16[64,7296]{1,0:T(8,128)(2,1)S(1)}, bf16[64,7296]{1,0:T(8,128)(2,1)}, u32[]{:S(2)}, u32[]{:S(2)}) collective-permute-start(bf16[64,7296]{1,0:T(8,128)(2,1)S(1)} %pad_maximum_fusion.refs_0_), channel_id=1, source_target_pairs={{4,8},{8,4},{6,10},{10,6},{5,9},{9,5},{7,11},{11,7},{20,24},{24,20... | collective-permute-start | bytes 2801672 | tf_op jit(solution)/shard_map/ppermute | solution.py:204
  7.5 22.8 %collective-permute-start.2 = (bf16[64,7296]{1,0:T(8,128)(2,1)S(1)}, bf16[64,7296]{1,0:T(8,128)(2,1)S(1)}, u32[]{:S(2)}, u32[]{:S(2)}) collective-permute-start(bf16[64,7296]{1,0:T(8,128)(2,1)S(1)} %pad_maximum_fusion.refs_0_), channel_id=1, source_target_pairs={{0,2},{2,0},{4,6},{6,4},{8,10},{10,8},{12,14},{14,12},{1,3},{3,1},... | collective-permute-start | bytes 2801672 | tf_op jit(solution)/shard_map/ppermute | solution.py:204
  9.0 53.6 %collective-permute-start.7 = (bf16[1,7168,512]{2,1,0:T(8,128)(2,1)}, bf16[1,7168,512]{2,1,0:T(8,128)(2,1)}, u32[]{:S(2)}, u32[]{:S(2)}) collective-permute-start(bf16[1,7168,512]{2,1,0:T(8,128)(2,1)} %refs_5_.3), channel_id=1, source_target_pairs={{0,1},{1,0},{2,3},{3,2},{4,5},{5,4},{6,7},{7,6},{8,9},{9,8},{10,11... | collective-permute-start | bytes 22020104 | tf_op jit(solution)/shard_map/ppermute | solution.py:210
  30.3 3.7 %copy-start.1 = (bf16[64,7296]{1,0:T(8,128)(2,1)}, bf16[64,7296]{1,0:T(8,128)(2,1)S(1)}, u32[]{:S(2)}) copy-start(bf16[64,7296]{1,0:T(8,128)(2,1)S(1)} %collective-permute-done.2.refs_1_) | copy-start | bytes 2801668
  30.3 3.0 %copy-start = (bf16[1,7168,512]{2,1,0:T(8,128)(2,1)}, bf16[1,7168,512]{2,1,0:T(8,128)(2,1)S(1)}, u32[]{:S(2)}) copy-start(bf16[1,7168,512]{2,1,0:T(8,128)(2,1)S(1)} %collective-permute-done.8.refs_5_.refs_7_.refs_6_) | copy-start | bytes 22020100
  30.3 32.3 %collective-permute-start.9 = (bf16[1,512,7168]{2,1,0:T(8,128)(2,1)}, bf16[1,512,7168]{2,1,0:T(8,128)(2,1)}, u32[]{:S(2)}, u32[]{:S(2)}) collective-permute-start(bf16[1,512,7168]{2,1,0:T(8,128)(2,1)} %refs_8_.1), channel_id=1, source_target_pairs={{0,1},{1,0},{2,3},{3,2},{4,5},{5,4},{6,7},{7,6},{8,9},{9,8},{10,11... | collective-permute-start | bytes 22020104 | tf_op jit(solution)/shard_map/ppermute | solution.py:210
  33.3 3.6 %collective-permute-start.3 = (bf16[64,7296]{1,0:T(8,128)(2,1)}, bf16[64,7296]{1,0:T(8,128)(2,1)S(1)}, u32[]{:S(2)}, u32[]{:S(2)}) collective-permute-start(bf16[64,7296]{1,0:T(8,128)(2,1)} %collective-permute-done.refs_2_), channel_id=1, source_target_pairs={{4,8},{8,4},{6,10},{10,6},{5,9},{9,5},{7,11},{11,7},{20,24},{24,20... | collective-permute-start | bytes 2801672 | tf_op jit(solution)/shard_map/ppermute | solution.py:204
  34.0 22.3 %collective-permute-start.6 = (bf16[64,7296]{1,0:T(8,128)(2,1)}, bf16[64,7296]{1,0:T(8,128)(2,1)S(1)}, u32[]{:S(2)}, u32[]{:S(2)}) collective-permute-start(bf16[64,7296]{1,0:T(8,128)(2,1)} %collective-permute-done.refs_2_), channel_id=1, source_target_pairs={{0,2},{2,0},{4,6},{6,4},{8,10},{10,8},{12,14},{14,12},{1,3},{3,1},... | collective-permute-start | bytes 2801672 | tf_op jit(solution)/shard_map/ppermute | solution.py:204
  35.6 27.0 %collective-permute-start.5 = (bf16[64,7296]{1,0:T(8,128)(2,1)}, bf16[64,7296]{1,0:T(8,128)(2,1)}, u32[]{:S(2)}, u32[]{:S(2)}) collective-permute-start(bf16[64,7296]{1,0:T(8,128)(2,1)} %collective-permute-done.1), channel_id=1, source_target_pairs={{4,0},{6,2},{8,12},{10,14},{5,1},{7,3},{9,13},{11,15},{20,16},{22,... | collective-permute-start | bytes 2801672 | tf_op jit(solution)/shard_map/ppermute | solution.py:204
  36.9 44.7 %collective-permute-start.4 = (bf16[64,7296]{1,0:T(8,128)(2,1)S(1)}, bf16[64,7296]{1,0:T(8,128)(2,1)S(1)}, u32[]{:S(2)}, u32[]{:S(2)}) collective-permute-start(bf16[64,7296]{1,0:T(8,128)(2,1)S(1)} %collective-permute-done.3), channel_id=1, source_target_pairs={{4,0},{6,2},{8,12},{10,14},{5,1},{7,3},{9,13},{11,15},{20,16},{22,... | collective-permute-start | bytes 2801672 | tf_op jit(solution)/shard_map/ppermute | solution.py:204
  63.9 20.8 %collective-permute-start.10 = (bf16[64,7296]{1,0:T(8,128)(2,1)S(1)}, bf16[64,7296]{1,0:T(8,128)(2,1)S(1)}, u32[]{:S(2)}, u32[]{:S(2)}) collective-permute-start(bf16[64,7296]{1,0:T(8,128)(2,1)S(1)} %broadcast_select_fusion.1.refs_1_), channel_id=1, source_target_pairs={{0,2},{2,0},{4,6},{6,4},{8,10},{10,8},{12,14},{14,12},{1,3},{3,1},... | collective-permute-start | bytes 2801672 | tf_op jit(solution)/shard_map/ppermute | solution.py:204
  64.0 17.5 %collective-permute-start.11 = (bf16[32,7296]{1,0:T(8,128)(2,1)S(1)}, bf16[32,7296]{1,0:T(8,128)(2,1)S(1)}, u32[]{:S(2)}, u32[]{:S(2)}) collective-permute-start(bf16[32,7296]{1,0:T(8,128)(2,1)S(1)} %slice.21), channel_id=1, source_target_pairs={{4,8},{8,4},{6,10},{10,6},{5,9},{9,5},{7,11},{11,7},{20,24},{24,20... | collective-permute-start | bytes 1400840 | tf_op jit(solution)/shard_map/ppermute | solution.py:204
  84.7 2.6 %copy-start.2 = (bf16[64,7296]{1,0:T(8,128)(2,1)}, bf16[64,7296]{1,0:T(8,128)(2,1)S(1)}, u32[]{:S(2)}) copy-start(bf16[64,7296]{1,0:T(8,128)(2,1)S(1)} %collective-permute-done.10.refs_0_) | copy-start | bytes 2801668
  84.8 9.2 %collective-permute-start.12 = (bf16[32,7296]{1,0:T(8,128)(2,1)S(1)}, bf16[32,7296]{1,0:T(8,128)(2,1)S(1)}, u32[]{:S(2)}, u32[]{:S(2)}) collective-permute-start(bf16[32,7296]{1,0:T(8,128)(2,1)S(1)} %slice_select_fusion), channel_id=1, source_target_pairs={{0,2},{2,0},{4,6},{6,4},{8,10},{10,8},{12,14},{14,12},{1,3},{3,1},... | collective-permute-start | bytes 1400840 | tf_op jit(solution)/shard_map/ppermute | solution.py:204
  84.9 10.9 %collective-permute-start.13 = (bf16[32,7296]{1,0:T(8,128)(2,1)S(1)}, bf16[32,7296]{1,0:T(8,128)(2,1)S(1)}, u32[]{:S(2)}, u32[]{:S(2)}) collective-permute-start(bf16[32,7296]{1,0:T(8,128)(2,1)S(1)} %collective-permute-done.11), channel_id=1, source_target_pairs={{4,0},{6,2},{8,12},{10,14},{5,1},{7,3},{9,13},{11,15},{20,16},{22,... | collective-permute-start | bytes 1400840 | tf_op jit(solution)/shard_map/ppermute | solution.py:204
  112.0 13.5 %collective-permute-start.14 = (bf16[32,7168]{1,0:T(8,128)(2,1)S(1)}, bf16[32,7168]{1,0:T(8,128)(2,1)S(1)}, u32[]{:S(2)}, u32[]{:S(2)}) collective-permute-start(bf16[32,7168]{1,0:T(8,128)(2,1)S(1)} %get-tuple-element.80), channel_id=1, source_target_pairs={{0,2},{2,0},{4,6},{6,4},{8,10},{10,8},{12,14},{14,12},{1,3},{3,1},... | collective-permute-start | bytes 1376264 | tf_op jit(solution)/shard_map/ppermute | solution.py:204
  113.7 11.9 %collective-permute-start.15 = (bf16[32,7168]{1,0:T(8,128)(2,1)S(1)}, bf16[32,7168]{1,0:T(8,128)(2,1)S(1)}, u32[]{:S(2)}, u32[]{:S(2)}) collective-permute-start(bf16[32,7168]{1,0:T(8,128)(2,1)S(1)} %get-tuple-element.81), channel_id=1, source_target_pairs={{0,4},{2,6},{12,8},{14,10},{1,5},{3,7},{13,9},{15,11},{16,20},{18,... | collective-permute-start | bytes 1376264 | tf_op jit(solution)/shard_map/ppermute | solution.py:204
  115.2 24.4 %collective-permute-start.17 = (bf16[64,7168]{1,0:T(8,128)(2,1)S(1)}, bf16[64,7168]{1,0:T(8,128)(2,1)S(1)}, u32[]{:S(2)}, u32[]{:S(2)}) collective-permute-start(bf16[64,7168]{1,0:T(8,128)(2,1)S(1)} %get-tuple-element.83), channel_id=1, source_target_pairs={{0,2},{2,0},{4,6},{6,4},{8,10},{10,8},{12,14},{14,12},{1,3},{3,1},... | collective-permute-start | bytes 2752520 | tf_op jit(solution)/shard_map/ppermute | solution.py:204
  125.7 15.0 %collective-permute-start.16 = (bf16[64,7168]{1,0:T(8,128)(2,1)S(1)}, bf16[64,7168]{1,0:T(8,128)(2,1)S(1)}, u32[]{:S(2)}, u32[]{:S(2)}) collective-permute-start(bf16[64,7168]{1,0:T(8,128)(2,1)S(1)} %pad_maximum_fusion.1), channel_id=1, source_target_pairs={{0,4},{2,6},{12,8},{14,10},{1,5},{3,7},{13,9},{15,11},{16,20},{18,... | collective-permute-start | bytes 2752520 | tf_op jit(solution)/shard_map/ppermute | solution.py:204
  127.4 0.7 collective-permute-start.18
  141.3 26.3 %collective-permute-start.19 = (bf16[64,7168]{1,0:T(8,128)(2,1)S(1)}, bf16[64,7168]{1,0:T(8,128)(2,1)S(1)}, u32[]{:S(2)}, u32[]{:S(2)}) collective-permute-start(bf16[64,7168]{1,0:T(8,128)(2,1)S(1)} %add_convert_fusion.4), channel_id=1, source_target_pairs={{4,8},{8,4},{6,10},{10,6},{5,9},{9,5},{7,11},{11,7},{20,24},{24,20... | collective-permute-start | bytes 2752520 | tf_op jit(solution)/shard_map/ppermute | solution.py:204
  142.0 25.6 %collective-permute-start.20 = (bf16[64,7168]{1,0:T(8,128)(2,1)S(1)}, bf16[64,7168]{1,0:T(8,128)(2,1)S(1)}, u32[]{:S(2)}, u32[]{:S(2)}) collective-permute-start(bf16[64,7168]{1,0:T(8,128)(2,1)S(1)} %add_convert_fusion.3), channel_id=1, source_target_pairs={{0,4},{2,6},{12,8},{14,10},{1,5},{3,7},{13,9},{15,11},{16,20},{18,... | collective-permute-start | bytes 2752520 | tf_op jit(solution)/shard_map/ppermute | solution.py:204
  148.7 19.0 %collective-permute-start.21 = (bf16[32,7168]{1,0:T(8,128)(2,1)S(1)}, bf16[32,7168]{1,0:T(8,128)(2,1)S(1)}, u32[]{:S(2)}, u32[]{:S(2)}) collective-permute-start(bf16[32,7168]{1,0:T(8,128)(2,1)S(1)} %slice.27), channel_id=1, source_target_pairs={{0,2},{2,0},{4,6},{6,4},{8,10},{10,8},{12,14},{14,12},{1,3},{3,1},... | collective-permute-start | bytes 1376264 | tf_op jit(solution)/shard_map/ppermute | solution.py:204
  149.3 18.3 %collective-permute-start.22 = (bf16[32,7168]{1,0:T(8,128)(2,1)S(1)}, bf16[32,7168]{1,0:T(8,128)(2,1)S(1)}, u32[]{:S(2)}, u32[]{:S(2)}) collective-permute-start(bf16[32,7168]{1,0:T(8,128)(2,1)S(1)} %add_convert_fusion.5), channel_id=1, source_target_pairs={{0,2},{2,0},{4,6},{6,4},{8,10},{10,8},{12,14},{14,12},{1,3},{3,1},... | collective-permute-start | bytes 1376264 | tf_op jit(solution)/shard_map/ppermute | solution.py:204
  168.0 14.2 %collective-permute-start.24 = (bf16[64,7168]{1,0:T(8,128)(2,1)S(1)}, bf16[64,7168]{1,0:T(8,128)(2,1)S(1)}, u32[]{:S(2)}, u32[]{:S(2)}) collective-permute-start(bf16[64,7168]{1,0:T(8,128)(2,1)S(1)} %add_convert_fusion.2), channel_id=1, source_target_pairs={{0,4},{2,6},{4,0},{6,2},{8,12},{10,14},{12,8},{14,10},{1,5},{3,7},... | collective-permute-start | bytes 2752520 | tf_op jit(solution)/shard_map/ppermute | solution.py:204
  168.3 13.9 %collective-permute-start.25 = (bf16[64,7168]{1,0:T(8,128)(2,1)S(1)}, bf16[64,7168]{1,0:T(8,128)(2,1)S(1)}, u32[]{:S(2)}, u32[]{:S(2)}) collective-permute-start(bf16[64,7168]{1,0:T(8,128)(2,1)S(1)} %add_convert_fusion.1), channel_id=1, source_target_pairs={{4,8},{8,4},{6,10},{10,6},{5,9},{9,5},{7,11},{11,7},{20,24},{24,20... | collective-permute-start | bytes 2752520 | tf_op jit(solution)/shard_map/ppermute | solution.py:204
  169.0 14.2 %collective-permute-start.23 = (bf16[64,7168]{1,0:T(8,128)(2,1)S(1)}, bf16[64,7168]{1,0:T(8,128)(2,1)S(1)}, u32[]{:S(2)}, u32[]{:S(2)}) collective-permute-start(bf16[64,7168]{1,0:T(8,128)(2,1)S(1)} %get-tuple-element.103), channel_id=1, source_target_pairs={{0,2},{2,0},{4,6},{6,4},{8,10},{10,8},{12,14},{14,12},{1,3},{3,1},... | collective-permute-start | bytes 2752520 | tf_op jit(solution)/shard_map/ppermute | solution.py:204
